TPU v7x, 256 devices: a whole 4x4x8 slice. The times are simulated.
256 devices in a mesh: ctx: 16 (over x, z_lo), ch: 16 (over y, z_hi, core).
Axes of the slice: x: 4, y: 4, z: 8 (z_hi: 2, z_lo: 4; z = z_hi * 4 + z_lo), core: 2. Of those that a mesh axis runs over, the one named last changes fastest.
Arguments:
- features: bfloat16 [3, 2048, 8192], P(None, 'ch', 'ctx'), may hold values from -6 to 6
- short_taps: float32 [3, 2048, 3], P(None, 'ch'), may hold values from -3.5 to 3.5
- decay: float32 [2048, 16], P(('ch', 'ctx')), may hold values from 6.1035156e-05 to 0.05
- residue: float32 [2048, 16], P(('ch', 'ctx')), may hold values from -0.32 to 0.32
- skip_bias: float32 [2048], P('ch'), may hold values from -4 to 4
- out_weight: bfloat16 [2048, 2048], P('ch'), may hold values from -0.125 to 0.125
Outputs:
- output: bfloat16 [2048, 8192], P('ch', 'ctx')
All inputs are finite; a program needn't handle non-finite values.
Results may differ from a plain program's by a relative error of at most 0.013.
Values may be sent and summed in bfloat16 or wider, within the bound.
No kernel may reach another device: no remote copies, remote signals or barrier semaphores. Data moves between devices by JAX's collectives and lax.ppermute only.
A program may use at most 64 MiB of HBM per device.

v0:
```python
import functools

import jax
import jax.numpy as jnp
from jax import lax
from jax.experimental import pallas as pl
from jax.experimental.pallas import tpu as pltpu
from jax.sharding import Mesh
from jax.sharding import PartitionSpec as P

CTX = ("x", "zl")
CH = ("y", "zh", "c")
LANES = 128
f32 = jnp.float32
bf16 = jnp.bfloat16


def shift(value, axis, steps):
    count = lax.axis_size(axis)
    return lax.ppermute(value, axis, [(i, (i + steps) % count) for i in range(count)])


def split_store(ref, index, value):
    high = value.astype(bf16)
    ref[(0,) + index] = high
    ref[(1,) + index] = (value - high.astype(f32)).astype(bf16)


def prep_body(decay, residue, decay_row, residue_row, bias, toeplitz, enter, leave, powers):
    owned, modes = decay.shape
    lane = lax.broadcasted_iota(jnp.int32, (owned, LANES), 1)
    moment = lane.astype(f32)
    impulse = jnp.where(lane == 0, bias[...], 0.0)
    for n in range(modes):
        impulse = impulse + residue[:, n : n + 1] * jnp.exp(-decay[:, n : n + 1] * moment)
    row = lax.broadcasted_iota(jnp.int32, (LANES, LANES), 0)
    col = lax.broadcasted_iota(jnp.int32, (LANES, LANES), 1)
    rate = decay_row[...]
    into = jnp.exp(-rate * (LANES - 1 - row).astype(f32))
    out_of = jnp.transpose(residue_row[...] * jnp.exp(-rate * (row + 1).astype(f32)))
    for c in range(owned):
        spread = jnp.broadcast_to(impulse[c : c + 1, :], (LANES, LANES))
        rolled = pltpu.roll(spread, 0, 1, stride=1, stride_axis=0)
        split_store(toeplitz, (c,), jnp.where(col >= row, rolled, 0.0))
        part = pl.ds(c * LANES, LANES)
        split_store(enter, (part, slice(None)), jnp.where(col // modes == c, into, 0.0))
        split_store(leave, (slice(None), part), jnp.where(row // modes == c, out_of, 0.0))
    for i in range(8):
        powers[i : i + 1, :] = jnp.exp(-rate * float(LANES << i))


def dot(a, b):
    return jnp.dot(a, b, preferred_element_type=f32)


def conv_body(kv, taps, toeplitz, enter, leave, powers, out, mixed_buf, conv_buf):
    shards, _, owned, tokens = kv.shape
    per = tokens // LANES
    blocks = shards * per
    lane = lax.broadcasted_iota(jnp.int32, (owned, LANES), 1)
    weights = [[taps[s, :, j : j + 1] for j in range(3)] for s in range(2)]
    zero = jnp.zeros((owned, LANES), f32)
    last = [(zero, zero), (zero, zero)]
    for b in range(blocks):
        k, j = divmod(b, per)
        product = None
        for s in range(2):
            now = kv[k, s, :, j * LANES : (j + 1) * LANES].astype(f32)
            one, two = pltpu.roll(now, 1, 1), pltpu.roll(now, 2, 1)
            w = weights[s]
            value = (
                w[0] * now
                + w[1] * jnp.where(lane < 1, last[s][0], one)
                + w[2] * jnp.where(lane < 2, last[s][1], two)
            )
            last[s] = (one, two)
            product = value if product is None else product * value
        mixed_buf[b] = product.astype(bf16).astype(f32)
    mixed = [mixed_buf[:, c, :].astype(bf16) for c in range(owned)]
    whole = jnp.concatenate(mixed, axis=1)
    state = dot(whole, enter[0]) + dot(whole, enter[1])
    row = lax.broadcasted_iota(jnp.int32, (blocks, LANES), 0)
    step, i = 1, 0
    while step < blocks:
        moved = jnp.where(row < step, 0.0, pltpu.roll(state, step, 0))
        state = state + powers[i : i + 1, :] * moved
        step, i = step * 2, i + 1
    state = jnp.where(row < 1, 0.0, pltpu.roll(state, 1, 0))
    high = state.astype(bf16)
    low = (state - high.astype(f32)).astype(bf16)
    for c in range(owned):
        part = pl.ds(c * LANES, LANES)
        value = dot(mixed[c], toeplitz[0, c]) + dot(mixed[c], toeplitz[1, c])
        value = value + dot(high, leave[0, :, part]) + dot(high, leave[1, :, part])
        conv_buf[:, c, :] = value + dot(low, leave[0, :, part])
    for b in range(blocks):
        k, j = divmod(b, per)
        value = conv_buf[b].astype(bf16)
        for h in range(out.shape[0]):
            out[h, k, :, j * LANES : (j + 1) * LANES] = value


def merge_body(y_unused, own, other, core, weight, out0, out1, out2, out3, gathered):
    half = own.shape[0] // 2
    me = core[0]
    for h in range(2):
        at = pl.multiple_of(h * 2 * half + me * half, half)
        gathered[pl.ds(at, half), :] = own[h * half : (h + 1) * half, :]
        at = pl.multiple_of(h * 2 * half + (1 - me) * half, half)
        gathered[pl.ds(at, half), :] = other[h * half : (h + 1) * half, :]


def vmem(count):
    return [pl.BlockSpec(memory_space=pltpu.VMEM)] * count


def convolve(kv, taps, decay, residue, bias, copies):
    owned, modes = decay.shape
    shards, _, _, tokens = kv.shape
    wide = owned * LANES
    mats = pl.pallas_call(
        prep_body,
        out_shape=(
            jax.ShapeDtypeStruct((2, owned, LANES, LANES), bf16),
            jax.ShapeDtypeStruct((2, wide, LANES), bf16),
            jax.ShapeDtypeStruct((2, LANES, wide), bf16),
            jax.ShapeDtypeStruct((8, LANES), f32),
        ),
        in_specs=vmem(5),
        out_specs=tuple(vmem(4)),
        cost_estimate=pl.CostEstimate(flops=2000000, bytes_accessed=1600000, transcendentals=70000),
        name="prep",
    )(decay, residue, decay.reshape(1, wide // modes * modes // LANES * modes), residue.reshape(1, owned * modes), bias)
    return mats


def conv_call(kv, taps, mats, copies):
    shards, _, owned, tokens = kv.shape
    blocks = shards * tokens // LANES
    return pl.pallas_call(
        conv_body,
        out_shape=jax.ShapeDtypeStruct((copies, shards, owned, tokens), bf16),
        in_specs=vmem(6),
        out_specs=vmem(1)[0],
        scratch_shapes=[pltpu.VMEM((blocks, owned, LANES), f32)] * 2,
        cost_estimate=pl.CostEstimate(flops=100000000, bytes_accessed=2500000, transcendentals=0),
        name="conv",
    )(kv, taps, *mats)


def merge_kernel(own, other, core, w0, w1, w2, w3, o0, o1, o2, o3, gathered):
    half = own.shape[0] // 2
    me = core[0]
    for h in range(2):
        at = pl.multiple_of((2 * h + me) * half, half)
        gathered[pl.ds(at, half), :] = own[h * half : (h + 1) * half, :]
        at = pl.multiple_of((2 * h + 1 - me) * half, half)
        gathered[pl.ds(at, half), :] = other[h * half : (h + 1) * half, :]
    for w, o in ((w2, o2), (w1, o1), (w3, o3), (w0, o0)):
        o[...] = dot(w[...], gathered[...]).astype(o.dtype)


def local(features, short_taps, decay, residue, skip_bias, out_weight):
    _, channels, tokens = features.shape
    shards = lax.axis_size("x") * lax.axis_size("zl")
    owned, modes = decay.shape
    ctx = lax.axis_index("x") * lax.axis_size("zl") + lax.axis_index("zl")
    y, zh, core = (lax.axis_index(a) for a in CH)
    ys = lax.axis_size("y")
    cols = out_weight.shape[1] // ys

    sent = features[1:].reshape(2, shards, owned, tokens).transpose(1, 0, 2, 3)
    kv = lax.all_to_all(sent, CTX, 0, 0, tiled=True)

    weights = [lax.dynamic_slice_in_dim(out_weight, y * cols, cols, 1)]
    for d in range(1, ys):
        block = lax.dynamic_slice_in_dim(out_weight, (y + ys - d) % ys * cols, cols, 1)
        weights.append(shift(block, "y", -d))

    total = shards
    rim = lax.ppermute(features[0, :, tokens - 2 :], CTX, [(i, i + 1) for i in range(total - 1)])
    longer = jnp.concatenate([rim, features[0]], axis=1).astype(f32)
    query = sum(
        short_taps[0, :, j : j + 1] * longer[:, 2 - j : 2 - j + tokens] for j in range(3)
    ).astype(bf16)
    query_other = shift(query, "zh", 1)

    taps = lax.dynamic_slice_in_dim(short_taps[1:], ctx * owned, owned, 1)
    bias = lax.dynamic_slice_in_dim(skip_bias, ctx * owned, owned, 0)[:, None]
    mats = pl.pallas_call(
        prep_body,
        out_shape=(
            jax.ShapeDtypeStruct((2, owned, LANES, LANES), bf16),
            jax.ShapeDtypeStruct((2, owned * LANES, LANES), bf16),
            jax.ShapeDtypeStruct((2, LANES, owned * LANES), bf16),
            jax.ShapeDtypeStruct((8, LANES), f32),
        ),
        in_specs=vmem(5),
        out_specs=tuple(vmem(4)),
        cost_estimate=pl.CostEstimate(flops=2000000, bytes_accessed=1600000, transcendentals=70000),
        name="prep",
    )(decay, residue, decay.reshape(1, -1), residue.reshape(1, -1), bias)
    conv = conv_call(kv, taps, mats, 2)
    conv = lax.all_to_all(
        conv.reshape(2 * shards, owned, tokens), ("zh",) + CTX, 0, 0, tiled=True
    ).reshape(2, channels, tokens)
    first = zh == 0
    both = jnp.stack([jnp.where(first, query, query_other), jnp.where(first, query_other, query)])
    gated = (both.astype(f32) * conv.astype(f32)).astype(bf16).reshape(2 * channels, tokens)
    gated_other = shift(gated, "c", 1)
    rows = out_weight.shape[0]
    parts = pl.pallas_call(
        merge_kernel,
        out_shape=(jax.ShapeDtypeStruct((rows, tokens), f32),)
        + (jax.ShapeDtypeStruct((rows, tokens), bf16),) * 3,
        in_specs=vmem(2) + [pl.BlockSpec(memory_space=pltpu.SMEM)] + vmem(4),
        out_specs=tuple(vmem(4)),
        scratch_shapes=[pltpu.VMEM((4 * channels, tokens), bf16)],
        cost_estimate=pl.CostEstimate(flops=300000000, bytes_accessed=2500000, transcendentals=0),
        name="merge",
    )(gated, gated_other, core.reshape(1), *weights)
    total = parts[0]
    for d in range(1, ys):
        total = total + shift(parts[d], "y", d).astype(f32)
    return total.astype(bf16)


def solution(mesh):
    split = Mesh(mesh.devices.reshape(4, 4, 4, 2, 2), CTX + CH)
    in_specs = (
        P(None, CH, CTX),
        P(None, CH, None),
        P(CH + CTX, None),
        P(CH + CTX, None),
        P(CH),
        P(CH, None),
    )
    return jax.shard_map(local, mesh=split, in_specs=in_specs, out_specs=P(CH, CTX), check_vma=False)
```

profile of v0, /device:TPU:1, one launch (start us, length us, event | category | flops | bytes accessed | tf_op | source)
XLA Modules:
  0.0 80.5 jit_solution(15889082439691922194)
XLA Ops:
  0.0 1.7 %copy_bitcast_fusion = bf16[16,2,8,512]{3,2,1,0:T(8,128)(2,1)} fusion(bf16[3,128,512]{2,1,0:T(8,128)(2,1)} %param.6), kind=kLoop, calls=%fused_computation.9 | loop fusion | bytes 524288 | tf_op jit(solution)/shard_map/transpose | solution.py:172
  1.7 9.0 %all-to-all-start = ((bf16[16,2,8,512]{3,2,1,0:T(8,128)(2,1)}), bf16[16,2,8,512]{3,2,1,0:T(8,128)(2,1)S(1)}, u32[]{:S(2)}, u32[]{:S(2)}) async-start(bf16[16,2,8,512]{3,2,1,0:T(8,128)(2,1)} %copy_bitcast_fusion), calls=%async_computation | async-start | bytes 524288 | tf_op jit(solution)/shard_map/all_to_all | solution.py:173
  10.7 0.8 %slice_bitcast_fusion.2 = bf16[128,2]{1,0:T(8,128)(2,1)S(1)} fusion(bf16[3,128,512]{2,1,0:T(8,128)(2,1)} %param.6), kind=kLoop, calls=%fused_computation.16 | loop fusion | bytes 1024 | tf_op jit(solution)/shard_map/squeeze | solution.py:181
  11.6 3.3 %collective-permute-start = (bf16[128,2]{1,0:T(8,128)(2,1)S(1)}, bf16[128,2]{1,0:T(8,128)(2,1)S(1)}, u32[]{:S(2)}, u32[]{:S(2)}) collective-permute-start(bf16[128,2]{1,0:T(8,128)(2,1)S(1)} %slice_bitcast_fusion.2), channel_id=1, source_target_pairs={{0,16},{16,32},{32,48},{48,64},{64,80},{80,96},{96,112},{112,128},... | collective-permute-start | bytes 1544 | tf_op jit(solution)/shard_map/ppermute | solution.py:181
  14.9 0.0 copy-start.4
  14.9 0.7 copy-done.4
  15.6 0.1 dynamic-slice_bitcast_fusion
  15.6 0.7 slice-done
  16.3 0.1 constant_dynamic-slice_fusion.4
  16.4 0.9 %slice_bitcast_fusion.1 = bf16[128,512]{1,0:T(8,128)(2,1)S(1)} fusion(bf16[3,128,512]{2,1,0:T(8,128)(2,1)} %param.6), kind=kLoop, calls=%fused_computation.15 | loop fusion | bytes 262144 | tf_op jit(solution)/shard_map/squeeze | solution.py:182
  17.3 0.0 copy-start.5
  17.3 0.7 copy.12.taps
  18.0 0.6 reshape.27.decay_row
  18.6 0.1 copy-done.6
  18.7 0.6 reshape.28.residue_row
  19.3 0.7 copy.11.bias
  20.0 2.2 %prep.1 = (bf16[2,8,128,128]{3,2,1,0:T(8,128)(2,1)}, bf16[2,1024,128]{2,1,0:T(8,128)(2,1)}, bf16[2,128,1024]{2,1,0:T(8,128)(2,1)}, f32[8,128]{1,0:T(8,128)}) custom-call(f32[8,16]{1,0:T(8,128)} %decay.1, f32[8,16]{1,0:T(8,128)} %residue.1, f32[1,128]{1,0:T(1,128)} %reshape.27.decay_row, f32[1,128]{1,0:T(1,128)} %reshape.28.residue_row, f32[8,1]{1,0:T(8,128)} %copy.11.bias), custom_call_target="tpu_custom_call" | custom-call | flops 2000000 | bytes 1600000 | tf_op jit(solution)/shard_map/prep/pallas_call | solution.py:190
  22.2 0.0 collective-permute-done
  22.2 0.1 maximum_convert_fusion
  22.3 0.0 all-to-all-done.kv
  22.3 0.7 copy-done.1
  23.0 3.4 %conv.1 = bf16[2,16,8,512]{3,2,1,0:T(8,128)(2,1)} custom-call(bf16[16,2,8,512]{3,2,1,0:T(8,128)(2,1)} %copy-done.1, f32[2,8,3]{2,1,0:T(8,128)} %copy.12.taps, bf16[2,8,128,128]{3,2,1,0:T(8,128)(2,1)} %get-tuple-element.13.toeplitz, bf16[2,1024,128]{2,1,0:T(8,128)(2,1)} %get-tuple-element.14.enter, bf16[2,128,1024]{2,1,0:T(8,128)(2,1)} %get-tuple-element.15.leave, ...), custom_call_target="tpu_custom_call" | custom-call | flops 100000000 | bytes 2500000 | tf_op jit(solution)/shard_map/conv/pallas_call | solution.py:140
  26.5 8.3 %all-to-all-start.1 = ((bf16[32,8,512]{2,1,0:T(8,128)(2,1)}), bf16[32,8,512]{2,1,0:T(8,128)(2,1)S(1)}, u32[]{:S(2)}, u32[]{:S(2)}) async-start(bf16[32,8,512]{2,1,0:T(8,128)(2,1)} %bitcast.29), calls=%async_computation.1 | async-start | bytes 524288 | tf_op jit(solution)/shard_map/all_to_all | solution.py:204
  34.7 0.3 fusion.2
  35.0 5.2 %collective-permute-start.1 = (bf16[128,512]{1,0:T(8,128)(2,1)S(1)}, bf16[128,512]{1,0:T(8,128)(2,1)S(1)}, u32[]{:S(2)}, u32[]{:S(2)}) collective-permute-start(bf16[128,512]{1,0:T(8,128)(2,1)S(1)} %fusion.2), channel_id=1, source_target_pairs={{0,2},{2,0},{1,3},{3,1},{4,6},{6,4},{5,7},{7,5},{8,10},{10,8},{9,1... | collective-permute-start | bytes 393224 | tf_op jit(solution)/shard_map/ppermute | solution.py:20
  40.2 10.1 %collective-permute-done.1 = bf16[128,512]{1,0:T(8,128)(2,1)S(1)} collective-permute-done((bf16[128,512]{1,0:T(8,128)(2,1)S(1)}, bf16[128,512]{1,0:T(8,128)(2,1)S(1)}, u32[]{:S(2)}, u32[]{:S(2)}) %collective-permute-start.1) | collective-permute-done | bytes 131104 | tf_op jit(solution)/shard_map/ppermute | solution.py:20
  50.3 0.3 select_bitcast_fusion.1
  50.6 0.0 copy-start.2
  50.6 0.1 fusion.own
  50.7 2.6 %collective-permute-start.2 = (bf16[256,512]{1,0:T(8,128)(2,1)S(1)}, bf16[256,512]{1,0:T(8,128)(2,1)S(1)}, u32[]{:S(2)}, u32[]{:S(2)}) collective-permute-start(bf16[256,512]{1,0:T(8,128)(2,1)S(1)} %fusion.own), channel_id=1, source_target_pairs={{0,1},{1,0},{2,3},{3,2},{4,5},{5,4},{6,7},{7,6},{8,9},{9,8},{10,11... | collective-permute-start | bytes 786440 | tf_op jit(solution)/shard_map/ppermute | solution.py:20
  53.4 0.7 constant_dynamic-slice_fusion
  54.1 2.7 %collective-permute-start.3 = (bf16[128,512]{1,0:T(8,128)(2,1)S(1)}, bf16[128,512]{1,0:T(8,128)(2,1)S(1)}, u32[]{:S(2)}, u32[]{:S(2)}) collective-permute-start(bf16[128,512]{1,0:T(8,128)(2,1)S(1)} %get-tuple-element.22), channel_id=1, source_target_pairs={{0,12},{4,0},{8,4},{12,8},{1,13},{5,1},{9,5},{13,9},{2,14},{6,2},{... | collective-permute-start | bytes 393224 | tf_op jit(solution)/shard_map/ppermute | solution.py:20
  56.8 0.3 collective-permute-start.4
  57.2 0.7 collective-permute-start.5
  57.9 3.9 %collective-permute-done.3.w1 = bf16[128,512]{1,0:T(8,128)(2,1)S(1)} collective-permute-done((bf16[128,512]{1,0:T(8,128)(2,1)S(1)}, bf16[128,512]{1,0:T(8,128)(2,1)S(1)}, u32[]{:S(2)}, u32[]{:S(2)}) %collective-permute-start.3) | collective-permute-done | bytes 131104 | tf_op jit(solution)/shard_map/ppermute | solution.py:20
  61.7 0.5 collective-permute-done.4.w2
  62.2 3.9 %collective-permute-done.5.w3 = bf16[128,512]{1,0:T(8,128)(2,1)S(1)} collective-permute-done((bf16[128,512]{1,0:T(8,128)(2,1)S(1)}, bf16[128,512]{1,0:T(8,128)(2,1)S(1)}, u32[]{:S(2)}, u32[]{:S(2)}) %collective-permute-start.5) | collective-permute-done | bytes 131104 | tf_op jit(solution)/shard_map/ppermute | solution.py:20
  66.2 0.0 collective-permute-done.2.other
  66.2 0.6 copy-done.10
  66.8 0.1 copy-done.7
  66.9 2.4 %merge.1 = (f32[128,512]{1,0:T(8,128)}, bf16[128,512]{1,0:T(8,128)(2,1)}, bf16[128,512]{1,0:T(8,128)(2,1)}, bf16[128,512]{1,0:T(8,128)(2,1)}) custom-call(bf16[256,512]{1,0:T(8,128)(2,1)} %copy-done.3, bf16[256,512]{1,0:T(8,128)(2,1)} %copy-done.7, s32[1]{0:T(128)} %bitcast.13.core, bf16[128,512]{1,0:T(8,128)(2,1)} %get-tuple-element.23.w0, ...), custom_call_target="tpu_custom_call" | custom-call | flops 300000000 | bytes 2500000 | tf_op jit(solution)/shard_map/merge/pallas_call | solution.py:212
  69.3 0.0 collective-permute-start.8
  69.3 0.1 collective-permute-start.7
  69.4 1.4 %collective-permute-start.6 = (bf16[128,512]{1,0:T(8,128)(2,1)}, bf16[128,512]{1,0:T(8,128)(2,1)S(1)}, u32[]{:S(2)}, u32[]{:S(2)}) collective-permute-start(bf16[128,512]{1,0:T(8,128)(2,1)} %get-tuple-element.18), channel_id=1, source_target_pairs={{0,4},{4,8},{8,12},{12,0},{1,5},{5,9},{9,13},{13,1},{2,6},{6,10},{... | collective-permute-start | bytes 393224 | tf_op jit(solution)/shard_map/ppermute | solution.py:20
  70.8 2.9 %collective-permute-done.8 = bf16[128,512]{1,0:T(8,128)(2,1)S(1)} collective-permute-done((bf16[128,512]{1,0:T(8,128)(2,1)}, bf16[128,512]{1,0:T(8,128)(2,1)S(1)}, u32[]{:S(2)}, u32[]{:S(2)}) %collective-permute-start.8) | collective-permute-done | bytes 131104 | tf_op jit(solution)/shard_map/ppermute | solution.py:20
  73.7 1.3 %collective-permute-done.7 = bf16[128,512]{1,0:T(8,128)(2,1)S(1)} collective-permute-done((bf16[128,512]{1,0:T(8,128)(2,1)}, bf16[128,512]{1,0:T(8,128)(2,1)S(1)}, u32[]{:S(2)}, u32[]{:S(2)}) %collective-permute-start.7) | collective-permute-done | bytes 131104 | tf_op jit(solution)/shard_map/ppermute | solution.py:20
  75.0 3.8 %collective-permute-done.6 = bf16[128,512]{1,0:T(8,128)(2,1)S(1)} collective-permute-done((bf16[128,512]{1,0:T(8,128)(2,1)}, bf16[128,512]{1,0:T(8,128)(2,1)S(1)}, u32[]{:S(2)}, u32[]{:S(2)}) %collective-permute-start.6) | collective-permute-done | bytes 131104 | tf_op jit(solution)/shard_map/ppermute | solution.py:20
  78.8 1.7 %add_convert_fusion = bf16[128,512]{1,0:T(8,128)(2,1)} fusion(bf16[128,512]{1,0:T(8,128)(2,1)S(1)} %collective-permute-done.8, bf16[128,512]{1,0:T(8,128)(2,1)S(1)} %collective-permute-done.7, f32[128,512]{1,0:T(8,128)} %get-tuple-element.17, bf16[128,512]{1,0:T(8,128)(2,1)S(1)} %collective-permute-done.6), kind=kLoop, calls=%fused_computation.10 | loop fusion | flops 458752 | bytes 786432 | tf_op jit(solution)/shard_map/convert_element_type | solution.py:225
  (18 shorter events, 0.1 us)
Async XLA Ops:
  0.0 15.6 %copy-start = (f32[128]{0:T(128)S(1)}, f32[128]{0:T(128)}, u32[]{:S(2)}) copy-start(f32[128]{0:T(128)} %param.10) | copy-start | bytes 1540
  1.7 20.6 %all-to-all-start = ((bf16[16,2,8,512]{3,2,1,0:T(8,128)(2,1)}), bf16[16,2,8,512]{3,2,1,0:T(8,128)(2,1)S(1)}, u32[]{:S(2)}, u32[]{:S(2)}) async-start(bf16[16,2,8,512]{3,2,1,0:T(8,128)(2,1)} %copy_bitcast_fusion), calls=%async_computation | async-start | bytes 524288 | tf_op jit(solution)/shard_map/all_to_all | solution.py:173
  11.6 10.6 %collective-permute-start = (bf16[128,2]{1,0:T(8,128)(2,1)S(1)}, bf16[128,2]{1,0:T(8,128)(2,1)S(1)}, u32[]{:S(2)}, u32[]{:S(2)}) collective-permute-start(bf16[128,2]{1,0:T(8,128)(2,1)S(1)} %slice_bitcast_fusion.2), channel_id=1, source_target_pairs={{0,16},{16,32},{32,48},{48,64},{64,80},{80,96},{96,112},{112,128},... | collective-permute-start | bytes 1544 | tf_op jit(solution)/shard_map/ppermute | solution.py:181
  14.9 0.7 copy-start.4
  15.6 0.7 slice-start
  17.3 0.7 copy-start.5
  18.0 0.7 copy-start.6
  22.3 0.7 copy-start.1
  26.5 24.2 %all-to-all-start.1 = ((bf16[32,8,512]{2,1,0:T(8,128)(2,1)}), bf16[32,8,512]{2,1,0:T(8,128)(2,1)S(1)}, u32[]{:S(2)}, u32[]{:S(2)}) async-start(bf16[32,8,512]{2,1,0:T(8,128)(2,1)} %bitcast.29), calls=%async_computation.1 | async-start | bytes 524288 | tf_op jit(solution)/shard_map/all_to_all | solution.py:204
  35.0 15.3 %collective-permute-start.1 = (bf16[128,512]{1,0:T(8,128)(2,1)S(1)}, bf16[128,512]{1,0:T(8,128)(2,1)S(1)}, u32[]{:S(2)}, u32[]{:S(2)}) collective-permute-start(bf16[128,512]{1,0:T(8,128)(2,1)S(1)} %fusion.2), channel_id=1, source_target_pairs={{0,2},{2,0},{1,3},{3,1},{4,6},{6,4},{5,7},{7,5},{8,10},{10,8},{9,1... | collective-permute-start | bytes 393224 | tf_op jit(solution)/shard_map/ppermute | solution.py:20
  50.6 2.8 %copy-start.2 = (bf16[128,2048]{1,0:T(8,128)(2,1)S(1)}, bf16[128,2048]{1,0:T(8,128)(2,1)}, u32[]{:S(2)}) copy-start(bf16[128,2048]{1,0:T(8,128)(2,1)} %param.11) | copy-start | bytes 1572868
  50.7 3.3 %copy-start.3 = (bf16[256,512]{1,0:T(8,128)(2,1)}, bf16[256,512]{1,0:T(8,128)(2,1)S(1)}, u32[]{:S(2)}) copy-start(bf16[256,512]{1,0:T(8,128)(2,1)S(1)} %fusion.own) | copy-start | bytes 786436
  50.7 15.4 %collective-permute-start.2 = (bf16[256,512]{1,0:T(8,128)(2,1)S(1)}, bf16[256,512]{1,0:T(8,128)(2,1)S(1)}, u32[]{:S(2)}, u32[]{:S(2)}) collective-permute-start(bf16[256,512]{1,0:T(8,128)(2,1)S(1)} %fusion.own), channel_id=1, source_target_pairs={{0,1},{1,0},{2,3},{3,2},{4,5},{5,4},{6,7},{7,6},{8,9},{9,8},{10,11... | collective-permute-start | bytes 786440 | tf_op jit(solution)/shard_map/ppermute | solution.py:20
  54.1 7.6 %collective-permute-start.3 = (bf16[128,512]{1,0:T(8,128)(2,1)S(1)}, bf16[128,512]{1,0:T(8,128)(2,1)S(1)}, u32[]{:S(2)}, u32[]{:S(2)}) collective-permute-start(bf16[128,512]{1,0:T(8,128)(2,1)S(1)} %get-tuple-element.22), channel_id=1, source_target_pairs={{0,12},{4,0},{8,4},{12,8},{1,13},{5,1},{9,5},{13,9},{2,14},{6,2},{... | collective-permute-start | bytes 393224 | tf_op jit(solution)/shard_map/ppermute | solution.py:20
  56.8 5.4 %collective-permute-start.4 = (bf16[128,512]{1,0:T(8,128)(2,1)S(1)}, bf16[128,512]{1,0:T(8,128)(2,1)S(1)}, u32[]{:S(2)}, u32[]{:S(2)}) collective-permute-start(bf16[128,512]{1,0:T(8,128)(2,1)S(1)} %get-tuple-element.24), channel_id=1, source_target_pairs={{0,8},{4,12},{8,0},{12,4},{1,9},{5,13},{9,1},{13,5},{2,10},{6,14},... | collective-permute-start | bytes 393224 | tf_op jit(solution)/shard_map/ppermute | solution.py:20
  57.2 9.0 %collective-permute-start.5 = (bf16[128,512]{1,0:T(8,128)(2,1)S(1)}, bf16[128,512]{1,0:T(8,128)(2,1)S(1)}, u32[]{:S(2)}, u32[]{:S(2)}) collective-permute-start(bf16[128,512]{1,0:T(8,128)(2,1)S(1)} %get-tuple-element.21), channel_id=1, source_target_pairs={{0,4},{4,8},{8,12},{12,0},{1,5},{5,9},{9,13},{13,1},{2,6},{6,10},{... | collective-permute-start | bytes 393224 | tf_op jit(solution)/shard_map/ppermute | solution.py:20
  61.7 4.5 %copy-start.8 = (bf16[128,512]{1,0:T(8,128)(2,1)}, bf16[128,512]{1,0:T(8,128)(2,1)S(1)}, u32[]{:S(2)}) copy-start(bf16[128,512]{1,0:T(8,128)(2,1)S(1)} %collective-permute-done.3.w1) | copy-start | bytes 393220
  62.2 3.9 %copy-start.9 = (bf16[128,512]{1,0:T(8,128)(2,1)}, bf16[128,512]{1,0:T(8,128)(2,1)S(1)}, u32[]{:S(2)}) copy-start(bf16[128,512]{1,0:T(8,128)(2,1)S(1)} %collective-permute-done.4.w2) | copy-start | bytes 393220
  66.2 0.7 copy-start.10
  66.2 0.8 copy-start.7
  69.3 4.4 %collective-permute-start.8 = (bf16[128,512]{1,0:T(8,128)(2,1)}, bf16[128,512]{1,0:T(8,128)(2,1)S(1)}, u32[]{:S(2)}, u32[]{:S(2)}) collective-permute-start(bf16[128,512]{1,0:T(8,128)(2,1)} %get-tuple-element.20), channel_id=1, source_target_pairs={{0,12},{4,0},{8,4},{12,8},{1,13},{5,1},{9,5},{13,9},{2,14},{6,2},{... | collective-permute-start | bytes 393224 | tf_op jit(solution)/shard_map/ppermute | solution.py:20
  69.3 5.7 %collective-permute-start.7 = (bf16[128,512]{1,0:T(8,128)(2,1)}, bf16[128,512]{1,0:T(8,128)(2,1)S(1)}, u32[]{:S(2)}, u32[]{:S(2)}) collective-permute-start(bf16[128,512]{1,0:T(8,128)(2,1)} %get-tuple-element.19), channel_id=1, source_target_pairs={{0,8},{4,12},{8,0},{12,4},{1,9},{5,13},{9,1},{13,5},{2,10},{6,14},... | collective-permute-start | bytes 393224 | tf_op jit(solution)/shard_map/ppermute | solution.py:20
  69.4 9.4 %collective-permute-start.6 = (bf16[128,512]{1,0:T(8,128)(2,1)}, bf16[128,512]{1,0:T(8,128)(2,1)S(1)}, u32[]{:S(2)}, u32[]{:S(2)}) collective-permute-start(bf16[128,512]{1,0:T(8,128)(2,1)} %get-tuple-element.18), channel_id=1, source_target_pairs={{0,4},{4,8},{8,12},{12,0},{1,5},{5,9},{9,13},{13,1},{2,6},{6,10},{... | collective-permute-start | bytes 393224 | tf_op jit(solution)/shard_map/ppermute | solution.py:20
where the time goes:
time: 81.1 us; the launch traced here: 80.5 us
  starting transfers between devices  33.7 us (42%)
  waiting for transfers between devices  26.4 us (33%)
  local copies, waits for them, and re-layouts  9.8 us (12%)
  Pallas kernels  8.04 us (10%)
  other arithmetic  2.42 us (3%)
    ppermute x8, waiting for transfers between devices, shift(): lax.ppermute(value, axis, [(i, (i + steps) % count) for i in range(count)])  26.4 us
    ppermute x8, starting transfers between devices, shift(): lax.ppermute(value, axis, [(i, (i + steps) % count) for i in range(count)])  13.1 us
    all_to_all x1, starting transfers between devices, local(): kv = lax.all_to_all(sent, CTX, 0, 0, tiled=True)  9.01 us
    all_to_all x1, starting transfers between devices, local(): lax.all_to_all(conv.reshape(2 * shards, owned, tokens), ('zh',) + CTX, 0,...  8.29 us
    pallas_call x1, Pallas kernels, conv_call(): pl.pallas_call(conv_body, out_shape=jax.ShapeDtypeStruct((copies, shards,...  3.42 us
    ppermute x1, starting transfers between devices, local(): lax.ppermute(features[0, :, tokens - 2:], CTX, [(i, i + 1) for i in range...  3.26 us
    unnamed x23, local copies, waits for them, and re-layouts  2.96 us
    pallas_call x1, Pallas kernels, local(): pl.pallas_call(merge_kernel, out_shape=(jax.ShapeDtypeStruct((rows, token...  2.41 us
  transfers between devices with their start and end apart: 11, of which 7 were waited for; matrix products, arithmetic and copies ran while one was open for 7% of the time, Pallas kernels for 3%

commit v1 on v0

v1 whole, which is shorter than its diff:
```python
import jax
import jax.numpy as jnp
from jax import lax
from jax.experimental import pallas as pl
from jax.experimental.pallas import tpu as pltpu
from jax.sharding import Mesh
from jax.sharding import PartitionSpec as P

CTX = ("x", "zl")
CH = ("y", "zh", "c")
GO = ("x", "zl")
BACK = ("x", "zl", "zh")
LANES = 128
TAPS = 3
f32 = jnp.float32
bf16 = jnp.bfloat16
in_vmem = pl.BlockSpec(memory_space=pltpu.VMEM)


def shift(value, axis, steps):
    count = lax.axis_size(axis)
    return lax.ppermute(value, axis, [(i, (i + steps) % count) for i in range(count)])


def place(order, k, h=0):
    at = {"x": k // 4, "zl": k % 4, "zh": h}
    size = {"x": 4, "zl": 4, "zh": 2}
    index = 0
    for axis in order:
        index = index * size[axis] + at[axis]
    return index


def near(value):
    return pltpu.with_memory_space_constraint(value, pltpu.VMEM)


def params(**kwargs):
    return pltpu.CompilerParams(vmem_limit_bytes=16 << 20, **kwargs)


def ctx_index():
    return lax.axis_index("x") * lax.axis_size("zl") + lax.axis_index("zl")


def split_store(ref, index, value):
    high = value.astype(bf16)
    ref[(0,) + index] = high
    ref[(1,) + index] = (value - high.astype(f32)).astype(bf16)


def pack_body(features_hbm, taps_hbm, sent, features, short_taps, sem):
    copies = [pltpu.make_async_copy(taps_hbm, short_taps, sem.at[3])]
    for s in range(3):
        copies.append(pltpu.make_async_copy(features_hbm.at[s], features.at[s], sem.at[s]))
    for copy in copies:
        copy.start()
    for copy in copies:
        copy.wait()
    _, channels, tokens = features.shape
    shards, owned, _ = sent.shape
    per = tokens // LANES
    rows = [short_taps[s] for s in range(3)]
    filler = jnp.zeros((LANES - 3 * TAPS, channels), f32)
    columns = jnp.transpose(jnp.concatenate(rows + [filler], axis=0))
    lane = lax.broadcasted_iota(jnp.int32, (owned, LANES), 1)
    zero = jnp.zeros((owned, LANES), f32)
    for k in range(shards):
        at = slice(k * owned, (k + 1) * owned)
        rims = zero
        value = [[], [], []]
        for s in range(3):
            w = [
                jnp.broadcast_to(columns[at, i : i + 1], (owned, LANES))
                for i in range(s * TAPS, (s + 1) * TAPS)
            ]
            last = (zero, zero)
            for j in range(per):
                now = features[s, at, j * LANES : (j + 1) * LANES].astype(f32)
                one, two = pltpu.roll(now, 1, 1), pltpu.roll(now, 2, 1)
                value[s].append(
                    w[0] * now
                    + w[1] * jnp.where(lane < 1, last[0], one)
                    + w[2] * jnp.where(lane < 2, last[1], two)
                )
                last = (one, two)
                if j == 0:
                    head = pltpu.roll(now, 4 * s, 1) if s else now
                    rims = jnp.where((lane == 4 * s) | (lane == 4 * s + 1), head, rims)
                if j == per - 1:
                    tail = pltpu.roll(now, 4 * s + 4, 1)
                    rims = jnp.where((lane == 4 * s + 2) | (lane == 4 * s + 3), tail, rims)
        for j in range(per):
            part = slice(j * LANES, (j + 1) * LANES)
            sent[place(GO, k), :, part] = (value[1][j] * value[2][j]).astype(bf16)
            part = slice(tokens + j * LANES, tokens + (j + 1) * LANES)
            sent[place(GO, k), :, part] = value[0][j].astype(bf16)
        sent[place(GO, k), :, 2 * tokens :] = rims.astype(bf16)


def prep_body(decay, residue, skip_bias, short_taps, toeplitz, enter, leave, powers, taps):
    owned, modes = decay.shape
    lane = lax.broadcasted_iota(jnp.int32, (owned, LANES), 1)
    sub = lax.broadcasted_iota(jnp.int32, (owned, LANES), 0)
    mine = lane == sub + ctx_index() * owned

    def own_column(values):
        picked = jnp.sum(jnp.where(mine, values, 0.0), axis=1, keepdims=True)
        return jnp.broadcast_to(picked, (owned, LANES))

    def as_row(values):
        tiled = jnp.concatenate([values] * owned, axis=1)
        return jnp.sum(jnp.where(lane // modes == sub, tiled, 0.0), axis=0, keepdims=True)

    for s in range(3):
        for j in range(TAPS):
            taps[s * TAPS + j] = own_column(short_taps[s, j : j + 1, :])
    moment = lane.astype(f32)
    impulse = jnp.where(lane == 0, own_column(skip_bias[...]), 0.0)
    rates, weights = decay[...], residue[...]
    for n in range(modes):
        impulse = impulse + weights[:, n : n + 1] * jnp.exp(-rates[:, n : n + 1] * moment)
    row = lax.broadcasted_iota(jnp.int32, (LANES, LANES), 0)
    col = lax.broadcasted_iota(jnp.int32, (LANES, LANES), 1)
    rate = as_row(rates)
    into = jnp.exp(-rate * (LANES - 1 - row).astype(f32))
    out_of = jnp.transpose(as_row(weights) * jnp.exp(-rate * (row + 1).astype(f32)))
    for c in range(owned):
        spread = jnp.broadcast_to(impulse[c : c + 1, :], (LANES, LANES))
        rolled = pltpu.roll(spread, 0, 1, stride=1, stride_axis=0)
        split_store(toeplitz, (c,), jnp.where(col >= row, rolled, 0.0))
        part = pl.ds(c * LANES, LANES)
        split_store(enter, (part, slice(None)), jnp.where(col // modes == c, into, 0.0))
        split_store(leave, (slice(None), part), jnp.where(row // modes == c, out_of, 0.0))
    for i in range(8):
        powers[i : i + 1, :] = jnp.exp(-rate * float(LANES << i))


def dot(a, b):
    return jnp.dot(a, b, preferred_element_type=f32)


def conv_body(held, taps, toeplitz, enter, leave, powers, w1, w2, w3, out, mixed_buf, query_buf, conv_buf):
    shards, owned, _ = held.shape
    tokens = out.shape[-1]
    per = tokens // LANES
    blocks = shards * per
    lane = lax.broadcasted_iota(jnp.int32, (owned, LANES), 1)
    weights = [
        jnp.where(lane < 4, taps[j], jnp.where(lane < 8, taps[TAPS + j], taps[2 * TAPS + j]))
        for j in range(TAPS)
    ]
    before = jnp.zeros((owned, LANES), f32)
    for k in range(shards):
        rims = held[place(GO, k), :, 2 * tokens :].astype(f32)
        older = pltpu.roll(before, LANES - 2, 1)
        middle = jnp.where(lane % 4 == 0, pltpu.roll(before, LANES - 3, 1), pltpu.roll(rims, 1, 1))
        head = weights[0] * rims + weights[1] * middle + weights[2] * older
        before = rims
        fixed = pltpu.roll(head, LANES - 4, 1) * pltpu.roll(head, LANES - 8, 1)
        for j in range(per):
            now = held[place(GO, k), :, j * LANES : (j + 1) * LANES].astype(f32)
            query = held[place(GO, k), :, tokens + j * LANES : tokens + (j + 1) * LANES].astype(f32)
            if j == 0:
                now = jnp.where(lane < 2, fixed.astype(bf16).astype(f32), now)
                query = jnp.where(lane < 2, head, query)
            mixed_buf[k * per + j] = now
            query_buf[k * per + j] = query
    mixed = [mixed_buf[:, c, :].astype(bf16) for c in range(owned)]
    whole = jnp.concatenate(mixed, axis=1)
    state = dot(whole, enter[0]) + dot(whole, enter[1])
    row = lax.broadcasted_iota(jnp.int32, (blocks, LANES), 0)
    step, i = 1, 0
    while step < blocks:
        moved = jnp.where(row < step, 0.0, pltpu.roll(state, step, 0))
        state = state + powers[i : i + 1, :] * moved
        step, i = step * 2, i + 1
    state = jnp.where(row < 1, 0.0, pltpu.roll(state, 1, 0))
    high = state.astype(bf16)
    low = (state - high.astype(f32)).astype(bf16)
    for c in range(owned):
        part = pl.ds(c * LANES, LANES)
        value = dot(mixed[c], toeplitz[0, c]) + dot(mixed[c], toeplitz[1, c])
        value = value + dot(high, leave[0, :, part]) + dot(high, leave[1, :, part])
        conv_buf[:, c, :] = value + dot(low, leave[0, :, part])
    for b in range(blocks):
        k, j = divmod(b, per)
        value = (query_buf[b] * conv_buf[b]).astype(bf16)
        for h in range(2):
            out[place(BACK, k, h), :, j * LANES : (j + 1) * LANES] = value


def settle_body(gated, w1, w2, w3, out):
    count, owned, _ = gated.shape
    for h in range(2):
        rows = [gated[place(BACK, k, h)] for k in range(count // 2)]
        out[pl.ds(h * (count // 2) * owned, count // 2 * owned), :] = jnp.concatenate(rows, axis=0)


def merge_body(core, own, other, w0, w1, w2, w3, o0, o1, o2, o3, gathered):
    half = own.shape[0] // 2
    me = core[0]
    for h in range(2):
        at = pl.multiple_of((2 * h + me) * half, half)
        gathered[pl.ds(at, half), :] = own[h * half : (h + 1) * half, :]
        at = pl.multiple_of((2 * h + 1 - me) * half, half)
        gathered[pl.ds(at, half), :] = other[h * half : (h + 1) * half, :]
    for w, o in ((w2, o2), (w1, o1), (w3, o3), (w0, o0)):
        o[...] = dot(w[...], gathered[...]).astype(o.dtype)


def add_body(o0, o1, o2, o3, out):
    total = o0[...] + o1[...].astype(f32) + o2[...].astype(f32) + o3[...].astype(f32)
    out[...] = total.astype(out.dtype)


def local(features, short_taps, decay, residue, skip_bias, out_weight):
    _, channels, tokens = features.shape
    shards = lax.axis_size("x") * lax.axis_size("zl")
    owned, modes = decay.shape
    blocks = shards * tokens // LANES
    y, zh, core = (lax.axis_index(a) for a in CH)

    columns = short_taps.transpose(0, 2, 1)
    sent = pl.pallas_call(
        pack_body,
        out_shape=pltpu.VMEM((shards, owned, 2 * tokens + LANES), bf16),
        in_specs=[pl.BlockSpec(memory_space=pltpu.HBM)] * 2,
        out_specs=in_vmem,
        scratch_shapes=[
            pltpu.VMEM(features.shape, bf16),
            pltpu.VMEM(columns.shape, f32),
            pltpu.SemaphoreType.DMA((4,)),
        ],
        compiler_params=params(),
        name="pack",
    )(*(pltpu.with_memory_space_constraint(a, pltpu.HBM) for a in (features, columns)))
    held = lax.all_to_all(sent, GO, 0, 0, tiled=True)

    ys = lax.axis_size("y")
    cols = out_weight.shape[1] // ys
    weights = [lax.dynamic_slice_in_dim(out_weight, y * cols, cols, 1)]
    for d in range(1, ys):
        block = lax.dynamic_slice_in_dim(out_weight, (y + ys - d) % ys * cols, cols, 1)
        weights.append(shift(block, "y", -d))

    mats = pl.pallas_call(
        prep_body,
        out_shape=(
            pltpu.VMEM((2, owned, LANES, LANES), bf16),
            pltpu.VMEM((2, owned * LANES, LANES), bf16),
            pltpu.VMEM((2, LANES, owned * LANES), bf16),
            pltpu.VMEM((8, LANES), f32),
            pltpu.VMEM((3 * TAPS, owned, LANES), f32),
        ),
        in_specs=[in_vmem] * 4,
        out_specs=(in_vmem,) * 5,
        cost_estimate=pl.CostEstimate(flops=2000000, bytes_accessed=1600000, transcendentals=70000),
        compiler_params=params(),
        name="prep",
    )(decay, residue, skip_bias.reshape(1, -1), columns)
    toeplitz, enter, leave, powers, taps = mats
    gated = pl.pallas_call(
        conv_body,
        out_shape=pltpu.VMEM((2 * shards, owned, tokens), bf16),
        in_specs=[in_vmem] * 6 + [pl.BlockSpec(memory_space=pl.ANY)] * 3,
        out_specs=in_vmem,
        scratch_shapes=[pltpu.VMEM((blocks, owned, LANES), f32)] * 3,
        cost_estimate=pl.CostEstimate(flops=100000000, bytes_accessed=2500000, transcendentals=0),
        compiler_params=params(),
        name="conv",
    )(*map(near, (held, taps, toeplitz, enter, leave, powers)), *weights[1:])
    gated = lax.all_to_all(gated, BACK, 0, 0, tiled=True)
    gated = pl.pallas_call(
        settle_body,
        out_shape=pltpu.VMEM((2 * channels, tokens), bf16),
        in_specs=[in_vmem] + [pl.BlockSpec(memory_space=pl.ANY)] * 3,
        out_specs=in_vmem,
        compiler_params=params(),
        name="settle",
    )(near(gated), *weights[1:])
    other = shift(gated, "c", 1)
    rows = out_weight.shape[0]
    parts = pl.pallas_call(
        merge_body,
        out_shape=(pltpu.VMEM((rows, tokens), f32),) + (pltpu.VMEM((rows, tokens), bf16),) * 3,
        in_specs=[pl.BlockSpec(memory_space=pltpu.SMEM)] + [in_vmem] * 6,
        out_specs=(in_vmem,) * 4,
        scratch_shapes=[pltpu.VMEM((4 * channels, tokens), bf16)],
        cost_estimate=pl.CostEstimate(flops=300000000, bytes_accessed=2500000, transcendentals=0),
        compiler_params=params(),
        name="merge",
    )(core.reshape(1), near(gated), near(other), *map(near, weights))
    arrived = [parts[0]] + [shift(parts[d], "y", d) for d in (1, 2, 3)]
    return pl.pallas_call(
        add_body,
        out_shape=jax.ShapeDtypeStruct((rows, tokens), bf16),
        in_specs=[in_vmem] * 4,
        out_specs=in_vmem,
        compiler_params=params(),
        name="add",
    )(*map(near, arrived))


def solution(mesh):
    split = Mesh(mesh.devices.reshape(4, 4, 4, 2, 2), CTX + CH)
    in_specs = (
        P(None, CH, CTX),
        P(None, CH, None),
        P(CH + CTX, None),
        P(CH + CTX, None),
        P(CH),
        P(CH, None),
    )
    return jax.shard_map(local, mesh=split, in_specs=in_specs, out_specs=P(CH, CTX), check_vma=False)
```

time: 81.1 us -> 56.9 us (0.70)
  blocking collectives: 0 us -> 17.4 us
  waiting for transfers between devices: 26.4 us -> 11.8 us
  starting transfers between devices: 33.7 us -> 21.8 us
  local copies, waits for them, and re-layouts: 9.8 us -> 0.07 us
  Pallas kernels: 8.04 us -> 5.42 us
  other arithmetic: 2.42 us -> 0 us
    all_to_all x0 -> x1, blocking collectives: none -> 17.4 us  [local(): gated = lax.all_to_all(gated, BACK, 0, 0, tiled=True)]
    ppermute x8 -> x7, waiting for transfers between devices: 26.4 us -> 10.5 us  [shift(): lax.ppermute(value, axis, [(i, (i + steps) % count) for i in range(count)])]
    all_to_all x2 -> x1, starting transfers between devices: 17.3 us -> 9.03 us  [local(): held = lax.all_to_all(sent, GO, 0, 0, tiled=True)]
    ppermute x1 -> x0, starting transfers between devices: 3.26 us -> none  [local(): lax.ppermute(features[0, :, tokens - 2:], CTX, [(i, i + 1) for i in range...]
    unnamed x23 -> x10, local copies, waits for them, and re-layouts: 2.96 us -> 0.03 us
    pallas_call x3 -> x6, Pallas kernels: 8.04 us -> 5.42 us  [the longest x1 2.57 us: local(): pl.pallas_call(pack_body, out_shape=pltpu.VMEM((shards, owned, 2 * tokens...]
    convert_element_type x4 -> x0, other arithmetic: 2.13 us -> none  [the longest x1 1.67 us: local(): return total.astype(bf16)]
    squeeze x2 -> x0, local copies, waits for them, and re-layouts: 1.75 us -> none  [the longest x1 0.91 us: local(): longer = jnp.concatenate([rim, features[0]], axis=1).astype(f32)]
  transfers between devices with their start and end apart: 11 -> 8, of which waited for: 7 -> 7; matrix products, arithmetic and copies ran while one was open for 7% -> 0% of each run, Pallas kernels for 3% -> 1%
where the time goes in v1:
time: 56.9 us; the launch traced here: 56.7 us
  starting transfers between devices  21.8 us (38%)
  blocking collectives  17.4 us (31%)
  waiting for transfers between devices  11.8 us (21%)
  Pallas kernels  5.42 us (10%)
    all_to_all x1, blocking collectives, local(): gated = lax.all_to_all(gated, BACK, 0, 0, tiled=True)  17.4 us
    ppermute x7, starting transfers between devices, shift(): lax.ppermute(value, axis, [(i, (i + steps) % count) for i in range(count)])  12.8 us
    ppermute x7, waiting for transfers between devices, shift(): lax.ppermute(value, axis, [(i, (i + steps) % count) for i in range(count)])  10.5 us
    all_to_all x1, starting transfers between devices, local(): held = lax.all_to_all(sent, GO, 0, 0, tiled=True)  9.03 us
    pallas_call x1, Pallas kernels, local(): pl.pallas_call(pack_body, out_shape=pltpu.VMEM((shards, owned, 2 * tokens...  2.57 us
    all_to_all x1, waiting for transfers between devices, local(): held = lax.all_to_all(sent, GO, 0, 0, tiled=True)  1.25 us
  transfers between devices with their start and end apart: 8, of which 7 were waited for; matrix products, arithmetic and copies ran while one was open for 0% of the time, Pallas kernels for 1%

profile of v1, /device:TPU:1, one launch (start us, length us, event | category | flops | bytes accessed | tf_op | source)
XLA Modules:
  0.0 56.7 jit_solution(857414979593650871)
XLA Ops:
  0.0 0.0 copy-start.4
  0.0 2.6 %pack.1 = bf16[16,8,1152]{2,1,0:T(8,128)(2,1)} custom-call(bf16[3,128,512]{2,1,0:T(8,128)(2,1)} %features_hbm.1, f32[3,3,128]{2,1,0:T(4,128)} %bitcast.3), custom_call_target="tpu_custom_call" | custom-call | tf_op jit(solution)/shard_map/pack/pallas_call | solution.py:225
  2.6 9.0 %all-to-all-start = ((bf16[16,8,1152]{2,1,0:T(8,128)(2,1)}), bf16[16,8,1152]{2,1,0:T(8,128)(2,1)S(1)}, u32[]{:S(2)}, u32[]{:S(2)}) async-start(bf16[16,8,1152]{2,1,0:T(8,128)(2,1)} %pack.1), calls=%async_computation | async-start | bytes 589824 | tf_op jit(solution)/shard_map/all_to_all | solution.py:238
  11.7 0.0 copy-done.4
  11.7 0.0 copy-start.1
  11.7 0.0 copy-start.2
  11.8 0.0 copy-start
  11.8 3.0 %collective-permute-start.1 = (bf16[128,512]{1,0:T(8,128)(2,1)S(1)}, bf16[128,512]{1,0:T(8,128)(2,1)S(1)}, u32[]{:S(2)}, u32[]{:S(2)}) collective-permute-start(bf16[128,512]{1,0:T(8,128)(2,1)S(1)} %get-tuple-element.24), channel_id=1, source_target_pairs={{0,8},{4,12},{8,0},{12,4},{1,9},{5,13},{9,1},{13,5},{2,10},{6,14},... | collective-permute-start | bytes 393224 | tf_op jit(solution)/shard_map/ppermute | solution.py:22
  14.8 0.8 %collective-permute-start = (bf16[128,512]{1,0:T(8,128)(2,1)S(1)}, bf16[128,512]{1,0:T(8,128)(2,1)S(1)}, u32[]{:S(2)}, u32[]{:S(2)}) collective-permute-start(bf16[128,512]{1,0:T(8,128)(2,1)S(1)} %get-tuple-element.25), channel_id=1, source_target_pairs={{0,12},{4,0},{8,4},{12,8},{1,13},{5,1},{9,5},{13,9},{2,14},{6,2},{... | collective-permute-start | bytes 393224 | tf_op jit(solution)/shard_map/ppermute | solution.py:22
  15.5 0.0 copy-start.3
  15.5 0.7 %collective-permute-start.2 = (bf16[128,512]{1,0:T(8,128)(2,1)S(1)}, bf16[128,512]{1,0:T(8,128)(2,1)S(1)}, u32[]{:S(2)}, u32[]{:S(2)}) collective-permute-start(bf16[128,512]{1,0:T(8,128)(2,1)S(1)} %get-tuple-element.26), channel_id=1, source_target_pairs={{0,4},{4,8},{8,12},{12,0},{1,5},{5,9},{9,13},{13,1},{2,6},{6,10},{... | collective-permute-start | bytes 393224 | tf_op jit(solution)/shard_map/ppermute | solution.py:22
  16.2 0.0 copy-done.1
  16.2 0.0 copy-done.2
  16.2 0.0 copy-done
  16.2 0.0 copy-done.3
  16.2 0.5 prep.1
  16.8 0.4 collective-permute-done.1.w2
  17.2 3.4 %collective-permute-done.w1 = bf16[128,512]{1,0:T(8,128)(2,1)S(1)} collective-permute-done((bf16[128,512]{1,0:T(8,128)(2,1)S(1)}, bf16[128,512]{1,0:T(8,128)(2,1)S(1)}, u32[]{:S(2)}, u32[]{:S(2)}) %collective-permute-start) | collective-permute-done | bytes 131104 | tf_op jit(solution)/shard_map/ppermute | solution.py:22
  20.6 0.4 collective-permute-done.2.w3
  20.9 1.2 %all-to-all-done.held = bf16[16,8,1152]{2,1,0:T(8,128)(2,1)S(1)} async-done(((bf16[16,8,1152]{2,1,0:T(8,128)(2,1)}), bf16[16,8,1152]{2,1,0:T(8,128)(2,1)S(1)}, u32[]{:S(2)}, u32[]{:S(2)}) %all-to-all-start) | async-done | bytes 294944 | tf_op jit(solution)/shard_map/all_to_all | solution.py:238
  22.2 1.1 %conv.1 = bf16[32,8,512]{2,1,0:T(8,128)(2,1)S(1)} custom-call(bf16[16,8,1152]{2,1,0:T(8,128)(2,1)S(1)} %all-to-all-done.held, f32[9,8,128]{2,1,0:T(8,128)S(1)} %get-tuple-element.14.taps, bf16[2,8,128,128]{3,2,1,0:T(8,128)(2,1)S(1)} %get-tuple-element.15.toeplitz, bf16[2,1024,128]{2,1,0:T(8,128)(2,1)S(1)} %get-tuple-element.16.enter, ...), custom_call_target="tpu_custom_call" | custom-call | flops 100000000 | bytes 2500000 | tf_op jit(solution)/shard_map/conv/pallas_call | solution.py:263
  23.3 17.4 %all_to_all.10.gated = bf16[32,8,512]{2,1,0:T(8,128)(2,1)S(1)} all-to-all(bf16[32,8,512]{2,1,0:T(8,128)(2,1)S(1)} %conv.1), channel_id=1, replica_groups=mesh['x'=4,'zl'=4,'y'=4,'zh'=2,'c'=2] {'x','zl','zh'}, dimensions={0} | all-to-all | bytes 524288 | tf_op jit(solution)/shard_map/all_to_all | solution.py:273
  40.8 4.2 %collective-permute-start.3 = (bf16[256,512]{1,0:T(8,128)(2,1)S(1)}, bf16[256,512]{1,0:T(8,128)(2,1)S(1)}, u32[]{:S(2)}, u32[]{:S(2)}) collective-permute-start(bf16[256,512]{1,0:T(8,128)(2,1)S(1)} %settle.1.own), channel_id=1, source_target_pairs={{0,1},{1,0},{2,3},{3,2},{4,5},{5,4},{6,7},{7,6},{8,9},{9,8},{10,11... | collective-permute-start | bytes 786440 | tf_op jit(solution)/shard_map/ppermute | solution.py:22
  45.0 1.2 %collective-permute-done.3.other = bf16[256,512]{1,0:T(8,128)(2,1)S(1)} collective-permute-done((bf16[256,512]{1,0:T(8,128)(2,1)S(1)}, bf16[256,512]{1,0:T(8,128)(2,1)S(1)}, u32[]{:S(2)}, u32[]{:S(2)}) %collective-permute-start.3) | collective-permute-done | bytes 262176 | tf_op jit(solution)/shard_map/ppermute | solution.py:22
  46.2 0.5 merge.1
  46.7 0.6 %collective-permute-start.4 = (bf16[128,512]{1,0:T(8,128)(2,1)S(1)}, bf16[128,512]{1,0:T(8,128)(2,1)S(1)}, u32[]{:S(2)}, u32[]{:S(2)}) collective-permute-start(bf16[128,512]{1,0:T(8,128)(2,1)S(1)} %get-tuple-element.20), channel_id=1, source_target_pairs={{0,4},{4,8},{8,12},{12,0},{1,5},{5,9},{9,13},{13,1},{2,6},{6,10},{... | collective-permute-start | bytes 393224 | tf_op jit(solution)/shard_map/ppermute | solution.py:22
  47.3 2.6 %collective-permute-start.5 = (bf16[128,512]{1,0:T(8,128)(2,1)S(1)}, bf16[128,512]{1,0:T(8,128)(2,1)S(1)}, u32[]{:S(2)}, u32[]{:S(2)}) collective-permute-start(bf16[128,512]{1,0:T(8,128)(2,1)S(1)} %get-tuple-element.21), channel_id=1, source_target_pairs={{0,8},{4,12},{8,0},{12,4},{1,9},{5,13},{9,1},{13,5},{2,10},{6,14},... | collective-permute-start | bytes 393224 | tf_op jit(solution)/shard_map/ppermute | solution.py:22
  49.9 0.9 %collective-permute-start.6 = (bf16[128,512]{1,0:T(8,128)(2,1)S(1)}, bf16[128,512]{1,0:T(8,128)(2,1)S(1)}, u32[]{:S(2)}, u32[]{:S(2)}) collective-permute-start(bf16[128,512]{1,0:T(8,128)(2,1)S(1)} %get-tuple-element.22), channel_id=1, source_target_pairs={{0,12},{4,0},{8,4},{12,8},{1,13},{5,1},{9,5},{13,9},{2,14},{6,2},{... | collective-permute-start | bytes 393224 | tf_op jit(solution)/shard_map/ppermute | solution.py:22
  50.8 1.9 %collective-permute-done.4.o1 = bf16[128,512]{1,0:T(8,128)(2,1)S(1)} collective-permute-done((bf16[128,512]{1,0:T(8,128)(2,1)S(1)}, bf16[128,512]{1,0:T(8,128)(2,1)S(1)}, u32[]{:S(2)}, u32[]{:S(2)}) %collective-permute-start.4) | collective-permute-done | bytes 131104 | tf_op jit(solution)/shard_map/ppermute | solution.py:22
  52.6 3.3 %collective-permute-done.5.o2 = bf16[128,512]{1,0:T(8,128)(2,1)S(1)} collective-permute-done((bf16[128,512]{1,0:T(8,128)(2,1)S(1)}, bf16[128,512]{1,0:T(8,128)(2,1)S(1)}, u32[]{:S(2)}, u32[]{:S(2)}) %collective-permute-start.5) | collective-permute-done | bytes 131104 | tf_op jit(solution)/shard_map/ppermute | solution.py:22
  56.0 0.0 collective-permute-done.6.o3
  56.0 0.7 %add.42 = bf16[128,512]{1,0:T(8,128)(2,1)} custom-call(f32[128,512]{1,0:T(8,128)S(1)} %get-tuple-element.19.o0, bf16[128,512]{1,0:T(8,128)(2,1)S(1)} %collective-permute-done.4.o1, bf16[128,512]{1,0:T(8,128)(2,1)S(1)} %collective-permute-done.5.o2, bf16[128,512]{1,0:T(8,128)(2,1)S(1)} %collective-permute-done.6.o3), custom_call_target="tpu_custom_call" | custom-call | tf_op jit(solution)/shard_map/add/pallas_call | solution.py:295
  (2 shorter events, 0.1 us)
Async XLA Ops:
  0.0 11.7 %copy-start.4 = (bf16[128,2048]{1,0:T(8,128)(2,1)S(1)}, bf16[128,2048]{1,0:T(8,128)(2,1)}, u32[]{:S(2)}) copy-start(bf16[128,2048]{1,0:T(8,128)(2,1)} %param.11) | copy-start | bytes 1572868
  2.6 19.6 %all-to-all-start = ((bf16[16,8,1152]{2,1,0:T(8,128)(2,1)}), bf16[16,8,1152]{2,1,0:T(8,128)(2,1)S(1)}, u32[]{:S(2)}, u32[]{:S(2)}) async-start(bf16[16,8,1152]{2,1,0:T(8,128)(2,1)} %pack.1), calls=%async_computation | async-start | bytes 589824 | tf_op jit(solution)/shard_map/all_to_all | solution.py:238
  11.7 4.6 %copy-start.1 = (f32[8,16]{1,0:T(8,128)S(1)}, f32[8,16]{1,0:T(8,128)}, u32[]{:S(2)}) copy-start(f32[8,16]{1,0:T(8,128)} %decay.1) | copy-start | bytes 1540
  11.7 4.6 %copy-start.2 = (f32[8,16]{1,0:T(8,128)S(1)}, f32[8,16]{1,0:T(8,128)}, u32[]{:S(2)}) copy-start(f32[8,16]{1,0:T(8,128)} %residue.1) | copy-start | bytes 1540
  11.8 4.5 %copy-start = (f32[3,128,3]{1,2,0:T(4,128)S(1)}, f32[3,128,3]{1,2,0:T(4,128)}, u32[]{:S(2)}) copy-start(f32[3,128,3]{1,2,0:T(4,128)} %param.7) | copy-start | bytes 13828
  11.8 5.4 %collective-permute-start.1 = (bf16[128,512]{1,0:T(8,128)(2,1)S(1)}, bf16[128,512]{1,0:T(8,128)(2,1)S(1)}, u32[]{:S(2)}, u32[]{:S(2)}) collective-permute-start(bf16[128,512]{1,0:T(8,128)(2,1)S(1)} %get-tuple-element.24), channel_id=1, source_target_pairs={{0,8},{4,12},{8,0},{12,4},{1,9},{5,13},{9,1},{13,5},{2,10},{6,14},... | collective-permute-start | bytes 393224 | tf_op jit(solution)/shard_map/ppermute | solution.py:22
  14.8 5.8 %collective-permute-start = (bf16[128,512]{1,0:T(8,128)(2,1)S(1)}, bf16[128,512]{1,0:T(8,128)(2,1)S(1)}, u32[]{:S(2)}, u32[]{:S(2)}) collective-permute-start(bf16[128,512]{1,0:T(8,128)(2,1)S(1)} %get-tuple-element.25), channel_id=1, source_target_pairs={{0,12},{4,0},{8,4},{12,8},{1,13},{5,1},{9,5},{13,9},{2,14},{6,2},{... | collective-permute-start | bytes 393224 | tf_op jit(solution)/shard_map/ppermute | solution.py:22
  15.5 0.7 %copy-start.3 = (f32[128]{0:T(128)S(1)}, f32[128]{0:T(128)}, u32[]{:S(2)}) copy-start(f32[128]{0:T(128)} %param.10) | copy-start | bytes 1540
  15.5 5.4 %collective-permute-start.2 = (bf16[128,512]{1,0:T(8,128)(2,1)S(1)}, bf16[128,512]{1,0:T(8,128)(2,1)S(1)}, u32[]{:S(2)}, u32[]{:S(2)}) collective-permute-start(bf16[128,512]{1,0:T(8,128)(2,1)S(1)} %get-tuple-element.26), channel_id=1, source_target_pairs={{0,4},{4,8},{8,12},{12,0},{1,5},{5,9},{9,13},{13,1},{2,6},{6,10},{... | collective-permute-start | bytes 393224 | tf_op jit(solution)/shard_map/ppermute | solution.py:22
  40.8 5.4 %collective-permute-start.3 = (bf16[256,512]{1,0:T(8,128)(2,1)S(1)}, bf16[256,512]{1,0:T(8,128)(2,1)S(1)}, u32[]{:S(2)}, u32[]{:S(2)}) collective-permute-start(bf16[256,512]{1,0:T(8,128)(2,1)S(1)} %settle.1.own), channel_id=1, source_target_pairs={{0,1},{1,0},{2,3},{3,2},{4,5},{5,4},{6,7},{7,6},{8,9},{9,8},{10,11... | collective-permute-start | bytes 786440 | tf_op jit(solution)/shard_map/ppermute | solution.py:22
  46.7 6.0 %collective-permute-start.4 = (bf16[128,512]{1,0:T(8,128)(2,1)S(1)}, bf16[128,512]{1,0:T(8,128)(2,1)S(1)}, u32[]{:S(2)}, u32[]{:S(2)}) collective-permute-start(bf16[128,512]{1,0:T(8,128)(2,1)S(1)} %get-tuple-element.20), channel_id=1, source_target_pairs={{0,4},{4,8},{8,12},{12,0},{1,5},{5,9},{9,13},{13,1},{2,6},{6,10},{... | collective-permute-start | bytes 393224 | tf_op jit(solution)/shard_map/ppermute | solution.py:22
  47.3 8.7 %collective-permute-start.5 = (bf16[128,512]{1,0:T(8,128)(2,1)S(1)}, bf16[128,512]{1,0:T(8,128)(2,1)S(1)}, u32[]{:S(2)}, u32[]{:S(2)}) collective-permute-start(bf16[128,512]{1,0:T(8,128)(2,1)S(1)} %get-tuple-element.21), channel_id=1, source_target_pairs={{0,8},{4,12},{8,0},{12,4},{1,9},{5,13},{9,1},{13,5},{2,10},{6,14},... | collective-permute-start | bytes 393224 | tf_op jit(solution)/shard_map/ppermute | solution.py:22
  49.9 6.1 %collective-permute-start.6 = (bf16[128,512]{1,0:T(8,128)(2,1)S(1)}, bf16[128,512]{1,0:T(8,128)(2,1)S(1)}, u32[]{:S(2)}, u32[]{:S(2)}) collective-permute-start(bf16[128,512]{1,0:T(8,128)(2,1)S(1)} %get-tuple-element.22), channel_id=1, source_target_pairs={{0,12},{4,0},{8,4},{12,8},{1,13},{5,1},{9,5},{13,9},{2,14},{6,2},{... | collective-permute-start | bytes 393224 | tf_op jit(solution)/shard_map/ppermute | solution.py:22

commit v2 on v1

--- a/solution.py
+++ b/solution.py
@@ -8,10 +8,12 @@
 
 CTX = ("x", "zl")
 CH = ("y", "zh", "c")
-GO = ("x", "zl")
-BACK = ("x", "zl", "zh")
+GO = ("zl", "x")
+BACK = ("zh", "zl", "x")
 LANES = 128
 TAPS = 3
+ORDER = (2, 1, 3)
+WAIT = 20_000_000_000
 f32 = jnp.float32
 bf16 = jnp.bfloat16
 in_vmem = pl.BlockSpec(memory_space=pltpu.VMEM)
@@ -25,10 +27,16 @@
 def place(order, k, h=0):
     at = {"x": k // 4, "zl": k % 4, "zh": h}
     size = {"x": 4, "zl": 4, "zh": 2}
-    index = 0
+    index, count = 0, 1
     for axis in order:
         index = index * size[axis] + at[axis]
-    return index
+        count *= size[axis]
+    return count - 1 - index
+
+
+def exchange(value, order):
+    backwards = [list(reversed(range(value.shape[0])))]
+    return lax.all_to_all(value, order, 0, 0, axis_index_groups=backwards, tiled=True)
 
 
 def near(value):
@@ -140,7 +148,7 @@
     return jnp.dot(a, b, preferred_element_type=f32)
 
 
-def conv_body(held, taps, toeplitz, enter, leave, powers, w1, w2, w3, out, mixed_buf, query_buf, conv_buf):
+def conv_body(held, taps, toeplitz, enter, leave, powers, out, mixed_buf, query_buf, conv_buf):
     shards, owned, _ = held.shape
     tokens = out.shape[-1]
     per = tokens // LANES
@@ -190,23 +198,32 @@
             out[place(BACK, k, h), :, j * LANES : (j + 1) * LANES] = value
 
 
-def settle_body(gated, w1, w2, w3, out):
+def hold_body(gated, w1, w2, w3, out):
+    out[...] = gated[...]
+
+
+def settle_body(gated, out):
     count, owned, _ = gated.shape
     for h in range(2):
         rows = [gated[place(BACK, k, h)] for k in range(count // 2)]
         out[pl.ds(h * (count // 2) * owned, count // 2 * owned), :] = jnp.concatenate(rows, axis=0)
 
 
-def merge_body(core, own, other, w0, w1, w2, w3, o0, o1, o2, o3, gathered):
+def columns_of(w, core, half):
+    return [w[:, pl.ds(pl.multiple_of((2 * h + core) * half, half), half)] for h in range(2)]
+
+
+def own_body(core, own, w0, w1, w2, w3, o0, o1, o2, o3):
     half = own.shape[0] // 2
-    me = core[0]
-    for h in range(2):
-        at = pl.multiple_of((2 * h + me) * half, half)
-        gathered[pl.ds(at, half), :] = own[h * half : (h + 1) * half, :]
-        at = pl.multiple_of((2 * h + 1 - me) * half, half)
-        gathered[pl.ds(at, half), :] = other[h * half : (h + 1) * half, :]
-    for w, o in ((w2, o2), (w1, o1), (w3, o3), (w0, o0)):
-        o[...] = dot(w[...], gathered[...]).astype(o.dtype)
+    for w, o in ((w0, o0), (w1, o1), (w2, o2), (w3, o3)):
+        o[...] = dot(jnp.concatenate(columns_of(w, core[0], half), axis=1), own[...])
+
+
+def other_body(core, other, w0, w1, w2, w3, a0, a1, a2, a3, o0, o1, o2, o3):
+    half = other.shape[0] // 2
+    for w, a, o in ((w2, a2, o2), (w1, a1, o1), (w3, a3, o3), (w0, a0, o0)):
+        term = dot(jnp.concatenate(columns_of(w, 1 - core[0], half), axis=1), other[...])
+        o[...] = (a[...] + term).astype(o.dtype)
 
 
 def add_body(o0, o1, o2, o3, out):
@@ -235,14 +252,15 @@
         compiler_params=params(),
         name="pack",
     )(*(pltpu.with_memory_space_constraint(a, pltpu.HBM) for a in (features, columns)))
-    held = lax.all_to_all(sent, GO, 0, 0, tiled=True)
+    held = exchange(sent, GO)
 
     ys = lax.axis_size("y")
     cols = out_weight.shape[1] // ys
-    weights = [lax.dynamic_slice_in_dim(out_weight, y * cols, cols, 1)]
-    for d in range(1, ys):
+    weights = {0: lax.dynamic_slice_in_dim(out_weight, y * cols, cols, 1)}
+    for d in ORDER:
         block = lax.dynamic_slice_in_dim(out_weight, (y + ys - d) % ys * cols, cols, 1)
-        weights.append(shift(block, "y", -d))
+        weights[d] = shift(block, "y", -d)
+    weights = [weights[d] for d in range(ys)]
 
     mats = pl.pallas_call(
         prep_body,
@@ -263,34 +281,52 @@
     gated = pl.pallas_call(
         conv_body,
         out_shape=pltpu.VMEM((2 * shards, owned, tokens), bf16),
-        in_specs=[in_vmem] * 6 + [pl.BlockSpec(memory_space=pl.ANY)] * 3,
+        in_specs=[in_vmem] * 6,
         out_specs=in_vmem,
         scratch_shapes=[pltpu.VMEM((blocks, owned, LANES), f32)] * 3,
-        cost_estimate=pl.CostEstimate(flops=100000000, bytes_accessed=2500000, transcendentals=0),
+        cost_estimate=pl.CostEstimate(flops=WAIT, bytes_accessed=2500000, transcendentals=0),
         compiler_params=params(),
         name="conv",
-    )(*map(near, (held, taps, toeplitz, enter, leave, powers)), *weights[1:])
-    gated = lax.all_to_all(gated, BACK, 0, 0, tiled=True)
+    )(*map(near, (held, taps, toeplitz, enter, leave, powers)))
+    gated = pl.pallas_call(
+        hold_body,
+        out_shape=pltpu.VMEM((2 * shards, owned, tokens), bf16),
+        in_specs=[in_vmem] + [pl.BlockSpec(memory_space=pl.ANY)] * 3,
+        out_specs=in_vmem,
+        compiler_params=params(),
+        name="hold",
+    )(near(gated), *(weights[d] for d in ORDER))
+    gated = exchange(gated, BACK)
     gated = pl.pallas_call(
         settle_body,
         out_shape=pltpu.VMEM((2 * channels, tokens), bf16),
-        in_specs=[in_vmem] + [pl.BlockSpec(memory_space=pl.ANY)] * 3,
+        in_specs=[in_vmem],
         out_specs=in_vmem,
         compiler_params=params(),
         name="settle",
-    )(near(gated), *weights[1:])
+    )(near(gated))
     other = shift(gated, "c", 1)
     rows = out_weight.shape[0]
+    one = core.reshape(1)
+    close = [near(w) for w in weights]
+    sums = pl.pallas_call(
+        own_body,
+        out_shape=(pltpu.VMEM((rows, tokens), f32),) * 4,
+        in_specs=[pl.BlockSpec(memory_space=pltpu.SMEM)] + [in_vmem] * 5,
+        out_specs=(in_vmem,) * 4,
+        cost_estimate=pl.CostEstimate(flops=150000000, bytes_accessed=1500000, transcendentals=0),
+        compiler_params=params(),
+        name="own",
+    )(one, near(gated), *close)
     parts = pl.pallas_call(
-        merge_body,
+        other_body,
         out_shape=(pltpu.VMEM((rows, tokens), f32),) + (pltpu.VMEM((rows, tokens), bf16),) * 3,
-        in_specs=[pl.BlockSpec(memory_space=pltpu.SMEM)] + [in_vmem] * 6,
+        in_specs=[pl.BlockSpec(memory_space=pltpu.SMEM)] + [in_vmem] * 9,
         out_specs=(in_vmem,) * 4,
-        scratch_shapes=[pltpu.VMEM((4 * channels, tokens), bf16)],
-        cost_estimate=pl.CostEstimate(flops=300000000, bytes_accessed=2500000, transcendentals=0),
-        compiler_params=params(),
-        name="merge",
-    )(core.reshape(1), near(gated), near(other), *map(near, weights))
+        cost_estimate=pl.CostEstimate(flops=150000000, bytes_accessed=1500000, transcendentals=0),
+        compiler_params=params(),
+        name="other",
+    )(one, near(other), *close, *map(near, sums))
     arrived = [parts[0]] + [shift(parts[d], "y", d) for d in (1, 2, 3)]
     return pl.pallas_call(
         add_body,

time: 56.9 us -> 53.8 us (0.946)
  waiting for transfers between devices: 11.8 us -> 8.71 us
  blocking collectives: 17.4 us -> 15.3 us
  starting transfers between devices: 21.8 us -> 23.7 us
    ppermute x7, waiting for transfers between devices: 10.5 us -> 6.26 us  [shift(): lax.ppermute(value, axis, [(i, (i + steps) % count) for i in range(count)])]
    all_to_all x1, blocking collectives: 17.4 us -> 15.3 us  [exchange(): lax.all_to_all(value, order, 0, 0, axis_index_groups=backwards, tiled=True)]
    all_to_all x1, starting transfers between devices: 9.03 us -> 10.8 us  [exchange(): lax.all_to_all(value, order, 0, 0, axis_index_groups=backwards, tiled=True)]
    all_to_all x1, waiting for transfers between devices: 1.25 us -> 2.45 us  [exchange(): lax.all_to_all(value, order, 0, 0, axis_index_groups=backwards, tiled=True)]
  transfers between devices with their start and end apart: 8 -> 8, of which waited for: 7 -> 6; matrix products, arithmetic and copies ran while one was open for 0% -> 0% of each run, Pallas kernels for 1% -> 4%
where the time goes in v2:
time: 53.8 us; the launch traced here: 53.4 us
  starting transfers between devices  23.7 us (44%)
  blocking collectives  15.3 us (28%)
  waiting for transfers between devices  8.71 us (16%)
  Pallas kernels  5.57 us (10%)
    all_to_all x1, blocking collectives, exchange(): lax.all_to_all(value, order, 0, 0, axis_index_groups=backwards, tiled=True)  15.3 us
    ppermute x7, starting transfers between devices, shift(): lax.ppermute(value, axis, [(i, (i + steps) % count) for i in range(count)])  12.9 us
    all_to_all x1, starting transfers between devices, exchange(): lax.all_to_all(value, order, 0, 0, axis_index_groups=backwards, tiled=True)  10.8 us
    ppermute x7, waiting for transfers between devices, shift(): lax.ppermute(value, axis, [(i, (i + steps) % count) for i in range(count)])  6.26 us
    pallas_call x1, Pallas kernels, local(): pl.pallas_call(pack_body, out_shape=pltpu.VMEM((shards, owned, 2 * tokens...  2.57 us
    all_to_all x1, waiting for transfers between devices, exchange(): lax.all_to_all(value, order, 0, 0, axis_index_groups=backwards, tiled=True)  2.45 us
    pallas_call x1, Pallas kernels, local(): pl.pallas_call(conv_body, out_shape=pltpu.VMEM((2 * shards, owned, tokens...  1.11 us
  transfers between devices with their start and end apart: 8, of which 6 were waited for; matrix products, arithmetic and copies ran while one was open for 0% of the time, Pallas kernels for 4%

profile of v2, /device:TPU:1, one launch (start us, length us, event | category | flops | bytes accessed | tf_op | source)
XLA Modules:
  0.0 53.4 jit_solution(15947682566765812188)
XLA Ops:
  0.0 0.0 copy-start.4
  0.0 2.6 %pack.1 = bf16[16,8,1152]{2,1,0:T(8,128)(2,1)} custom-call(bf16[3,128,512]{2,1,0:T(8,128)(2,1)} %features_hbm.1, f32[3,3,128]{2,1,0:T(4,128)} %bitcast.3), custom_call_target="tpu_custom_call" | custom-call | tf_op jit(solution)/shard_map/pack/pallas_call | solution.py:242
  2.6 10.8 %all-to-all-start = ((bf16[16,8,1152]{2,1,0:T(8,128)(2,1)}), bf16[16,8,1152]{2,1,0:T(8,128)(2,1)S(1)}, u32[]{:S(2)}, u32[]{:S(2)}) async-start(bf16[16,8,1152]{2,1,0:T(8,128)(2,1)} %pack.1), calls=%async_computation | async-start | bytes 589824 | tf_op jit(solution)/shard_map/all_to_all | solution.py:39
  13.4 0.0 copy-done.4
  13.4 0.0 copy-start.1
  13.4 0.0 copy-start.2
  13.5 0.0 copy-start
  13.5 3.0 %collective-permute-start = (bf16[128,512]{1,0:T(8,128)(2,1)S(1)}, bf16[128,512]{1,0:T(8,128)(2,1)S(1)}, u32[]{:S(2)}, u32[]{:S(2)}) collective-permute-start(bf16[128,512]{1,0:T(8,128)(2,1)S(1)} %get-tuple-element.33), channel_id=1, source_target_pairs={{0,8},{4,12},{8,0},{12,4},{1,9},{5,13},{9,1},{13,5},{2,10},{6,14},... | collective-permute-start | bytes 393224 | tf_op jit(solution)/shard_map/ppermute | solution.py:24
  16.5 0.8 %collective-permute-start.1 = (bf16[128,512]{1,0:T(8,128)(2,1)S(1)}, bf16[128,512]{1,0:T(8,128)(2,1)S(1)}, u32[]{:S(2)}, u32[]{:S(2)}) collective-permute-start(bf16[128,512]{1,0:T(8,128)(2,1)S(1)} %get-tuple-element.32), channel_id=1, source_target_pairs={{0,12},{4,0},{8,4},{12,8},{1,13},{5,1},{9,5},{13,9},{2,14},{6,2},{... | collective-permute-start | bytes 393224 | tf_op jit(solution)/shard_map/ppermute | solution.py:24
  17.3 0.0 copy-start.3
  17.3 0.7 %collective-permute-start.2 = (bf16[128,512]{1,0:T(8,128)(2,1)S(1)}, bf16[128,512]{1,0:T(8,128)(2,1)S(1)}, u32[]{:S(2)}, u32[]{:S(2)}) collective-permute-start(bf16[128,512]{1,0:T(8,128)(2,1)S(1)} %get-tuple-element.34), channel_id=1, source_target_pairs={{0,4},{4,8},{8,12},{12,0},{1,5},{5,9},{9,13},{13,1},{2,6},{6,10},{... | collective-permute-start | bytes 393224 | tf_op jit(solution)/shard_map/ppermute | solution.py:24
  17.9 0.0 copy-done.1
  17.9 0.0 copy-done.2
  17.9 0.0 copy-done
  18.0 0.0 copy-done.3
  18.0 0.5 prep.1
  18.5 2.4 %all-to-all-done.held = bf16[16,8,1152]{2,1,0:T(8,128)(2,1)S(1)} async-done(((bf16[16,8,1152]{2,1,0:T(8,128)(2,1)}), bf16[16,8,1152]{2,1,0:T(8,128)(2,1)S(1)}, u32[]{:S(2)}, u32[]{:S(2)}) %all-to-all-start) | async-done | bytes 294944 | tf_op jit(solution)/shard_map/all_to_all | solution.py:39
  20.9 1.1 %conv.1.gated = bf16[32,8,512]{2,1,0:T(8,128)(2,1)S(1)} custom-call(bf16[16,8,1152]{2,1,0:T(8,128)(2,1)S(1)} %all-to-all-done.held, f32[9,8,128]{2,1,0:T(8,128)S(1)} %get-tuple-element.18.taps, bf16[2,8,128,128]{3,2,1,0:T(8,128)(2,1)S(1)} %get-tuple-element.19.toeplitz, bf16[2,1024,128]{2,1,0:T(8,128)(2,1)S(1)} %get-tuple-element.20.enter, ...), custom_call_target="tpu_custom_call" | custom-call | flops 20000000000 | bytes 2500000 | tf_op jit(solution)/shard_map/conv/pallas_call | solution.py:281
  22.0 0.0 collective-permute-done.w1.w2
  22.0 0.0 collective-permute-done.1.w2.w1
  22.1 0.3 collective-permute-done.2.w3
  22.4 15.3 %all_to_all.10.gated = bf16[32,8,512]{2,1,0:T(8,128)(2,1)S(1)} all-to-all(bf16[32,8,512]{2,1,0:T(8,128)(2,1)S(1)} %hold.1), channel_id=1, replica_groups={{242,178,114,50,226,162,98,34,210,146,82,18,194,130,66,2,240,176,112,48..., dimensions={0} | all-to-all | bytes 524288 | tf_op jit(solution)/shard_map/all_to_all | solution.py:39
  37.7 4.4 %collective-permute-start.3 = (bf16[256,512]{1,0:T(8,128)(2,1)S(1)}, bf16[256,512]{1,0:T(8,128)(2,1)S(1)}, u32[]{:S(2)}, u32[]{:S(2)}) collective-permute-start(bf16[256,512]{1,0:T(8,128)(2,1)S(1)} %settle.1.own), channel_id=1, source_target_pairs={{0,1},{1,0},{2,3},{3,2},{4,5},{5,4},{6,7},{7,6},{8,9},{9,8},{10,11... | collective-permute-start | bytes 786440 | tf_op jit(solution)/shard_map/ppermute | solution.py:24
  42.2 0.3 own.1
  42.5 0.9 %collective-permute-done.3.other = bf16[256,512]{1,0:T(8,128)(2,1)S(1)} collective-permute-done((bf16[256,512]{1,0:T(8,128)(2,1)S(1)}, bf16[256,512]{1,0:T(8,128)(2,1)S(1)}, u32[]{:S(2)}, u32[]{:S(2)}) %collective-permute-start.3) | collective-permute-done | bytes 262176 | tf_op jit(solution)/shard_map/ppermute | solution.py:24
  43.3 0.3 other.1
  43.6 0.4 collective-permute-start.4
  44.1 2.4 %collective-permute-start.5 = (bf16[128,512]{1,0:T(8,128)(2,1)S(1)}, bf16[128,512]{1,0:T(8,128)(2,1)S(1)}, u32[]{:S(2)}, u32[]{:S(2)}) collective-permute-start(bf16[128,512]{1,0:T(8,128)(2,1)S(1)} %get-tuple-element.29), channel_id=1, source_target_pairs={{0,8},{4,12},{8,0},{12,4},{1,9},{5,13},{9,1},{13,5},{2,10},{6,14},... | collective-permute-start | bytes 393224 | tf_op jit(solution)/shard_map/ppermute | solution.py:24
  46.5 1.2 %collective-permute-start.6 = (bf16[128,512]{1,0:T(8,128)(2,1)S(1)}, bf16[128,512]{1,0:T(8,128)(2,1)S(1)}, u32[]{:S(2)}, u32[]{:S(2)}) collective-permute-start(bf16[128,512]{1,0:T(8,128)(2,1)S(1)} %get-tuple-element.30), channel_id=1, source_target_pairs={{0,12},{4,0},{8,4},{12,8},{1,13},{5,1},{9,5},{13,9},{2,14},{6,2},{... | collective-permute-start | bytes 393224 | tf_op jit(solution)/shard_map/ppermute | solution.py:24
  47.6 2.0 %collective-permute-done.4.o1 = bf16[128,512]{1,0:T(8,128)(2,1)S(1)} collective-permute-done((bf16[128,512]{1,0:T(8,128)(2,1)S(1)}, bf16[128,512]{1,0:T(8,128)(2,1)S(1)}, u32[]{:S(2)}, u32[]{:S(2)}) %collective-permute-start.4) | collective-permute-done | bytes 131104 | tf_op jit(solution)/shard_map/ppermute | solution.py:24
  49.6 2.9 %collective-permute-done.5.o2 = bf16[128,512]{1,0:T(8,128)(2,1)S(1)} collective-permute-done((bf16[128,512]{1,0:T(8,128)(2,1)S(1)}, bf16[128,512]{1,0:T(8,128)(2,1)S(1)}, u32[]{:S(2)}, u32[]{:S(2)}) %collective-permute-start.5) | collective-permute-done | bytes 131104 | tf_op jit(solution)/shard_map/ppermute | solution.py:24
  52.5 0.2 collective-permute-done.6.o3
  52.7 0.7 %add.42 = bf16[128,512]{1,0:T(8,128)(2,1)} custom-call(f32[128,512]{1,0:T(8,128)S(1)} %get-tuple-element.27.o0, bf16[128,512]{1,0:T(8,128)(2,1)S(1)} %collective-permute-done.4.o1, bf16[128,512]{1,0:T(8,128)(2,1)S(1)} %collective-permute-done.5.o2, bf16[128,512]{1,0:T(8,128)(2,1)S(1)} %collective-permute-done.6.o3), custom_call_target="tpu_custom_call" | custom-call | tf_op jit(solution)/shard_map/add/pallas_call | solution.py:331
  (3 shorter events, 0.1 us)
Async XLA Ops:
  0.0 13.4 %copy-start.4 = (bf16[128,2048]{1,0:T(8,128)(2,1)S(1)}, bf16[128,2048]{1,0:T(8,128)(2,1)}, u32[]{:S(2)}) copy-start(bf16[128,2048]{1,0:T(8,128)(2,1)} %param.11) | copy-start | bytes 1572868
  2.6 18.3 %all-to-all-start = ((bf16[16,8,1152]{2,1,0:T(8,128)(2,1)}), bf16[16,8,1152]{2,1,0:T(8,128)(2,1)S(1)}, u32[]{:S(2)}, u32[]{:S(2)}) async-start(bf16[16,8,1152]{2,1,0:T(8,128)(2,1)} %pack.1), calls=%async_computation | async-start | bytes 589824 | tf_op jit(solution)/shard_map/all_to_all | solution.py:39
  13.4 4.6 %copy-start.1 = (f32[8,16]{1,0:T(8,128)S(1)}, f32[8,16]{1,0:T(8,128)}, u32[]{:S(2)}) copy-start(f32[8,16]{1,0:T(8,128)} %decay.1) | copy-start | bytes 1540
  13.4 4.6 %copy-start.2 = (f32[8,16]{1,0:T(8,128)S(1)}, f32[8,16]{1,0:T(8,128)}, u32[]{:S(2)}) copy-start(f32[8,16]{1,0:T(8,128)} %residue.1) | copy-start | bytes 1540
  13.5 4.5 %copy-start = (f32[3,128,3]{1,2,0:T(4,128)S(1)}, f32[3,128,3]{1,2,0:T(4,128)}, u32[]{:S(2)}) copy-start(f32[3,128,3]{1,2,0:T(4,128)} %param.7) | copy-start | bytes 13828
  13.5 8.6 %collective-permute-start = (bf16[128,512]{1,0:T(8,128)(2,1)S(1)}, bf16[128,512]{1,0:T(8,128)(2,1)S(1)}, u32[]{:S(2)}, u32[]{:S(2)}) collective-permute-start(bf16[128,512]{1,0:T(8,128)(2,1)S(1)} %get-tuple-element.33), channel_id=1, source_target_pairs={{0,8},{4,12},{8,0},{12,4},{1,9},{5,13},{9,1},{13,5},{2,10},{6,14},... | collective-permute-start | bytes 393224 | tf_op jit(solution)/shard_map/ppermute | solution.py:24
  16.5 5.6 %collective-permute-start.1 = (bf16[128,512]{1,0:T(8,128)(2,1)S(1)}, bf16[128,512]{1,0:T(8,128)(2,1)S(1)}, u32[]{:S(2)}, u32[]{:S(2)}) collective-permute-start(bf16[128,512]{1,0:T(8,128)(2,1)S(1)} %get-tuple-element.32), channel_id=1, source_target_pairs={{0,12},{4,0},{8,4},{12,8},{1,13},{5,1},{9,5},{13,9},{2,14},{6,2},{... | collective-permute-start | bytes 393224 | tf_op jit(solution)/shard_map/ppermute | solution.py:24
  17.3 0.7 %copy-start.3 = (f32[128]{0:T(128)S(1)}, f32[128]{0:T(128)}, u32[]{:S(2)}) copy-start(f32[128]{0:T(128)} %param.10) | copy-start | bytes 1540
  17.3 5.1 %collective-permute-start.2 = (bf16[128,512]{1,0:T(8,128)(2,1)S(1)}, bf16[128,512]{1,0:T(8,128)(2,1)S(1)}, u32[]{:S(2)}, u32[]{:S(2)}) collective-permute-start(bf16[128,512]{1,0:T(8,128)(2,1)S(1)} %get-tuple-element.34), channel_id=1, source_target_pairs={{0,4},{4,8},{8,12},{12,0},{1,5},{5,9},{9,13},{13,1},{2,6},{6,10},{... | collective-permute-start | bytes 393224 | tf_op jit(solution)/shard_map/ppermute | solution.py:24
  37.7 5.6 %collective-permute-start.3 = (bf16[256,512]{1,0:T(8,128)(2,1)S(1)}, bf16[256,512]{1,0:T(8,128)(2,1)S(1)}, u32[]{:S(2)}, u32[]{:S(2)}) collective-permute-start(bf16[256,512]{1,0:T(8,128)(2,1)S(1)} %settle.1.own), channel_id=1, source_target_pairs={{0,1},{1,0},{2,3},{3,2},{4,5},{5,4},{6,7},{7,6},{8,9},{9,8},{10,11... | collective-permute-start | bytes 786440 | tf_op jit(solution)/shard_map/ppermute | solution.py:24
  43.6 6.0 %collective-permute-start.4 = (bf16[128,512]{1,0:T(8,128)(2,1)S(1)}, bf16[128,512]{1,0:T(8,128)(2,1)S(1)}, u32[]{:S(2)}, u32[]{:S(2)}) collective-permute-start(bf16[128,512]{1,0:T(8,128)(2,1)S(1)} %get-tuple-element.28), channel_id=1, source_target_pairs={{0,4},{4,8},{8,12},{12,0},{1,5},{5,9},{9,13},{13,1},{2,6},{6,10},{... | collective-permute-start | bytes 393224 | tf_op jit(solution)/shard_map/ppermute | solution.py:24
  44.1 8.4 %collective-permute-start.5 = (bf16[128,512]{1,0:T(8,128)(2,1)S(1)}, bf16[128,512]{1,0:T(8,128)(2,1)S(1)}, u32[]{:S(2)}, u32[]{:S(2)}) collective-permute-start(bf16[128,512]{1,0:T(8,128)(2,1)S(1)} %get-tuple-element.29), channel_id=1, source_target_pairs={{0,8},{4,12},{8,0},{12,4},{1,9},{5,13},{9,1},{13,5},{2,10},{6,14},... | collective-permute-start | bytes 393224 | tf_op jit(solution)/shard_map/ppermute | solution.py:24
  46.5 6.3 %collective-permute-start.6 = (bf16[128,512]{1,0:T(8,128)(2,1)S(1)}, bf16[128,512]{1,0:T(8,128)(2,1)S(1)}, u32[]{:S(2)}, u32[]{:S(2)}) collective-permute-start(bf16[128,512]{1,0:T(8,128)(2,1)S(1)} %get-tuple-element.30), channel_id=1, source_target_pairs={{0,12},{4,0},{8,4},{12,8},{1,13},{5,1},{9,5},{13,9},{2,14},{6,2},{... | collective-permute-start | bytes 393224 | tf_op jit(solution)/shard_map/ppermute | solution.py:24

commit v3 on v2

--- a/solution.py
+++ b/solution.py
@@ -9,9 +9,10 @@
 CTX = ("x", "zl")
 CH = ("y", "zh", "c")
 GO = ("zl", "x")
-BACK = ("zh", "zl", "x")
+BACK = ("zl", "x", "zh")
 LANES = 128
 TAPS = 3
+TURN = {16: 4, 32: 0}
 ORDER = (2, 1, 3)
 WAIT = 20_000_000_000
 f32 = jnp.float32
@@ -34,9 +35,17 @@
     return count - 1 - index
 
 
+def spot(order, k, h=0):
+    count = 4 ** 2 * (2 if "zh" in order else 1)
+    return lax.rem(place(order, k, h) + lax.axis_index("c") * (count - TURN[count]), count)
+
+
 def exchange(value, order):
-    backwards = [list(reversed(range(value.shape[0])))]
-    return lax.all_to_all(value, order, 0, 0, axis_index_groups=backwards, tiled=True)
+    count = value.shape[0]
+    groups = [
+        [2 * (count - 1 - (i + c * TURN[count]) % count) + c for i in range(count)] for c in (0, 1)
+    ]
+    return lax.all_to_all(value, order + ("c",), 0, 0, axis_index_groups=groups, tiled=True)
 
 
 def near(value):
@@ -100,10 +109,10 @@
                     rims = jnp.where((lane == 4 * s + 2) | (lane == 4 * s + 3), tail, rims)
         for j in range(per):
             part = slice(j * LANES, (j + 1) * LANES)
-            sent[place(GO, k), :, part] = (value[1][j] * value[2][j]).astype(bf16)
+            sent[spot(GO, k), :, part] = (value[1][j] * value[2][j]).astype(bf16)
             part = slice(tokens + j * LANES, tokens + (j + 1) * LANES)
-            sent[place(GO, k), :, part] = value[0][j].astype(bf16)
-        sent[place(GO, k), :, 2 * tokens :] = rims.astype(bf16)
+            sent[spot(GO, k), :, part] = value[0][j].astype(bf16)
+        sent[spot(GO, k), :, 2 * tokens :] = rims.astype(bf16)
 
 
 def prep_body(decay, residue, skip_bias, short_taps, toeplitz, enter, leave, powers, taps):
@@ -160,15 +169,15 @@
     ]
     before = jnp.zeros((owned, LANES), f32)
     for k in range(shards):
-        rims = held[place(GO, k), :, 2 * tokens :].astype(f32)
+        rims = held[spot(GO, k), :, 2 * tokens :].astype(f32)
         older = pltpu.roll(before, LANES - 2, 1)
         middle = jnp.where(lane % 4 == 0, pltpu.roll(before, LANES - 3, 1), pltpu.roll(rims, 1, 1))
         head = weights[0] * rims + weights[1] * middle + weights[2] * older
         before = rims
         fixed = pltpu.roll(head, LANES - 4, 1) * pltpu.roll(head, LANES - 8, 1)
         for j in range(per):
-            now = held[place(GO, k), :, j * LANES : (j + 1) * LANES].astype(f32)
-            query = held[place(GO, k), :, tokens + j * LANES : tokens + (j + 1) * LANES].astype(f32)
+            now = held[spot(GO, k), :, j * LANES : (j + 1) * LANES].astype(f32)
+            query = held[spot(GO, k), :, tokens + j * LANES : tokens + (j + 1) * LANES].astype(f32)
             if j == 0:
                 now = jnp.where(lane < 2, fixed.astype(bf16).astype(f32), now)
                 query = jnp.where(lane < 2, head, query)
@@ -195,7 +204,7 @@
         k, j = divmod(b, per)
         value = (query_buf[b] * conv_buf[b]).astype(bf16)
         for h in range(2):
-            out[place(BACK, k, h), :, j * LANES : (j + 1) * LANES] = value
+            out[spot(BACK, k, h), :, j * LANES : (j + 1) * LANES] = value
 
 
 def hold_body(gated, w1, w2, w3, out):
@@ -205,7 +214,7 @@
 def settle_body(gated, out):
     count, owned, _ = gated.shape
     for h in range(2):
-        rows = [gated[place(BACK, k, h)] for k in range(count // 2)]
+        rows = [gated[spot(BACK, k, h)] for k in range(count // 2)]
         out[pl.ds(h * (count // 2) * owned, count // 2 * owned), :] = jnp.concatenate(rows, axis=0)
 
 
@@ -327,7 +336,7 @@
         compiler_params=params(),
         name="other",
     )(one, near(other), *close, *map(near, sums))
-    arrived = [parts[0]] + [shift(parts[d], "y", d) for d in (1, 2, 3)]
+    arrived = [parts[0]] + [shift(parts[d], "y", d) for d in (2, 1, 3)]
     return pl.pallas_call(
         add_body,
         out_shape=jax.ShapeDtypeStruct((rows, tokens), bf16),

time: 53.8 us -> 54 us (level)
  waiting for transfers between devices: 8.71 us -> 10.6 us
  starting transfers between devices: 23.7 us -> 22 us
    ppermute x7, waiting for transfers between devices: 6.26 us -> 8.97 us  [shift(): lax.ppermute(value, axis, [(i, (i + steps) % count) for i in range(count)])]
    all_to_all x1, starting transfers between devices: 10.8 us -> 9.8 us  [exchange(): lax.all_to_all(value, order + ('c',), 0, 0, axis_index_groups=groups, til...]
    all_to_all x1, waiting for transfers between devices: 2.45 us -> 1.63 us  [exchange(): lax.all_to_all(value, order + ('c',), 0, 0, axis_index_groups=groups, til...]
    ppermute x7, starting transfers between devices: 12.9 us -> 12.2 us  [shift(): lax.ppermute(value, axis, [(i, (i + steps) % count) for i in range(count)])]
  transfers between devices with their start and end apart: 8 -> 8, of which waited for: 6 -> 5; matrix products, arithmetic and copies ran while one was open for 0% -> 0% of each run, Pallas kernels for 4% -> 4%
where the time goes in v3:
time: 54 us; the launch traced here: 53.8 us
  starting transfers between devices  22 us (41%)
  blocking collectives  15.4 us (29%)
  waiting for transfers between devices  10.6 us (20%)
  Pallas kernels  5.64 us (10%)
    all_to_all x1, blocking collectives, exchange(): lax.all_to_all(value, order + ('c',), 0, 0, axis_index_groups=groups, til...  15.4 us
    ppermute x7, starting transfers between devices, shift(): lax.ppermute(value, axis, [(i, (i + steps) % count) for i in range(count)])  12.2 us
    all_to_all x1, starting transfers between devices, exchange(): lax.all_to_all(value, order + ('c',), 0, 0, axis_index_groups=groups, til...  9.8 us
    ppermute x7, waiting for transfers between devices, shift(): lax.ppermute(value, axis, [(i, (i + steps) % count) for i in range(count)])  8.97 us
    pallas_call x1, Pallas kernels, local(): pl.pallas_call(pack_body, out_shape=pltpu.VMEM((shards, owned, 2 * tokens...  2.57 us
    all_to_all x1, waiting for transfers between devices, exchange(): lax.all_to_all(value, order + ('c',), 0, 0, axis_index_groups=groups, til...  1.63 us
    pallas_call x1, Pallas kernels, local(): pl.pallas_call(conv_body, out_shape=pltpu.VMEM((2 * shards, owned, tokens...  1.14 us
  transfers between devices with their start and end apart: 8, of which 5 were waited for; matrix products, arithmetic and copies ran while one was open for 0% of the time, Pallas kernels for 4%

profile of v3, /device:TPU:1, one launch (start us, length us, event | category | flops | bytes accessed | tf_op | source)
XLA Modules:
  0.0 53.8 jit_solution(9974648424518369151)
XLA Ops:
  0.0 0.0 copy-start.4
  0.0 2.6 %pack.1 = bf16[16,8,1152]{2,1,0:T(8,128)(2,1)} custom-call(bf16[3,128,512]{2,1,0:T(8,128)(2,1)} %features_hbm.1, f32[3,3,128]{2,1,0:T(4,128)} %bitcast.3), custom_call_target="tpu_custom_call" | custom-call | tf_op jit(solution)/shard_map/pack/pallas_call | solution.py:251
  2.6 9.8 %all-to-all-start = ((bf16[16,8,1152]{2,1,0:T(8,128)(2,1)}), bf16[16,8,1152]{2,1,0:T(8,128)(2,1)S(1)}, u32[]{:S(2)}, u32[]{:S(2)}) async-start(bf16[16,8,1152]{2,1,0:T(8,128)(2,1)} %pack.1), calls=%async_computation | async-start | bytes 589824 | tf_op jit(solution)/shard_map/all_to_all | solution.py:48
  12.4 0.0 copy-done.4
  12.4 0.0 copy-start.1
  12.4 0.0 copy-start.2
  12.5 0.0 copy-start
  12.5 3.0 %collective-permute-start = (bf16[128,512]{1,0:T(8,128)(2,1)S(1)}, bf16[128,512]{1,0:T(8,128)(2,1)S(1)}, u32[]{:S(2)}, u32[]{:S(2)}) collective-permute-start(bf16[128,512]{1,0:T(8,128)(2,1)S(1)} %get-tuple-element.33), channel_id=1, source_target_pairs={{0,8},{4,12},{8,0},{12,4},{1,9},{5,13},{9,1},{13,5},{2,10},{6,14},... | collective-permute-start | bytes 393224 | tf_op jit(solution)/shard_map/ppermute | solution.py:25
  15.5 0.8 %collective-permute-start.1 = (bf16[128,512]{1,0:T(8,128)(2,1)S(1)}, bf16[128,512]{1,0:T(8,128)(2,1)S(1)}, u32[]{:S(2)}, u32[]{:S(2)}) collective-permute-start(bf16[128,512]{1,0:T(8,128)(2,1)S(1)} %get-tuple-element.32), channel_id=1, source_target_pairs={{0,12},{4,0},{8,4},{12,8},{1,13},{5,1},{9,5},{13,9},{2,14},{6,2},{... | collective-permute-start | bytes 393224 | tf_op jit(solution)/shard_map/ppermute | solution.py:25
  16.3 0.0 copy-start.3
  16.3 0.7 %collective-permute-start.2 = (bf16[128,512]{1,0:T(8,128)(2,1)S(1)}, bf16[128,512]{1,0:T(8,128)(2,1)S(1)}, u32[]{:S(2)}, u32[]{:S(2)}) collective-permute-start(bf16[128,512]{1,0:T(8,128)(2,1)S(1)} %get-tuple-element.34), channel_id=1, source_target_pairs={{0,4},{4,8},{8,12},{12,0},{1,5},{5,9},{9,13},{13,1},{2,6},{6,10},{... | collective-permute-start | bytes 393224 | tf_op jit(solution)/shard_map/ppermute | solution.py:25
  17.0 0.0 copy-done.1
  17.0 0.0 copy-done.2
  17.0 0.0 copy-done
  17.0 0.0 copy-done.3
  17.0 0.5 prep.1
  17.5 1.6 %all-to-all-done.held = bf16[16,8,1152]{2,1,0:T(8,128)(2,1)S(1)} async-done(((bf16[16,8,1152]{2,1,0:T(8,128)(2,1)}), bf16[16,8,1152]{2,1,0:T(8,128)(2,1)S(1)}, u32[]{:S(2)}, u32[]{:S(2)}) %all-to-all-start) | async-done | bytes 294944 | tf_op jit(solution)/shard_map/all_to_all | solution.py:48
  19.1 1.1 %conv.1.gated = bf16[32,8,512]{2,1,0:T(8,128)(2,1)S(1)} custom-call(bf16[16,8,1152]{2,1,0:T(8,128)(2,1)S(1)} %all-to-all-done.held, f32[9,8,128]{2,1,0:T(8,128)S(1)} %get-tuple-element.18.taps, bf16[2,8,128,128]{3,2,1,0:T(8,128)(2,1)S(1)} %get-tuple-element.19.toeplitz, bf16[2,1024,128]{2,1,0:T(8,128)(2,1)S(1)} %get-tuple-element.20.enter, ...), custom_call_target="tpu_custom_call" | custom-call | flops 20000000000 | bytes 2500000 | tf_op jit(solution)/shard_map/conv/pallas_call | solution.py:290
  20.2 0.0 collective-permute-done.w1.w2
  20.3 0.0 collective-permute-done.1.w2.w1
  20.3 1.9 %collective-permute-done.2.w3 = bf16[128,512]{1,0:T(8,128)(2,1)S(1)} collective-permute-done((bf16[128,512]{1,0:T(8,128)(2,1)S(1)}, bf16[128,512]{1,0:T(8,128)(2,1)S(1)}, u32[]{:S(2)}, u32[]{:S(2)}) %collective-permute-start.2) | collective-permute-done | bytes 131104 | tf_op jit(solution)/shard_map/ppermute | solution.py:25
  22.2 15.4 %all_to_all.10.gated = bf16[32,8,512]{2,1,0:T(8,128)(2,1)S(1)} all-to-all(bf16[32,8,512]{2,1,0:T(8,128)(2,1)S(1)} %hold.1), channel_id=1, replica_groups={{242,240,178,176,114,112,50,48,226,224,162,160,98,96,34,32,210,208,146,..., dimensions={0} | all-to-all | bytes 524288 | tf_op jit(solution)/shard_map/all_to_all | solution.py:48
  37.6 0.1 settle.1.own
  37.7 4.1 %collective-permute-start.3 = (bf16[256,512]{1,0:T(8,128)(2,1)S(1)}, bf16[256,512]{1,0:T(8,128)(2,1)S(1)}, u32[]{:S(2)}, u32[]{:S(2)}) collective-permute-start(bf16[256,512]{1,0:T(8,128)(2,1)S(1)} %settle.1.own), channel_id=1, source_target_pairs={{0,1},{1,0},{2,3},{3,2},{4,5},{5,4},{6,7},{7,6},{8,9},{9,8},{10,11... | collective-permute-start | bytes 786440 | tf_op jit(solution)/shard_map/ppermute | solution.py:25
  41.8 0.3 own.1
  42.1 0.9 %collective-permute-done.3.other = bf16[256,512]{1,0:T(8,128)(2,1)S(1)} collective-permute-done((bf16[256,512]{1,0:T(8,128)(2,1)S(1)}, bf16[256,512]{1,0:T(8,128)(2,1)S(1)}, u32[]{:S(2)}, u32[]{:S(2)}) %collective-permute-start.3) | collective-permute-done | bytes 262176 | tf_op jit(solution)/shard_map/ppermute | solution.py:25
  43.0 0.3 other.1
  43.3 1.0 %collective-permute-start.4 = (bf16[128,512]{1,0:T(8,128)(2,1)S(1)}, bf16[128,512]{1,0:T(8,128)(2,1)S(1)}, u32[]{:S(2)}, u32[]{:S(2)}) collective-permute-start(bf16[128,512]{1,0:T(8,128)(2,1)S(1)} %get-tuple-element.28), channel_id=1, source_target_pairs={{0,8},{4,12},{8,0},{12,4},{1,9},{5,13},{9,1},{13,5},{2,10},{6,14},... | collective-permute-start | bytes 393224 | tf_op jit(solution)/shard_map/ppermute | solution.py:25
  44.2 0.4 collective-permute-start.5
  44.6 2.3 %collective-permute-start.6 = (bf16[128,512]{1,0:T(8,128)(2,1)S(1)}, bf16[128,512]{1,0:T(8,128)(2,1)S(1)}, u32[]{:S(2)}, u32[]{:S(2)}) collective-permute-start(bf16[128,512]{1,0:T(8,128)(2,1)S(1)} %get-tuple-element.30), channel_id=1, source_target_pairs={{0,12},{4,0},{8,4},{12,8},{1,13},{5,1},{9,5},{13,9},{2,14},{6,2},{... | collective-permute-start | bytes 393224 | tf_op jit(solution)/shard_map/ppermute | solution.py:25
  46.9 2.7 %collective-permute-done.4.o1 = bf16[128,512]{1,0:T(8,128)(2,1)S(1)} collective-permute-done((bf16[128,512]{1,0:T(8,128)(2,1)S(1)}, bf16[128,512]{1,0:T(8,128)(2,1)S(1)}, u32[]{:S(2)}, u32[]{:S(2)}) %collective-permute-start.4) | collective-permute-done | bytes 131104 | tf_op jit(solution)/shard_map/ppermute | solution.py:25
  49.6 3.5 %collective-permute-done.5.o2 = bf16[128,512]{1,0:T(8,128)(2,1)S(1)} collective-permute-done((bf16[128,512]{1,0:T(8,128)(2,1)S(1)}, bf16[128,512]{1,0:T(8,128)(2,1)S(1)}, u32[]{:S(2)}, u32[]{:S(2)}) %collective-permute-start.5) | collective-permute-done | bytes 131104 | tf_op jit(solution)/shard_map/ppermute | solution.py:25
  53.1 0.0 collective-permute-done.6.o3
  53.1 0.7 %add.42 = bf16[128,512]{1,0:T(8,128)(2,1)} custom-call(f32[128,512]{1,0:T(8,128)S(1)} %get-tuple-element.27.o0, bf16[128,512]{1,0:T(8,128)(2,1)S(1)} %collective-permute-done.4.o1, bf16[128,512]{1,0:T(8,128)(2,1)S(1)} %collective-permute-done.5.o2, bf16[128,512]{1,0:T(8,128)(2,1)S(1)} %collective-permute-done.6.o3), custom_call_target="tpu_custom_call" | custom-call | tf_op jit(solution)/shard_map/add/pallas_call | solution.py:340
  (2 shorter events, 0.1 us)
Async XLA Ops:
  0.0 12.4 %copy-start.4 = (bf16[128,2048]{1,0:T(8,128)(2,1)S(1)}, bf16[128,2048]{1,0:T(8,128)(2,1)}, u32[]{:S(2)}) copy-start(bf16[128,2048]{1,0:T(8,128)(2,1)} %param.11) | copy-start | bytes 1572868
  2.6 16.5 %all-to-all-start = ((bf16[16,8,1152]{2,1,0:T(8,128)(2,1)}), bf16[16,8,1152]{2,1,0:T(8,128)(2,1)S(1)}, u32[]{:S(2)}, u32[]{:S(2)}) async-start(bf16[16,8,1152]{2,1,0:T(8,128)(2,1)} %pack.1), calls=%async_computation | async-start | bytes 589824 | tf_op jit(solution)/shard_map/all_to_all | solution.py:48
  12.4 4.6 %copy-start.1 = (f32[8,16]{1,0:T(8,128)S(1)}, f32[8,16]{1,0:T(8,128)}, u32[]{:S(2)}) copy-start(f32[8,16]{1,0:T(8,128)} %decay.1) | copy-start | bytes 1540
  12.4 4.6 %copy-start.2 = (f32[8,16]{1,0:T(8,128)S(1)}, f32[8,16]{1,0:T(8,128)}, u32[]{:S(2)}) copy-start(f32[8,16]{1,0:T(8,128)} %residue.1) | copy-start | bytes 1540
  12.5 4.5 %copy-start = (f32[3,128,3]{1,2,0:T(4,128)S(1)}, f32[3,128,3]{1,2,0:T(4,128)}, u32[]{:S(2)}) copy-start(f32[3,128,3]{1,2,0:T(4,128)} %param.7) | copy-start | bytes 13828
  12.5 7.8 %collective-permute-start = (bf16[128,512]{1,0:T(8,128)(2,1)S(1)}, bf16[128,512]{1,0:T(8,128)(2,1)S(1)}, u32[]{:S(2)}, u32[]{:S(2)}) collective-permute-start(bf16[128,512]{1,0:T(8,128)(2,1)S(1)} %get-tuple-element.33), channel_id=1, source_target_pairs={{0,8},{4,12},{8,0},{12,4},{1,9},{5,13},{9,1},{13,5},{2,10},{6,14},... | collective-permute-start | bytes 393224 | tf_op jit(solution)/shard_map/ppermute | solution.py:25
  15.5 4.8 %collective-permute-start.1 = (bf16[128,512]{1,0:T(8,128)(2,1)S(1)}, bf16[128,512]{1,0:T(8,128)(2,1)S(1)}, u32[]{:S(2)}, u32[]{:S(2)}) collective-permute-start(bf16[128,512]{1,0:T(8,128)(2,1)S(1)} %get-tuple-element.32), channel_id=1, source_target_pairs={{0,12},{4,0},{8,4},{12,8},{1,13},{5,1},{9,5},{13,9},{2,14},{6,2},{... | collective-permute-start | bytes 393224 | tf_op jit(solution)/shard_map/ppermute | solution.py:25
  16.3 0.7 %copy-start.3 = (f32[128]{0:T(128)S(1)}, f32[128]{0:T(128)}, u32[]{:S(2)}) copy-start(f32[128]{0:T(128)} %param.10) | copy-start | bytes 1540
  16.3 5.9 %collective-permute-start.2 = (bf16[128,512]{1,0:T(8,128)(2,1)S(1)}, bf16[128,512]{1,0:T(8,128)(2,1)S(1)}, u32[]{:S(2)}, u32[]{:S(2)}) collective-permute-start(bf16[128,512]{1,0:T(8,128)(2,1)S(1)} %get-tuple-element.34), channel_id=1, source_target_pairs={{0,4},{4,8},{8,12},{12,0},{1,5},{5,9},{9,13},{13,1},{2,6},{6,10},{... | collective-permute-start | bytes 393224 | tf_op jit(solution)/shard_map/ppermute | solution.py:25
  37.7 5.3 %collective-permute-start.3 = (bf16[256,512]{1,0:T(8,128)(2,1)S(1)}, bf16[256,512]{1,0:T(8,128)(2,1)S(1)}, u32[]{:S(2)}, u32[]{:S(2)}) collective-permute-start(bf16[256,512]{1,0:T(8,128)(2,1)S(1)} %settle.1.own), channel_id=1, source_target_pairs={{0,1},{1,0},{2,3},{3,2},{4,5},{5,4},{6,7},{7,6},{8,9},{9,8},{10,11... | collective-permute-start | bytes 786440 | tf_op jit(solution)/shard_map/ppermute | solution.py:25
  43.3 6.3 %collective-permute-start.4 = (bf16[128,512]{1,0:T(8,128)(2,1)S(1)}, bf16[128,512]{1,0:T(8,128)(2,1)S(1)}, u32[]{:S(2)}, u32[]{:S(2)}) collective-permute-start(bf16[128,512]{1,0:T(8,128)(2,1)S(1)} %get-tuple-element.28), channel_id=1, source_target_pairs={{0,8},{4,12},{8,0},{12,4},{1,9},{5,13},{9,1},{13,5},{2,10},{6,14},... | collective-permute-start | bytes 393224 | tf_op jit(solution)/shard_map/ppermute | solution.py:25
  44.2 8.9 %collective-permute-start.5 = (bf16[128,512]{1,0:T(8,128)(2,1)S(1)}, bf16[128,512]{1,0:T(8,128)(2,1)S(1)}, u32[]{:S(2)}, u32[]{:S(2)}) collective-permute-start(bf16[128,512]{1,0:T(8,128)(2,1)S(1)} %get-tuple-element.29), channel_id=1, source_target_pairs={{0,4},{4,8},{8,12},{12,0},{1,5},{5,9},{9,13},{13,1},{2,6},{6,10},{... | collective-permute-start | bytes 393224 | tf_op jit(solution)/shard_map/ppermute | solution.py:25
  44.6 8.4 %collective-permute-start.6 = (bf16[128,512]{1,0:T(8,128)(2,1)S(1)}, bf16[128,512]{1,0:T(8,128)(2,1)S(1)}, u32[]{:S(2)}, u32[]{:S(2)}) collective-permute-start(bf16[128,512]{1,0:T(8,128)(2,1)S(1)} %get-tuple-element.30), channel_id=1, source_target_pairs={{0,12},{4,0},{8,4},{12,8},{1,13},{5,1},{9,5},{13,9},{2,14},{6,2},{... | collective-permute-start | bytes 393224 | tf_op jit(solution)/shard_map/ppermute | solution.py:25

commit v4 on v3

--- a/solution.py
+++ b/solution.py
@@ -12,7 +12,7 @@
 BACK = ("zl", "x", "zh")
 LANES = 128
 TAPS = 3
-TURN = {16: 4, 32: 0}
+TURN = {16: (8, 4), 32: (4, 0)}
 ORDER = (2, 1, 3)
 WAIT = 20_000_000_000
 f32 = jnp.float32
@@ -37,13 +37,15 @@
 
 def spot(order, k, h=0):
     count = 4 ** 2 * (2 if "zh" in order else 1)
-    return lax.rem(place(order, k, h) + lax.axis_index("c") * (count - TURN[count]), count)
+    first, second = TURN[count]
+    turned = jnp.where(lax.axis_index("c") == 0, count - first, count - second)
+    return lax.rem(place(order, k, h) + turned, count)
 
 
 def exchange(value, order):
     count = value.shape[0]
     groups = [
-        [2 * (count - 1 - (i + c * TURN[count]) % count) + c for i in range(count)] for c in (0, 1)
+        [2 * (count - 1 - (i + TURN[count][c]) % count) + c for i in range(count)] for c in (0, 1)
     ]
     return lax.all_to_all(value, order + ("c",), 0, 0, axis_index_groups=groups, tiled=True)
 
@@ -60,10 +62,9 @@
     return lax.axis_index("x") * lax.axis_size("zl") + lax.axis_index("zl")
 
 
-def split_store(ref, index, value):
+def split(value):
     high = value.astype(bf16)
-    ref[(0,) + index] = high
-    ref[(1,) + index] = (value - high.astype(f32)).astype(bf16)
+    return high, (value - high.astype(f32)).astype(bf16)
 
 
 def pack_body(features_hbm, taps_hbm, sent, features, short_taps, sem):
@@ -145,10 +146,17 @@
     for c in range(owned):
         spread = jnp.broadcast_to(impulse[c : c + 1, :], (LANES, LANES))
         rolled = pltpu.roll(spread, 0, 1, stride=1, stride_axis=0)
-        split_store(toeplitz, (c,), jnp.where(col >= row, rolled, 0.0))
-        part = pl.ds(c * LANES, LANES)
-        split_store(enter, (part, slice(None)), jnp.where(col // modes == c, into, 0.0))
-        split_store(leave, (slice(None), part), jnp.where(row // modes == c, out_of, 0.0))
+        high, low = split(jnp.where(col >= row, rolled, 0.0))
+        toeplitz[c, :LANES, :] = high
+        toeplitz[c, LANES:, :] = low
+        part = slice(c * LANES, (c + 1) * LANES)
+        high, low = split(jnp.where(col // modes == c, into, 0.0))
+        enter[part, :LANES] = high
+        enter[part, LANES:] = low
+        high, low = split(jnp.where(row // modes == c, out_of, 0.0))
+        leave[:LANES, part] = high
+        leave[LANES : 2 * LANES, part] = high
+        leave[2 * LANES :, part] = low
     for i in range(8):
         powers[i : i + 1, :] = jnp.exp(-rate * float(LANES << i))
 
@@ -185,7 +193,8 @@
             query_buf[k * per + j] = query
     mixed = [mixed_buf[:, c, :].astype(bf16) for c in range(owned)]
     whole = jnp.concatenate(mixed, axis=1)
-    state = dot(whole, enter[0]) + dot(whole, enter[1])
+    state = dot(whole, enter[...])
+    state = state[:, :LANES] + state[:, LANES:]
     row = lax.broadcasted_iota(jnp.int32, (blocks, LANES), 0)
     step, i = 1, 0
     while step < blocks:
@@ -193,13 +202,11 @@
         state = state + powers[i : i + 1, :] * moved
         step, i = step * 2, i + 1
     state = jnp.where(row < 1, 0.0, pltpu.roll(state, 1, 0))
-    high = state.astype(bf16)
-    low = (state - high.astype(f32)).astype(bf16)
+    high, low = split(state)
+    carried = dot(jnp.concatenate([high, low, high], axis=1), leave[...])
     for c in range(owned):
-        part = pl.ds(c * LANES, LANES)
-        value = dot(mixed[c], toeplitz[0, c]) + dot(mixed[c], toeplitz[1, c])
-        value = value + dot(high, leave[0, :, part]) + dot(high, leave[1, :, part])
-        conv_buf[:, c, :] = value + dot(low, leave[0, :, part])
+        value = dot(jnp.concatenate([mixed[c], mixed[c]], axis=1), toeplitz[c])
+        conv_buf[:, c, :] = value + carried[:, c * LANES : (c + 1) * LANES]
     for b in range(blocks):
         k, j = divmod(b, per)
         value = (query_buf[b] * conv_buf[b]).astype(bf16)
@@ -274,9 +281,9 @@
     mats = pl.pallas_call(
         prep_body,
         out_shape=(
-            pltpu.VMEM((2, owned, LANES, LANES), bf16),
-            pltpu.VMEM((2, owned * LANES, LANES), bf16),
-            pltpu.VMEM((2, LANES, owned * LANES), bf16),
+            pltpu.VMEM((owned, 2 * LANES, LANES), bf16),
+            pltpu.VMEM((owned * LANES, 2 * LANES), bf16),
+            pltpu.VMEM((3 * LANES, owned * LANES), bf16),
             pltpu.VMEM((8, LANES), f32),
             pltpu.VMEM((3 * TAPS, owned, LANES), f32),
         ),

time: 54 us -> 52.2 us (0.967)
  waiting for transfers between devices: 10.6 us -> 7.93 us
  blocking collectives: 15.4 us -> 16.5 us
    all_to_all x1, waiting for transfers between devices: 1.63 us -> 0.01 us  [exchange(): lax.all_to_all(value, order + ('c',), 0, 0, axis_index_groups=groups, til...]
    all_to_all x1, blocking collectives: 15.4 us -> 16.5 us  [exchange(): lax.all_to_all(value, order + ('c',), 0, 0, axis_index_groups=groups, til...]
    ppermute x7, waiting for transfers between devices: 8.97 us -> 7.93 us  [shift(): lax.ppermute(value, axis, [(i, (i + steps) % count) for i in range(count)])]
  transfers between devices with their start and end apart: 8 -> 8, of which waited for: 5 -> 6; matrix products, arithmetic and copies ran while one was open for 0% -> 0% of each run, Pallas kernels for 4% -> 4%
where the time goes in v4:
time: 52.2 us; the launch traced here: 52 us
  starting transfers between devices  21.9 us (42%)
  blocking collectives  16.5 us (32%)
  waiting for transfers between devices  7.93 us (15%)
  Pallas kernels  5.56 us (11%)
    all_to_all x1, blocking collectives, exchange(): lax.all_to_all(value, order + ('c',), 0, 0, axis_index_groups=groups, til...  16.5 us
    ppermute x7, starting transfers between devices, shift(): lax.ppermute(value, axis, [(i, (i + steps) % count) for i in range(count)])  12.1 us
    all_to_all x1, starting transfers between devices, exchange(): lax.all_to_all(value, order + ('c',), 0, 0, axis_index_groups=groups, til...  9.8 us
    ppermute x7, waiting for transfers between devices, shift(): lax.ppermute(value, axis, [(i, (i + steps) % count) for i in range(count)])  7.93 us
    pallas_call x1, Pallas kernels, local(): pl.pallas_call(pack_body, out_shape=pltpu.VMEM((shards, owned, 2 * tokens...  2.58 us
  transfers between devices with their start and end apart: 8, of which 6 were waited for; matrix products, arithmetic and copies ran while one was open for 0% of the time, Pallas kernels for 4%

profile of v4, /device:TPU:1, one launch (start us, length us, event | category | flops | bytes accessed | tf_op | source)
XLA Modules:
  0.0 52.0 jit_solution(11255794772501972600)
XLA Ops:
  0.0 0.0 copy-start.4
  0.0 2.6 %pack.1 = bf16[16,8,1152]{2,1,0:T(8,128)(2,1)} custom-call(bf16[3,128,512]{2,1,0:T(8,128)(2,1)} %features_hbm.1, f32[3,3,128]{2,1,0:T(4,128)} %bitcast.3), custom_call_target="tpu_custom_call" | custom-call | tf_op jit(solution)/shard_map/pack/pallas_call | solution.py:258
  2.6 9.8 %all-to-all-start = ((bf16[16,8,1152]{2,1,0:T(8,128)(2,1)}), bf16[16,8,1152]{2,1,0:T(8,128)(2,1)S(1)}, u32[]{:S(2)}, u32[]{:S(2)}) async-start(bf16[16,8,1152]{2,1,0:T(8,128)(2,1)} %pack.1), calls=%async_computation | async-start | bytes 589824 | tf_op jit(solution)/shard_map/all_to_all | solution.py:50
  12.4 0.0 copy-done.4
  12.4 0.0 copy-start.1
  12.4 0.0 copy-start.2
  12.5 0.0 copy-start
  12.5 3.0 %collective-permute-start = (bf16[128,512]{1,0:T(8,128)(2,1)S(1)}, bf16[128,512]{1,0:T(8,128)(2,1)S(1)}, u32[]{:S(2)}, u32[]{:S(2)}) collective-permute-start(bf16[128,512]{1,0:T(8,128)(2,1)S(1)} %get-tuple-element.33), channel_id=1, source_target_pairs={{0,8},{4,12},{8,0},{12,4},{1,9},{5,13},{9,1},{13,5},{2,10},{6,14},... | collective-permute-start | bytes 393224 | tf_op jit(solution)/shard_map/ppermute | solution.py:25
  15.5 0.8 %collective-permute-start.1 = (bf16[128,512]{1,0:T(8,128)(2,1)S(1)}, bf16[128,512]{1,0:T(8,128)(2,1)S(1)}, u32[]{:S(2)}, u32[]{:S(2)}) collective-permute-start(bf16[128,512]{1,0:T(8,128)(2,1)S(1)} %get-tuple-element.32), channel_id=1, source_target_pairs={{0,12},{4,0},{8,4},{12,8},{1,13},{5,1},{9,5},{13,9},{2,14},{6,2},{... | collective-permute-start | bytes 393224 | tf_op jit(solution)/shard_map/ppermute | solution.py:25
  16.3 0.0 copy-start.3
  16.3 0.7 %collective-permute-start.2 = (bf16[128,512]{1,0:T(8,128)(2,1)S(1)}, bf16[128,512]{1,0:T(8,128)(2,1)S(1)}, u32[]{:S(2)}, u32[]{:S(2)}) collective-permute-start(bf16[128,512]{1,0:T(8,128)(2,1)S(1)} %get-tuple-element.34), channel_id=1, source_target_pairs={{0,4},{4,8},{8,12},{12,0},{1,5},{5,9},{9,13},{13,1},{2,6},{6,10},{... | collective-permute-start | bytes 393224 | tf_op jit(solution)/shard_map/ppermute | solution.py:25
  17.0 0.0 copy-done.1
  17.0 0.0 copy-done.2
  17.0 0.0 copy-done
  17.0 0.0 copy-done.3
  17.0 0.6 %prep.1 = (bf16[8,256,128]{2,1,0:T(8,128)(2,1)S(1)}, bf16[1024,256]{1,0:T(8,128)(2,1)S(1)}, bf16[384,1024]{1,0:T(8,128)(2,1)S(1)}, f32[8,128]{1,0:T(8,128)S(1)}, f32[9,8,128]{2,1,0:T(8,128)S(1)}) custom-call(f32[8,16]{1,0:T(8,128)S(1)} %copy-done.1, f32[8,16]{1,0:T(8,128)S(1)} %copy-done.2, f32[1,128]{1,0:T(1,128)S(1)} %bitcast.5, f32[3,3,128]{2,1,0:T(4,128)S(1)} %bitcast.4), custom_call_target="tpu_custom_call" | custom-call | flops 2000000 | bytes 1600000 | tf_op jit(solution)/shard_map/prep/pallas_call | solution.py:281
  17.6 0.0 all-to-all-done.held
  17.6 1.0 %conv.1.gated = bf16[32,8,512]{2,1,0:T(8,128)(2,1)S(1)} custom-call(bf16[16,8,1152]{2,1,0:T(8,128)(2,1)S(1)} %all-to-all-done.held, f32[9,8,128]{2,1,0:T(8,128)S(1)} %get-tuple-element.18.taps, bf16[8,256,128]{2,1,0:T(8,128)(2,1)S(1)} %get-tuple-element.19.toeplitz, bf16[1024,256]{1,0:T(8,128)(2,1)S(1)} %get-tuple-element.20.enter, ...), custom_call_target="tpu_custom_call" | custom-call | flops 20000000000 | bytes 2500000 | tf_op jit(solution)/shard_map/conv/pallas_call | solution.py:297
  18.6 0.0 collective-permute-done.w1.w2
  18.6 2.3 %collective-permute-done.1.w2.w1 = bf16[128,512]{1,0:T(8,128)(2,1)S(1)} collective-permute-done((bf16[128,512]{1,0:T(8,128)(2,1)S(1)}, bf16[128,512]{1,0:T(8,128)(2,1)S(1)}, u32[]{:S(2)}, u32[]{:S(2)}) %collective-permute-start.1) | collective-permute-done | bytes 131104 | tf_op jit(solution)/shard_map/ppermute | solution.py:25
  20.9 0.7 %collective-permute-done.2.w3 = bf16[128,512]{1,0:T(8,128)(2,1)S(1)} collective-permute-done((bf16[128,512]{1,0:T(8,128)(2,1)S(1)}, bf16[128,512]{1,0:T(8,128)(2,1)S(1)}, u32[]{:S(2)}, u32[]{:S(2)}) %collective-permute-start.2) | collective-permute-done | bytes 131104 | tf_op jit(solution)/shard_map/ppermute | solution.py:25
  21.7 16.5 %all_to_all.10.gated = bf16[32,8,512]{2,1,0:T(8,128)(2,1)S(1)} all-to-all(bf16[32,8,512]{2,1,0:T(8,128)(2,1)S(1)} %hold.1), channel_id=1, replica_groups={{114,112,50,48,226,224,162,160,98,96,34,32,210,208,146,144,82,80,18,16,..., dimensions={0} | all-to-all | bytes 524288 | tf_op jit(solution)/shard_map/all_to_all | solution.py:50
  38.1 0.1 settle.1.own
  38.2 2.0 %collective-permute-start.3 = (bf16[256,512]{1,0:T(8,128)(2,1)S(1)}, bf16[256,512]{1,0:T(8,128)(2,1)S(1)}, u32[]{:S(2)}, u32[]{:S(2)}) collective-permute-start(bf16[256,512]{1,0:T(8,128)(2,1)S(1)} %settle.1.own), channel_id=1, source_target_pairs={{0,1},{1,0},{2,3},{3,2},{4,5},{5,4},{6,7},{7,6},{8,9},{9,8},{10,11... | collective-permute-start | bytes 786440 | tf_op jit(solution)/shard_map/ppermute | solution.py:25
  40.2 0.3 own.1
  40.5 0.9 %collective-permute-done.3.other = bf16[256,512]{1,0:T(8,128)(2,1)S(1)} collective-permute-done((bf16[256,512]{1,0:T(8,128)(2,1)S(1)}, bf16[256,512]{1,0:T(8,128)(2,1)S(1)}, u32[]{:S(2)}, u32[]{:S(2)}) %collective-permute-start.3) | collective-permute-done | bytes 262176 | tf_op jit(solution)/shard_map/ppermute | solution.py:25
  41.3 0.3 other.1
  41.6 3.0 %collective-permute-start.4 = (bf16[128,512]{1,0:T(8,128)(2,1)S(1)}, bf16[128,512]{1,0:T(8,128)(2,1)S(1)}, u32[]{:S(2)}, u32[]{:S(2)}) collective-permute-start(bf16[128,512]{1,0:T(8,128)(2,1)S(1)} %get-tuple-element.28), channel_id=1, source_target_pairs={{0,8},{4,12},{8,0},{12,4},{1,9},{5,13},{9,1},{13,5},{2,10},{6,14},... | collective-permute-start | bytes 393224 | tf_op jit(solution)/shard_map/ppermute | solution.py:25
  44.6 0.5 %collective-permute-start.5 = (bf16[128,512]{1,0:T(8,128)(2,1)S(1)}, bf16[128,512]{1,0:T(8,128)(2,1)S(1)}, u32[]{:S(2)}, u32[]{:S(2)}) collective-permute-start(bf16[128,512]{1,0:T(8,128)(2,1)S(1)} %get-tuple-element.29), channel_id=1, source_target_pairs={{0,4},{4,8},{8,12},{12,0},{1,5},{5,9},{9,13},{13,1},{2,6},{6,10},{... | collective-permute-start | bytes 393224 | tf_op jit(solution)/shard_map/ppermute | solution.py:25
  45.2 2.2 %collective-permute-start.6 = (bf16[128,512]{1,0:T(8,128)(2,1)S(1)}, bf16[128,512]{1,0:T(8,128)(2,1)S(1)}, u32[]{:S(2)}, u32[]{:S(2)}) collective-permute-start(bf16[128,512]{1,0:T(8,128)(2,1)S(1)} %get-tuple-element.30), channel_id=1, source_target_pairs={{0,12},{4,0},{8,4},{12,8},{1,13},{5,1},{9,5},{13,9},{2,14},{6,2},{... | collective-permute-start | bytes 393224 | tf_op jit(solution)/shard_map/ppermute | solution.py:25
  47.3 0.6 %collective-permute-done.4.o1 = bf16[128,512]{1,0:T(8,128)(2,1)S(1)} collective-permute-done((bf16[128,512]{1,0:T(8,128)(2,1)S(1)}, bf16[128,512]{1,0:T(8,128)(2,1)S(1)}, u32[]{:S(2)}, u32[]{:S(2)}) %collective-permute-start.4) | collective-permute-done | bytes 131104 | tf_op jit(solution)/shard_map/ppermute | solution.py:25
  47.9 3.2 %collective-permute-done.5.o2 = bf16[128,512]{1,0:T(8,128)(2,1)S(1)} collective-permute-done((bf16[128,512]{1,0:T(8,128)(2,1)S(1)}, bf16[128,512]{1,0:T(8,128)(2,1)S(1)}, u32[]{:S(2)}, u32[]{:S(2)}) %collective-permute-start.5) | collective-permute-done | bytes 131104 | tf_op jit(solution)/shard_map/ppermute | solution.py:25
  51.1 0.2 collective-permute-done.6.o3
  51.3 0.7 %add.42 = bf16[128,512]{1,0:T(8,128)(2,1)} custom-call(f32[128,512]{1,0:T(8,128)S(1)} %get-tuple-element.27.o0, bf16[128,512]{1,0:T(8,128)(2,1)S(1)} %collective-permute-done.4.o1, bf16[128,512]{1,0:T(8,128)(2,1)S(1)} %collective-permute-done.5.o2, bf16[128,512]{1,0:T(8,128)(2,1)S(1)} %collective-permute-done.6.o3), custom_call_target="tpu_custom_call" | custom-call | tf_op jit(solution)/shard_map/add/pallas_call | solution.py:347
  (2 shorter events, 0.1 us)
Async XLA Ops:
  0.0 12.4 %copy-start.4 = (bf16[128,2048]{1,0:T(8,128)(2,1)S(1)}, bf16[128,2048]{1,0:T(8,128)(2,1)}, u32[]{:S(2)}) copy-start(bf16[128,2048]{1,0:T(8,128)(2,1)} %param.11) | copy-start | bytes 1572868
  2.6 15.0 %all-to-all-start = ((bf16[16,8,1152]{2,1,0:T(8,128)(2,1)}), bf16[16,8,1152]{2,1,0:T(8,128)(2,1)S(1)}, u32[]{:S(2)}, u32[]{:S(2)}) async-start(bf16[16,8,1152]{2,1,0:T(8,128)(2,1)} %pack.1), calls=%async_computation | async-start | bytes 589824 | tf_op jit(solution)/shard_map/all_to_all | solution.py:50
  12.4 4.6 %copy-start.1 = (f32[8,16]{1,0:T(8,128)S(1)}, f32[8,16]{1,0:T(8,128)}, u32[]{:S(2)}) copy-start(f32[8,16]{1,0:T(8,128)} %decay.1) | copy-start | bytes 1540
  12.4 4.6 %copy-start.2 = (f32[8,16]{1,0:T(8,128)S(1)}, f32[8,16]{1,0:T(8,128)}, u32[]{:S(2)}) copy-start(f32[8,16]{1,0:T(8,128)} %residue.1) | copy-start | bytes 1540
  12.5 4.5 %copy-start = (f32[3,128,3]{1,2,0:T(4,128)S(1)}, f32[3,128,3]{1,2,0:T(4,128)}, u32[]{:S(2)}) copy-start(f32[3,128,3]{1,2,0:T(4,128)} %param.7) | copy-start | bytes 13828
  12.5 6.1 %collective-permute-start = (bf16[128,512]{1,0:T(8,128)(2,1)S(1)}, bf16[128,512]{1,0:T(8,128)(2,1)S(1)}, u32[]{:S(2)}, u32[]{:S(2)}) collective-permute-start(bf16[128,512]{1,0:T(8,128)(2,1)S(1)} %get-tuple-element.33), channel_id=1, source_target_pairs={{0,8},{4,12},{8,0},{12,4},{1,9},{5,13},{9,1},{13,5},{2,10},{6,14},... | collective-permute-start | bytes 393224 | tf_op jit(solution)/shard_map/ppermute | solution.py:25
  15.5 5.4 %collective-permute-start.1 = (bf16[128,512]{1,0:T(8,128)(2,1)S(1)}, bf16[128,512]{1,0:T(8,128)(2,1)S(1)}, u32[]{:S(2)}, u32[]{:S(2)}) collective-permute-start(bf16[128,512]{1,0:T(8,128)(2,1)S(1)} %get-tuple-element.32), channel_id=1, source_target_pairs={{0,12},{4,0},{8,4},{12,8},{1,13},{5,1},{9,5},{13,9},{2,14},{6,2},{... | collective-permute-start | bytes 393224 | tf_op jit(solution)/shard_map/ppermute | solution.py:25
  16.3 0.7 %copy-start.3 = (f32[128]{0:T(128)S(1)}, f32[128]{0:T(128)}, u32[]{:S(2)}) copy-start(f32[128]{0:T(128)} %param.10) | copy-start | bytes 1540
  16.3 5.4 %collective-permute-start.2 = (bf16[128,512]{1,0:T(8,128)(2,1)S(1)}, bf16[128,512]{1,0:T(8,128)(2,1)S(1)}, u32[]{:S(2)}, u32[]{:S(2)}) collective-permute-start(bf16[128,512]{1,0:T(8,128)(2,1)S(1)} %get-tuple-element.34), channel_id=1, source_target_pairs={{0,4},{4,8},{8,12},{12,0},{1,5},{5,9},{9,13},{13,1},{2,6},{6,10},{... | collective-permute-start | bytes 393224 | tf_op jit(solution)/shard_map/ppermute | solution.py:25
  38.2 3.1 %collective-permute-start.3 = (bf16[256,512]{1,0:T(8,128)(2,1)S(1)}, bf16[256,512]{1,0:T(8,128)(2,1)S(1)}, u32[]{:S(2)}, u32[]{:S(2)}) collective-permute-start(bf16[256,512]{1,0:T(8,128)(2,1)S(1)} %settle.1.own), channel_id=1, source_target_pairs={{0,1},{1,0},{2,3},{3,2},{4,5},{5,4},{6,7},{7,6},{8,9},{9,8},{10,11... | collective-permute-start | bytes 786440 | tf_op jit(solution)/shard_map/ppermute | solution.py:25
  41.6 6.3 %collective-permute-start.4 = (bf16[128,512]{1,0:T(8,128)(2,1)S(1)}, bf16[128,512]{1,0:T(8,128)(2,1)S(1)}, u32[]{:S(2)}, u32[]{:S(2)}) collective-permute-start(bf16[128,512]{1,0:T(8,128)(2,1)S(1)} %get-tuple-element.28), channel_id=1, source_target_pairs={{0,8},{4,12},{8,0},{12,4},{1,9},{5,13},{9,1},{13,5},{2,10},{6,14},... | collective-permute-start | bytes 393224 | tf_op jit(solution)/shard_map/ppermute | solution.py:25
  44.6 6.5 %collective-permute-start.5 = (bf16[128,512]{1,0:T(8,128)(2,1)S(1)}, bf16[128,512]{1,0:T(8,128)(2,1)S(1)}, u32[]{:S(2)}, u32[]{:S(2)}) collective-permute-start(bf16[128,512]{1,0:T(8,128)(2,1)S(1)} %get-tuple-element.29), channel_id=1, source_target_pairs={{0,4},{4,8},{8,12},{12,0},{1,5},{5,9},{9,13},{13,1},{2,6},{6,10},{... | collective-permute-start | bytes 393224 | tf_op jit(solution)/shard_map/ppermute | solution.py:25
  45.2 6.1 %collective-permute-start.6 = (bf16[128,512]{1,0:T(8,128)(2,1)S(1)}, bf16[128,512]{1,0:T(8,128)(2,1)S(1)}, u32[]{:S(2)}, u32[]{:S(2)}) collective-permute-start(bf16[128,512]{1,0:T(8,128)(2,1)S(1)} %get-tuple-element.30), channel_id=1, source_target_pairs={{0,12},{4,0},{8,4},{12,8},{1,13},{5,1},{9,5},{13,9},{2,14},{6,2},{... | collective-permute-start | bytes 393224 | tf_op jit(solution)/shard_map/ppermute | solution.py:25

commit v5 on v4

--- a/solution.py
+++ b/solution.py
@@ -12,7 +12,7 @@
 BACK = ("zl", "x", "zh")
 LANES = 128
 TAPS = 3
-TURN = {16: (8, 4), 32: (4, 0)}
+TURN = {16: (8, 4), 32: (20, 4)}
 ORDER = (2, 1, 3)
 WAIT = 20_000_000_000
 f32 = jnp.float32

time: 52.2 us -> 51.4 us (0.985)
  blocking collectives: 16.5 us -> 14.1 us
  starting transfers between devices: 21.9 us -> 23.4 us
    all_to_all x1, blocking collectives: 16.5 us -> 14.1 us  [exchange(): lax.all_to_all(value, order + ('c',), 0, 0, axis_index_groups=groups, til...]
    ppermute x7, starting transfers between devices: 12.1 us -> 13.6 us  [shift(): lax.ppermute(value, axis, [(i, (i + steps) % count) for i in range(count)])]
where the time goes in v5:
time: 51.4 us; the launch traced here: 51.2 us
  starting transfers between devices  23.4 us (46%)
  blocking collectives  14.1 us (27%)
  waiting for transfers between devices  7.94 us (15%)
  Pallas kernels  5.56 us (11%)
    all_to_all x1, blocking collectives, exchange(): lax.all_to_all(value, order + ('c',), 0, 0, axis_index_groups=groups, til...  14.1 us
    ppermute x7, starting transfers between devices, shift(): lax.ppermute(value, axis, [(i, (i + steps) % count) for i in range(count)])  13.6 us
    all_to_all x1, starting transfers between devices, exchange(): lax.all_to_all(value, order + ('c',), 0, 0, axis_index_groups=groups, til...  9.8 us
    ppermute x7, waiting for transfers between devices, shift(): lax.ppermute(value, axis, [(i, (i + steps) % count) for i in range(count)])  7.94 us
    pallas_call x1, Pallas kernels, local(): pl.pallas_call(pack_body, out_shape=pltpu.VMEM((shards, owned, 2 * tokens...  2.58 us
  transfers between devices with their start and end apart: 8, of which 6 were waited for; matrix products, arithmetic and copies ran while one was open for 0% of the time, Pallas kernels for 4%

profile of v5, /device:TPU:1, one launch (start us, length us, event | category | flops | bytes accessed | tf_op | source)
XLA Modules:
  0.0 51.2 jit_solution(1220519228485140847)
XLA Ops:
  0.0 0.0 copy-start.4
  0.0 2.6 %pack.1 = bf16[16,8,1152]{2,1,0:T(8,128)(2,1)} custom-call(bf16[3,128,512]{2,1,0:T(8,128)(2,1)} %features_hbm.1, f32[3,3,128]{2,1,0:T(4,128)} %bitcast.3), custom_call_target="tpu_custom_call" | custom-call | tf_op jit(solution)/shard_map/pack/pallas_call | solution.py:258
  2.6 9.8 %all-to-all-start = ((bf16[16,8,1152]{2,1,0:T(8,128)(2,1)}), bf16[16,8,1152]{2,1,0:T(8,128)(2,1)S(1)}, u32[]{:S(2)}, u32[]{:S(2)}) async-start(bf16[16,8,1152]{2,1,0:T(8,128)(2,1)} %pack.1), calls=%async_computation | async-start | bytes 589824 | tf_op jit(solution)/shard_map/all_to_all | solution.py:50
  12.4 0.0 copy-done.4
  12.4 0.0 copy-start.1
  12.4 0.0 copy-start.2
  12.5 0.0 copy-start
  12.5 3.0 %collective-permute-start = (bf16[128,512]{1,0:T(8,128)(2,1)S(1)}, bf16[128,512]{1,0:T(8,128)(2,1)S(1)}, u32[]{:S(2)}, u32[]{:S(2)}) collective-permute-start(bf16[128,512]{1,0:T(8,128)(2,1)S(1)} %get-tuple-element.33), channel_id=1, source_target_pairs={{0,8},{4,12},{8,0},{12,4},{1,9},{5,13},{9,1},{13,5},{2,10},{6,14},... | collective-permute-start | bytes 393224 | tf_op jit(solution)/shard_map/ppermute | solution.py:25
  15.5 0.8 %collective-permute-start.1 = (bf16[128,512]{1,0:T(8,128)(2,1)S(1)}, bf16[128,512]{1,0:T(8,128)(2,1)S(1)}, u32[]{:S(2)}, u32[]{:S(2)}) collective-permute-start(bf16[128,512]{1,0:T(8,128)(2,1)S(1)} %get-tuple-element.32), channel_id=1, source_target_pairs={{0,12},{4,0},{8,4},{12,8},{1,13},{5,1},{9,5},{13,9},{2,14},{6,2},{... | collective-permute-start | bytes 393224 | tf_op jit(solution)/shard_map/ppermute | solution.py:25
  16.3 0.0 copy-start.3
  16.3 0.7 %collective-permute-start.2 = (bf16[128,512]{1,0:T(8,128)(2,1)S(1)}, bf16[128,512]{1,0:T(8,128)(2,1)S(1)}, u32[]{:S(2)}, u32[]{:S(2)}) collective-permute-start(bf16[128,512]{1,0:T(8,128)(2,1)S(1)} %get-tuple-element.34), channel_id=1, source_target_pairs={{0,4},{4,8},{8,12},{12,0},{1,5},{5,9},{9,13},{13,1},{2,6},{6,10},{... | collective-permute-start | bytes 393224 | tf_op jit(solution)/shard_map/ppermute | solution.py:25
  17.0 0.0 copy-done.1
  17.0 0.0 copy-done.2
  17.0 0.0 copy-done
  17.0 0.0 copy-done.3
  17.0 0.6 %prep.1 = (bf16[8,256,128]{2,1,0:T(8,128)(2,1)S(1)}, bf16[1024,256]{1,0:T(8,128)(2,1)S(1)}, bf16[384,1024]{1,0:T(8,128)(2,1)S(1)}, f32[8,128]{1,0:T(8,128)S(1)}, f32[9,8,128]{2,1,0:T(8,128)S(1)}) custom-call(f32[8,16]{1,0:T(8,128)S(1)} %copy-done.1, f32[8,16]{1,0:T(8,128)S(1)} %copy-done.2, f32[1,128]{1,0:T(1,128)S(1)} %bitcast.5, f32[3,3,128]{2,1,0:T(4,128)S(1)} %bitcast.4), custom_call_target="tpu_custom_call" | custom-call | flops 2000000 | bytes 1600000 | tf_op jit(solution)/shard_map/prep/pallas_call | solution.py:281
  17.6 0.0 all-to-all-done.held
  17.6 1.0 %conv.1.gated = bf16[32,8,512]{2,1,0:T(8,128)(2,1)S(1)} custom-call(bf16[16,8,1152]{2,1,0:T(8,128)(2,1)S(1)} %all-to-all-done.held, f32[9,8,128]{2,1,0:T(8,128)S(1)} %get-tuple-element.18.taps, bf16[8,256,128]{2,1,0:T(8,128)(2,1)S(1)} %get-tuple-element.19.toeplitz, bf16[1024,256]{1,0:T(8,128)(2,1)S(1)} %get-tuple-element.20.enter, ...), custom_call_target="tpu_custom_call" | custom-call | flops 20000000000 | bytes 2500000 | tf_op jit(solution)/shard_map/conv/pallas_call | solution.py:297
  18.6 0.0 collective-permute-done.w1.w2
  18.6 2.3 %collective-permute-done.1.w2.w1 = bf16[128,512]{1,0:T(8,128)(2,1)S(1)} collective-permute-done((bf16[128,512]{1,0:T(8,128)(2,1)S(1)}, bf16[128,512]{1,0:T(8,128)(2,1)S(1)}, u32[]{:S(2)}, u32[]{:S(2)}) %collective-permute-start.1) | collective-permute-done | bytes 131104 | tf_op jit(solution)/shard_map/ppermute | solution.py:25
  20.9 0.7 %collective-permute-done.2.w3 = bf16[128,512]{1,0:T(8,128)(2,1)S(1)} collective-permute-done((bf16[128,512]{1,0:T(8,128)(2,1)S(1)}, bf16[128,512]{1,0:T(8,128)(2,1)S(1)}, u32[]{:S(2)}, u32[]{:S(2)}) %collective-permute-start.2) | collective-permute-done | bytes 131104 | tf_op jit(solution)/shard_map/ppermute | solution.py:25
  21.7 14.1 %all_to_all.10.gated = bf16[32,8,512]{2,1,0:T(8,128)(2,1)S(1)} all-to-all(bf16[32,8,512]{2,1,0:T(8,128)(2,1)S(1)} %hold.1), channel_id=1, replica_groups={{82,80,18,16,194,192,130,128,66,64,2,0,242,240,178,176,114,112,50,48,22..., dimensions={0} | all-to-all | bytes 524288 | tf_op jit(solution)/shard_map/all_to_all | solution.py:50
  35.8 0.1 settle.1.own
  35.9 3.5 %collective-permute-start.3 = (bf16[256,512]{1,0:T(8,128)(2,1)S(1)}, bf16[256,512]{1,0:T(8,128)(2,1)S(1)}, u32[]{:S(2)}, u32[]{:S(2)}) collective-permute-start(bf16[256,512]{1,0:T(8,128)(2,1)S(1)} %settle.1.own), channel_id=1, source_target_pairs={{0,1},{1,0},{2,3},{3,2},{4,5},{5,4},{6,7},{7,6},{8,9},{9,8},{10,11... | collective-permute-start | bytes 786440 | tf_op jit(solution)/shard_map/ppermute | solution.py:25
  39.4 0.3 own.1
  39.7 0.9 %collective-permute-done.3.other = bf16[256,512]{1,0:T(8,128)(2,1)S(1)} collective-permute-done((bf16[256,512]{1,0:T(8,128)(2,1)S(1)}, bf16[256,512]{1,0:T(8,128)(2,1)S(1)}, u32[]{:S(2)}, u32[]{:S(2)}) %collective-permute-start.3) | collective-permute-done | bytes 262176 | tf_op jit(solution)/shard_map/ppermute | solution.py:25
  40.6 0.3 other.1
  40.9 2.9 %collective-permute-start.4 = (bf16[128,512]{1,0:T(8,128)(2,1)S(1)}, bf16[128,512]{1,0:T(8,128)(2,1)S(1)}, u32[]{:S(2)}, u32[]{:S(2)}) collective-permute-start(bf16[128,512]{1,0:T(8,128)(2,1)S(1)} %get-tuple-element.28), channel_id=1, source_target_pairs={{0,8},{4,12},{8,0},{12,4},{1,9},{5,13},{9,1},{13,5},{2,10},{6,14},... | collective-permute-start | bytes 393224 | tf_op jit(solution)/shard_map/ppermute | solution.py:25
  43.8 0.6 %collective-permute-start.5 = (bf16[128,512]{1,0:T(8,128)(2,1)S(1)}, bf16[128,512]{1,0:T(8,128)(2,1)S(1)}, u32[]{:S(2)}, u32[]{:S(2)}) collective-permute-start(bf16[128,512]{1,0:T(8,128)(2,1)S(1)} %get-tuple-element.29), channel_id=1, source_target_pairs={{0,4},{4,8},{8,12},{12,0},{1,5},{5,9},{9,13},{13,1},{2,6},{6,10},{... | collective-permute-start | bytes 393224 | tf_op jit(solution)/shard_map/ppermute | solution.py:25
  44.4 2.1 %collective-permute-start.6 = (bf16[128,512]{1,0:T(8,128)(2,1)S(1)}, bf16[128,512]{1,0:T(8,128)(2,1)S(1)}, u32[]{:S(2)}, u32[]{:S(2)}) collective-permute-start(bf16[128,512]{1,0:T(8,128)(2,1)S(1)} %get-tuple-element.30), channel_id=1, source_target_pairs={{0,12},{4,0},{8,4},{12,8},{1,13},{5,1},{9,5},{13,9},{2,14},{6,2},{... | collective-permute-start | bytes 393224 | tf_op jit(solution)/shard_map/ppermute | solution.py:25
  46.5 0.7 %collective-permute-done.4.o1 = bf16[128,512]{1,0:T(8,128)(2,1)S(1)} collective-permute-done((bf16[128,512]{1,0:T(8,128)(2,1)S(1)}, bf16[128,512]{1,0:T(8,128)(2,1)S(1)}, u32[]{:S(2)}, u32[]{:S(2)}) %collective-permute-start.4) | collective-permute-done | bytes 131104 | tf_op jit(solution)/shard_map/ppermute | solution.py:25
  47.2 3.2 %collective-permute-done.5.o2 = bf16[128,512]{1,0:T(8,128)(2,1)S(1)} collective-permute-done((bf16[128,512]{1,0:T(8,128)(2,1)S(1)}, bf16[128,512]{1,0:T(8,128)(2,1)S(1)}, u32[]{:S(2)}, u32[]{:S(2)}) %collective-permute-start.5) | collective-permute-done | bytes 131104 | tf_op jit(solution)/shard_map/ppermute | solution.py:25
  50.3 0.1 collective-permute-done.6.o3
  50.5 0.7 %add.42 = bf16[128,512]{1,0:T(8,128)(2,1)} custom-call(f32[128,512]{1,0:T(8,128)S(1)} %get-tuple-element.27.o0, bf16[128,512]{1,0:T(8,128)(2,1)S(1)} %collective-permute-done.4.o1, bf16[128,512]{1,0:T(8,128)(2,1)S(1)} %collective-permute-done.5.o2, bf16[128,512]{1,0:T(8,128)(2,1)S(1)} %collective-permute-done.6.o3), custom_call_target="tpu_custom_call" | custom-call | tf_op jit(solution)/shard_map/add/pallas_call | solution.py:347
  (2 shorter events, 0.1 us)
Async XLA Ops:
  0.0 12.4 %copy-start.4 = (bf16[128,2048]{1,0:T(8,128)(2,1)S(1)}, bf16[128,2048]{1,0:T(8,128)(2,1)}, u32[]{:S(2)}) copy-start(bf16[128,2048]{1,0:T(8,128)(2,1)} %param.11) | copy-start | bytes 1572868
  2.6 15.0 %all-to-all-start = ((bf16[16,8,1152]{2,1,0:T(8,128)(2,1)}), bf16[16,8,1152]{2,1,0:T(8,128)(2,1)S(1)}, u32[]{:S(2)}, u32[]{:S(2)}) async-start(bf16[16,8,1152]{2,1,0:T(8,128)(2,1)} %pack.1), calls=%async_computation | async-start | bytes 589824 | tf_op jit(solution)/shard_map/all_to_all | solution.py:50
  12.4 4.6 %copy-start.1 = (f32[8,16]{1,0:T(8,128)S(1)}, f32[8,16]{1,0:T(8,128)}, u32[]{:S(2)}) copy-start(f32[8,16]{1,0:T(8,128)} %decay.1) | copy-start | bytes 1540
  12.4 4.6 %copy-start.2 = (f32[8,16]{1,0:T(8,128)S(1)}, f32[8,16]{1,0:T(8,128)}, u32[]{:S(2)}) copy-start(f32[8,16]{1,0:T(8,128)} %residue.1) | copy-start | bytes 1540
  12.5 4.5 %copy-start = (f32[3,128,3]{1,2,0:T(4,128)S(1)}, f32[3,128,3]{1,2,0:T(4,128)}, u32[]{:S(2)}) copy-start(f32[3,128,3]{1,2,0:T(4,128)} %param.7) | copy-start | bytes 13828
  12.5 6.1 %collective-permute-start = (bf16[128,512]{1,0:T(8,128)(2,1)S(1)}, bf16[128,512]{1,0:T(8,128)(2,1)S(1)}, u32[]{:S(2)}, u32[]{:S(2)}) collective-permute-start(bf16[128,512]{1,0:T(8,128)(2,1)S(1)} %get-tuple-element.33), channel_id=1, source_target_pairs={{0,8},{4,12},{8,0},{12,4},{1,9},{5,13},{9,1},{13,5},{2,10},{6,14},... | collective-permute-start | bytes 393224 | tf_op jit(solution)/shard_map/ppermute | solution.py:25
  15.5 5.4 %collective-permute-start.1 = (bf16[128,512]{1,0:T(8,128)(2,1)S(1)}, bf16[128,512]{1,0:T(8,128)(2,1)S(1)}, u32[]{:S(2)}, u32[]{:S(2)}) collective-permute-start(bf16[128,512]{1,0:T(8,128)(2,1)S(1)} %get-tuple-element.32), channel_id=1, source_target_pairs={{0,12},{4,0},{8,4},{12,8},{1,13},{5,1},{9,5},{13,9},{2,14},{6,2},{... | collective-permute-start | bytes 393224 | tf_op jit(solution)/shard_map/ppermute | solution.py:25
  16.3 0.7 %copy-start.3 = (f32[128]{0:T(128)S(1)}, f32[128]{0:T(128)}, u32[]{:S(2)}) copy-start(f32[128]{0:T(128)} %param.10) | copy-start | bytes 1540
  16.3 5.4 %collective-permute-start.2 = (bf16[128,512]{1,0:T(8,128)(2,1)S(1)}, bf16[128,512]{1,0:T(8,128)(2,1)S(1)}, u32[]{:S(2)}, u32[]{:S(2)}) collective-permute-start(bf16[128,512]{1,0:T(8,128)(2,1)S(1)} %get-tuple-element.34), channel_id=1, source_target_pairs={{0,4},{4,8},{8,12},{12,0},{1,5},{5,9},{9,13},{13,1},{2,6},{6,10},{... | collective-permute-start | bytes 393224 | tf_op jit(solution)/shard_map/ppermute | solution.py:25
  35.9 4.7 %collective-permute-start.3 = (bf16[256,512]{1,0:T(8,128)(2,1)S(1)}, bf16[256,512]{1,0:T(8,128)(2,1)S(1)}, u32[]{:S(2)}, u32[]{:S(2)}) collective-permute-start(bf16[256,512]{1,0:T(8,128)(2,1)S(1)} %settle.1.own), channel_id=1, source_target_pairs={{0,1},{1,0},{2,3},{3,2},{4,5},{5,4},{6,7},{7,6},{8,9},{9,8},{10,11... | collective-permute-start | bytes 786440 | tf_op jit(solution)/shard_map/ppermute | solution.py:25
  40.9 6.3 %collective-permute-start.4 = (bf16[128,512]{1,0:T(8,128)(2,1)S(1)}, bf16[128,512]{1,0:T(8,128)(2,1)S(1)}, u32[]{:S(2)}, u32[]{:S(2)}) collective-permute-start(bf16[128,512]{1,0:T(8,128)(2,1)S(1)} %get-tuple-element.28), channel_id=1, source_target_pairs={{0,8},{4,12},{8,0},{12,4},{1,9},{5,13},{9,1},{13,5},{2,10},{6,14},... | collective-permute-start | bytes 393224 | tf_op jit(solution)/shard_map/ppermute | solution.py:25
  43.8 6.6 %collective-permute-start.5 = (bf16[128,512]{1,0:T(8,128)(2,1)S(1)}, bf16[128,512]{1,0:T(8,128)(2,1)S(1)}, u32[]{:S(2)}, u32[]{:S(2)}) collective-permute-start(bf16[128,512]{1,0:T(8,128)(2,1)S(1)} %get-tuple-element.29), channel_id=1, source_target_pairs={{0,4},{4,8},{8,12},{12,0},{1,5},{5,9},{9,13},{13,1},{2,6},{6,10},{... | collective-permute-start | bytes 393224 | tf_op jit(solution)/shard_map/ppermute | solution.py:25
  44.4 6.1 %collective-permute-start.6 = (bf16[128,512]{1,0:T(8,128)(2,1)S(1)}, bf16[128,512]{1,0:T(8,128)(2,1)S(1)}, u32[]{:S(2)}, u32[]{:S(2)}) collective-permute-start(bf16[128,512]{1,0:T(8,128)(2,1)S(1)} %get-tuple-element.30), channel_id=1, source_target_pairs={{0,12},{4,0},{8,4},{12,8},{1,13},{5,1},{9,5},{13,9},{2,14},{6,2},{... | collective-permute-start | bytes 393224 | tf_op jit(solution)/shard_map/ppermute | solution.py:25

commit v6 on v5

--- a/solution.py
+++ b/solution.py
@@ -12,7 +12,7 @@
 BACK = ("zl", "x", "zh")
 LANES = 128
 TAPS = 3
-TURN = {16: (8, 4), 32: (20, 4)}
+TURN = {16: (8, 4), 32: (20, 12)}
 ORDER = (2, 1, 3)
 WAIT = 20_000_000_000
 f32 = jnp.float32

time: 51.4 us -> 51.1 us (level)
  transfers between devices with their start and end apart: 8 -> 8, of which waited for: 6 -> 5; matrix products, arithmetic and copies ran while one was open for 0% -> 0% of each run, Pallas kernels for 4% -> 4%
where the time goes in v6:
time: 51.1 us; the launch traced here: 50.9 us
  starting transfers between devices  23.4 us (46%)
  blocking collectives  13.8 us (27%)
  waiting for transfers between devices  8.02 us (16%)
  Pallas kernels  5.56 us (11%)
    all_to_all x1, blocking collectives, exchange(): lax.all_to_all(value, order + ('c',), 0, 0, axis_index_groups=groups, til...  13.8 us
    ppermute x7, starting transfers between devices, shift(): lax.ppermute(value, axis, [(i, (i + steps) % count) for i in range(count)])  13.6 us
    all_to_all x1, starting transfers between devices, exchange(): lax.all_to_all(value, order + ('c',), 0, 0, axis_index_groups=groups, til...  9.8 us
    ppermute x7, waiting for transfers between devices, shift(): lax.ppermute(value, axis, [(i, (i + steps) % count) for i in range(count)])  8.02 us
    pallas_call x1, Pallas kernels, local(): pl.pallas_call(pack_body, out_shape=pltpu.VMEM((shards, owned, 2 * tokens...  2.58 us
  transfers between devices with their start and end apart: 8, of which 5 were waited for; matrix products, arithmetic and copies ran while one was open for 0% of the time, Pallas kernels for 4%

profile of v6, /device:TPU:1, one launch (start us, length us, event | category | flops | bytes accessed | tf_op | source)
XLA Modules:
  0.0 50.9 jit_solution(16712053209166093850)
XLA Ops:
  0.0 0.0 copy-start.4
  0.0 2.6 %pack.1 = bf16[16,8,1152]{2,1,0:T(8,128)(2,1)} custom-call(bf16[3,128,512]{2,1,0:T(8,128)(2,1)} %features_hbm.1, f32[3,3,128]{2,1,0:T(4,128)} %bitcast.3), custom_call_target="tpu_custom_call" | custom-call | tf_op jit(solution)/shard_map/pack/pallas_call | solution.py:258
  2.6 9.8 %all-to-all-start = ((bf16[16,8,1152]{2,1,0:T(8,128)(2,1)}), bf16[16,8,1152]{2,1,0:T(8,128)(2,1)S(1)}, u32[]{:S(2)}, u32[]{:S(2)}) async-start(bf16[16,8,1152]{2,1,0:T(8,128)(2,1)} %pack.1), calls=%async_computation | async-start | bytes 589824 | tf_op jit(solution)/shard_map/all_to_all | solution.py:50
  12.4 0.0 copy-done.4
  12.4 0.0 copy-start.1
  12.4 0.0 copy-start.2
  12.5 0.0 copy-start
  12.5 3.0 %collective-permute-start = (bf16[128,512]{1,0:T(8,128)(2,1)S(1)}, bf16[128,512]{1,0:T(8,128)(2,1)S(1)}, u32[]{:S(2)}, u32[]{:S(2)}) collective-permute-start(bf16[128,512]{1,0:T(8,128)(2,1)S(1)} %get-tuple-element.33), channel_id=1, source_target_pairs={{0,8},{4,12},{8,0},{12,4},{1,9},{5,13},{9,1},{13,5},{2,10},{6,14},... | collective-permute-start | bytes 393224 | tf_op jit(solution)/shard_map/ppermute | solution.py:25
  15.5 0.8 %collective-permute-start.1 = (bf16[128,512]{1,0:T(8,128)(2,1)S(1)}, bf16[128,512]{1,0:T(8,128)(2,1)S(1)}, u32[]{:S(2)}, u32[]{:S(2)}) collective-permute-start(bf16[128,512]{1,0:T(8,128)(2,1)S(1)} %get-tuple-element.32), channel_id=1, source_target_pairs={{0,12},{4,0},{8,4},{12,8},{1,13},{5,1},{9,5},{13,9},{2,14},{6,2},{... | collective-permute-start | bytes 393224 | tf_op jit(solution)/shard_map/ppermute | solution.py:25
  16.3 0.0 copy-start.3
  16.3 0.7 %collective-permute-start.2 = (bf16[128,512]{1,0:T(8,128)(2,1)S(1)}, bf16[128,512]{1,0:T(8,128)(2,1)S(1)}, u32[]{:S(2)}, u32[]{:S(2)}) collective-permute-start(bf16[128,512]{1,0:T(8,128)(2,1)S(1)} %get-tuple-element.34), channel_id=1, source_target_pairs={{0,4},{4,8},{8,12},{12,0},{1,5},{5,9},{9,13},{13,1},{2,6},{6,10},{... | collective-permute-start | bytes 393224 | tf_op jit(solution)/shard_map/ppermute | solution.py:25
  17.0 0.0 copy-done.1
  17.0 0.0 copy-done.2
  17.0 0.0 copy-done
  17.0 0.0 copy-done.3
  17.0 0.6 %prep.1 = (bf16[8,256,128]{2,1,0:T(8,128)(2,1)S(1)}, bf16[1024,256]{1,0:T(8,128)(2,1)S(1)}, bf16[384,1024]{1,0:T(8,128)(2,1)S(1)}, f32[8,128]{1,0:T(8,128)S(1)}, f32[9,8,128]{2,1,0:T(8,128)S(1)}) custom-call(f32[8,16]{1,0:T(8,128)S(1)} %copy-done.1, f32[8,16]{1,0:T(8,128)S(1)} %copy-done.2, f32[1,128]{1,0:T(1,128)S(1)} %bitcast.5, f32[3,3,128]{2,1,0:T(4,128)S(1)} %bitcast.4), custom_call_target="tpu_custom_call" | custom-call | flops 2000000 | bytes 1600000 | tf_op jit(solution)/shard_map/prep/pallas_call | solution.py:281
  17.6 0.0 all-to-all-done.held
  17.6 1.0 %conv.1.gated = bf16[32,8,512]{2,1,0:T(8,128)(2,1)S(1)} custom-call(bf16[16,8,1152]{2,1,0:T(8,128)(2,1)S(1)} %all-to-all-done.held, f32[9,8,128]{2,1,0:T(8,128)S(1)} %get-tuple-element.18.taps, bf16[8,256,128]{2,1,0:T(8,128)(2,1)S(1)} %get-tuple-element.19.toeplitz, bf16[1024,256]{1,0:T(8,128)(2,1)S(1)} %get-tuple-element.20.enter, ...), custom_call_target="tpu_custom_call" | custom-call | flops 20000000000 | bytes 2500000 | tf_op jit(solution)/shard_map/conv/pallas_call | solution.py:297
  18.6 0.0 collective-permute-done.w1.w2
  18.6 2.3 %collective-permute-done.1.w2.w1 = bf16[128,512]{1,0:T(8,128)(2,1)S(1)} collective-permute-done((bf16[128,512]{1,0:T(8,128)(2,1)S(1)}, bf16[128,512]{1,0:T(8,128)(2,1)S(1)}, u32[]{:S(2)}, u32[]{:S(2)}) %collective-permute-start.1) | collective-permute-done | bytes 131104 | tf_op jit(solution)/shard_map/ppermute | solution.py:25
  20.9 0.7 %collective-permute-done.2.w3 = bf16[128,512]{1,0:T(8,128)(2,1)S(1)} collective-permute-done((bf16[128,512]{1,0:T(8,128)(2,1)S(1)}, bf16[128,512]{1,0:T(8,128)(2,1)S(1)}, u32[]{:S(2)}, u32[]{:S(2)}) %collective-permute-start.2) | collective-permute-done | bytes 131104 | tf_op jit(solution)/shard_map/ppermute | solution.py:25
  21.7 13.8 %all_to_all.10.gated = bf16[32,8,512]{2,1,0:T(8,128)(2,1)S(1)} all-to-all(bf16[32,8,512]{2,1,0:T(8,128)(2,1)S(1)} %hold.1), channel_id=1, replica_groups={{82,80,18,16,194,192,130,128,66,64,2,0,242,240,178,176,114,112,50,48,22..., dimensions={0} | all-to-all | bytes 524288 | tf_op jit(solution)/shard_map/all_to_all | solution.py:50
  35.5 0.1 settle.1.own
  35.5 3.7 %collective-permute-start.3 = (bf16[256,512]{1,0:T(8,128)(2,1)S(1)}, bf16[256,512]{1,0:T(8,128)(2,1)S(1)}, u32[]{:S(2)}, u32[]{:S(2)}) collective-permute-start(bf16[256,512]{1,0:T(8,128)(2,1)S(1)} %settle.1.own), channel_id=1, source_target_pairs={{0,1},{1,0},{2,3},{3,2},{4,5},{5,4},{6,7},{7,6},{8,9},{9,8},{10,11... | collective-permute-start | bytes 786440 | tf_op jit(solution)/shard_map/ppermute | solution.py:25
  39.2 0.3 own.1
  39.5 0.9 %collective-permute-done.3.other = bf16[256,512]{1,0:T(8,128)(2,1)S(1)} collective-permute-done((bf16[256,512]{1,0:T(8,128)(2,1)S(1)}, bf16[256,512]{1,0:T(8,128)(2,1)S(1)}, u32[]{:S(2)}, u32[]{:S(2)}) %collective-permute-start.3) | collective-permute-done | bytes 262176 | tf_op jit(solution)/shard_map/ppermute | solution.py:25
  40.4 0.3 other.1
  40.7 2.8 %collective-permute-start.4 = (bf16[128,512]{1,0:T(8,128)(2,1)S(1)}, bf16[128,512]{1,0:T(8,128)(2,1)S(1)}, u32[]{:S(2)}, u32[]{:S(2)}) collective-permute-start(bf16[128,512]{1,0:T(8,128)(2,1)S(1)} %get-tuple-element.28), channel_id=1, source_target_pairs={{0,8},{4,12},{8,0},{12,4},{1,9},{5,13},{9,1},{13,5},{2,10},{6,14},... | collective-permute-start | bytes 393224 | tf_op jit(solution)/shard_map/ppermute | solution.py:25
  43.4 0.6 %collective-permute-start.5 = (bf16[128,512]{1,0:T(8,128)(2,1)S(1)}, bf16[128,512]{1,0:T(8,128)(2,1)S(1)}, u32[]{:S(2)}, u32[]{:S(2)}) collective-permute-start(bf16[128,512]{1,0:T(8,128)(2,1)S(1)} %get-tuple-element.29), channel_id=1, source_target_pairs={{0,4},{4,8},{8,12},{12,0},{1,5},{5,9},{9,13},{13,1},{2,6},{6,10},{... | collective-permute-start | bytes 393224 | tf_op jit(solution)/shard_map/ppermute | solution.py:25
  44.0 2.1 %collective-permute-start.6 = (bf16[128,512]{1,0:T(8,128)(2,1)S(1)}, bf16[128,512]{1,0:T(8,128)(2,1)S(1)}, u32[]{:S(2)}, u32[]{:S(2)}) collective-permute-start(bf16[128,512]{1,0:T(8,128)(2,1)S(1)} %get-tuple-element.30), channel_id=1, source_target_pairs={{0,12},{4,0},{8,4},{12,8},{1,13},{5,1},{9,5},{13,9},{2,14},{6,2},{... | collective-permute-start | bytes 393224 | tf_op jit(solution)/shard_map/ppermute | solution.py:25
  46.1 0.8 %collective-permute-done.4.o1 = bf16[128,512]{1,0:T(8,128)(2,1)S(1)} collective-permute-done((bf16[128,512]{1,0:T(8,128)(2,1)S(1)}, bf16[128,512]{1,0:T(8,128)(2,1)S(1)}, u32[]{:S(2)}, u32[]{:S(2)}) %collective-permute-start.4) | collective-permute-done | bytes 131104 | tf_op jit(solution)/shard_map/ppermute | solution.py:25
  47.0 3.2 %collective-permute-done.5.o2 = bf16[128,512]{1,0:T(8,128)(2,1)S(1)} collective-permute-done((bf16[128,512]{1,0:T(8,128)(2,1)S(1)}, bf16[128,512]{1,0:T(8,128)(2,1)S(1)}, u32[]{:S(2)}, u32[]{:S(2)}) %collective-permute-start.5) | collective-permute-done | bytes 131104 | tf_op jit(solution)/shard_map/ppermute | solution.py:25
  50.2 0.0 collective-permute-done.6.o3
  50.2 0.7 %add.42 = bf16[128,512]{1,0:T(8,128)(2,1)} custom-call(f32[128,512]{1,0:T(8,128)S(1)} %get-tuple-element.27.o0, bf16[128,512]{1,0:T(8,128)(2,1)S(1)} %collective-permute-done.4.o1, bf16[128,512]{1,0:T(8,128)(2,1)S(1)} %collective-permute-done.5.o2, bf16[128,512]{1,0:T(8,128)(2,1)S(1)} %collective-permute-done.6.o3), custom_call_target="tpu_custom_call" | custom-call | tf_op jit(solution)/shard_map/add/pallas_call | solution.py:347
  (2 shorter events, 0.1 us)
Async XLA Ops:
  0.0 12.4 %copy-start.4 = (bf16[128,2048]{1,0:T(8,128)(2,1)S(1)}, bf16[128,2048]{1,0:T(8,128)(2,1)}, u32[]{:S(2)}) copy-start(bf16[128,2048]{1,0:T(8,128)(2,1)} %param.11) | copy-start | bytes 1572868
  2.6 15.0 %all-to-all-start = ((bf16[16,8,1152]{2,1,0:T(8,128)(2,1)}), bf16[16,8,1152]{2,1,0:T(8,128)(2,1)S(1)}, u32[]{:S(2)}, u32[]{:S(2)}) async-start(bf16[16,8,1152]{2,1,0:T(8,128)(2,1)} %pack.1), calls=%async_computation | async-start | bytes 589824 | tf_op jit(solution)/shard_map/all_to_all | solution.py:50
  12.4 4.6 %copy-start.1 = (f32[8,16]{1,0:T(8,128)S(1)}, f32[8,16]{1,0:T(8,128)}, u32[]{:S(2)}) copy-start(f32[8,16]{1,0:T(8,128)} %decay.1) | copy-start | bytes 1540
  12.4 4.6 %copy-start.2 = (f32[8,16]{1,0:T(8,128)S(1)}, f32[8,16]{1,0:T(8,128)}, u32[]{:S(2)}) copy-start(f32[8,16]{1,0:T(8,128)} %residue.1) | copy-start | bytes 1540
  12.5 4.5 %copy-start = (f32[3,128,3]{1,2,0:T(4,128)S(1)}, f32[3,128,3]{1,2,0:T(4,128)}, u32[]{:S(2)}) copy-start(f32[3,128,3]{1,2,0:T(4,128)} %param.7) | copy-start | bytes 13828
  12.5 6.1 %collective-permute-start = (bf16[128,512]{1,0:T(8,128)(2,1)S(1)}, bf16[128,512]{1,0:T(8,128)(2,1)S(1)}, u32[]{:S(2)}, u32[]{:S(2)}) collective-permute-start(bf16[128,512]{1,0:T(8,128)(2,1)S(1)} %get-tuple-element.33), channel_id=1, source_target_pairs={{0,8},{4,12},{8,0},{12,4},{1,9},{5,13},{9,1},{13,5},{2,10},{6,14},... | collective-permute-start | bytes 393224 | tf_op jit(solution)/shard_map/ppermute | solution.py:25
  15.5 5.4 %collective-permute-start.1 = (bf16[128,512]{1,0:T(8,128)(2,1)S(1)}, bf16[128,512]{1,0:T(8,128)(2,1)S(1)}, u32[]{:S(2)}, u32[]{:S(2)}) collective-permute-start(bf16[128,512]{1,0:T(8,128)(2,1)S(1)} %get-tuple-element.32), channel_id=1, source_target_pairs={{0,12},{4,0},{8,4},{12,8},{1,13},{5,1},{9,5},{13,9},{2,14},{6,2},{... | collective-permute-start | bytes 393224 | tf_op jit(solution)/shard_map/ppermute | solution.py:25
  16.3 0.7 %copy-start.3 = (f32[128]{0:T(128)S(1)}, f32[128]{0:T(128)}, u32[]{:S(2)}) copy-start(f32[128]{0:T(128)} %param.10) | copy-start | bytes 1540
  16.3 5.4 %collective-permute-start.2 = (bf16[128,512]{1,0:T(8,128)(2,1)S(1)}, bf16[128,512]{1,0:T(8,128)(2,1)S(1)}, u32[]{:S(2)}, u32[]{:S(2)}) collective-permute-start(bf16[128,512]{1,0:T(8,128)(2,1)S(1)} %get-tuple-element.34), channel_id=1, source_target_pairs={{0,4},{4,8},{8,12},{12,0},{1,5},{5,9},{9,13},{13,1},{2,6},{6,10},{... | collective-permute-start | bytes 393224 | tf_op jit(solution)/shard_map/ppermute | solution.py:25
  35.5 4.8 %collective-permute-start.3 = (bf16[256,512]{1,0:T(8,128)(2,1)S(1)}, bf16[256,512]{1,0:T(8,128)(2,1)S(1)}, u32[]{:S(2)}, u32[]{:S(2)}) collective-permute-start(bf16[256,512]{1,0:T(8,128)(2,1)S(1)} %settle.1.own), channel_id=1, source_target_pairs={{0,1},{1,0},{2,3},{3,2},{4,5},{5,4},{6,7},{7,6},{8,9},{9,8},{10,11... | collective-permute-start | bytes 786440 | tf_op jit(solution)/shard_map/ppermute | solution.py:25
  40.7 6.3 %collective-permute-start.4 = (bf16[128,512]{1,0:T(8,128)(2,1)S(1)}, bf16[128,512]{1,0:T(8,128)(2,1)S(1)}, u32[]{:S(2)}, u32[]{:S(2)}) collective-permute-start(bf16[128,512]{1,0:T(8,128)(2,1)S(1)} %get-tuple-element.28), channel_id=1, source_target_pairs={{0,8},{4,12},{8,0},{12,4},{1,9},{5,13},{9,1},{13,5},{2,10},{6,14},... | collective-permute-start | bytes 393224 | tf_op jit(solution)/shard_map/ppermute | solution.py:25
  43.4 6.8 %collective-permute-start.5 = (bf16[128,512]{1,0:T(8,128)(2,1)S(1)}, bf16[128,512]{1,0:T(8,128)(2,1)S(1)}, u32[]{:S(2)}, u32[]{:S(2)}) collective-permute-start(bf16[128,512]{1,0:T(8,128)(2,1)S(1)} %get-tuple-element.29), channel_id=1, source_target_pairs={{0,4},{4,8},{8,12},{12,0},{1,5},{5,9},{9,13},{13,1},{2,6},{6,10},{... | collective-permute-start | bytes 393224 | tf_op jit(solution)/shard_map/ppermute | solution.py:25
  44.0 6.2 %collective-permute-start.6 = (bf16[128,512]{1,0:T(8,128)(2,1)S(1)}, bf16[128,512]{1,0:T(8,128)(2,1)S(1)}, u32[]{:S(2)}, u32[]{:S(2)}) collective-permute-start(bf16[128,512]{1,0:T(8,128)(2,1)S(1)} %get-tuple-element.30), channel_id=1, source_target_pairs={{0,12},{4,0},{8,4},{12,8},{1,13},{5,1},{9,5},{13,9},{2,14},{6,2},{... | collective-permute-start | bytes 393224 | tf_op jit(solution)/shard_map/ppermute | solution.py:25

commit v7 on v6

--- a/solution.py
+++ b/solution.py
@@ -235,11 +235,17 @@
         o[...] = dot(jnp.concatenate(columns_of(w, core[0], half), axis=1), own[...])
 
 
-def other_body(core, other, w0, w1, w2, w3, a0, a1, a2, a3, o0, o1, o2, o3):
+def other_body(core, other, w1, w2, w3, a1, a2, a3, o1, o2, o3):
     half = other.shape[0] // 2
-    for w, a, o in ((w2, a2, o2), (w1, a1, o1), (w3, a3, o3), (w0, a0, o0)):
+    for w, a, o in ((w2, a2, o2), (w1, a1, o1), (w3, a3, o3)):
         term = dot(jnp.concatenate(columns_of(w, 1 - core[0], half), axis=1), other[...])
         o[...] = (a[...] + term).astype(o.dtype)
+
+
+def home_body(core, other, w0, a0, o0):
+    half = other.shape[0] // 2
+    term = dot(jnp.concatenate(columns_of(w0, 1 - core[0], half), axis=1), other[...])
+    o0[...] = a0[...] + term
 
 
 def add_body(o0, o1, o2, o3, out):
@@ -336,13 +342,23 @@
     )(one, near(gated), *close)
     parts = pl.pallas_call(
         other_body,
-        out_shape=(pltpu.VMEM((rows, tokens), f32),) + (pltpu.VMEM((rows, tokens), bf16),) * 3,
-        in_specs=[pl.BlockSpec(memory_space=pltpu.SMEM)] + [in_vmem] * 9,
-        out_specs=(in_vmem,) * 4,
-        cost_estimate=pl.CostEstimate(flops=150000000, bytes_accessed=1500000, transcendentals=0),
+        out_shape=(pltpu.VMEM((rows, tokens), bf16),) * 3,
+        in_specs=[pl.BlockSpec(memory_space=pltpu.SMEM)] + [in_vmem] * 7,
+        out_specs=(in_vmem,) * 3,
+        cost_estimate=pl.CostEstimate(flops=110000000, bytes_accessed=1500000, transcendentals=0),
         compiler_params=params(),
         name="other",
-    )(one, near(other), *close, *map(near, sums))
+    )(one, near(other), *close[1:], *map(near, sums[1:]))
+    home = pl.pallas_call(
+        home_body,
+        out_shape=pltpu.VMEM((rows, tokens), f32),
+        in_specs=[pl.BlockSpec(memory_space=pltpu.SMEM)] + [in_vmem] * 3,
+        out_specs=in_vmem,
+        cost_estimate=pl.CostEstimate(flops=40000000, bytes_accessed=500000, transcendentals=0),
+        compiler_params=params(),
+        name="home",
+    )(one, near(other), close[0], near(sums[0]))
+    parts = (home,) + tuple(parts)
     arrived = [parts[0]] + [shift(parts[d], "y", d) for d in (2, 1, 3)]
     return pl.pallas_call(
         add_body,

time: 51.1 us -> 51.1 us (level)
  no operation moved by 1% of the time
where the time goes in v7:
time: 51.1 us; the launch traced here: 50.9 us
  starting transfers between devices  23.4 us (46%)
  blocking collectives  13.8 us (27%)
  waiting for transfers between devices  7.84 us (15%)
  Pallas kernels  5.72 us (11%)
    all_to_all x1, blocking collectives, exchange(): lax.all_to_all(value, order + ('c',), 0, 0, axis_index_groups=groups, til...  13.8 us
    ppermute x7, starting transfers between devices, shift(): lax.ppermute(value, axis, [(i, (i + steps) % count) for i in range(count)])  13.6 us
    all_to_all x1, starting transfers between devices, exchange(): lax.all_to_all(value, order + ('c',), 0, 0, axis_index_groups=groups, til...  9.8 us
    ppermute x7, waiting for transfers between devices, shift(): lax.ppermute(value, axis, [(i, (i + steps) % count) for i in range(count)])  7.83 us
    pallas_call x1, Pallas kernels, local(): pl.pallas_call(pack_body, out_shape=pltpu.VMEM((shards, owned, 2 * tokens...  2.58 us
  transfers between devices with their start and end apart: 8, of which 5 were waited for; matrix products, arithmetic and copies ran while one was open for 0% of the time, Pallas kernels for 4%

profile of v7, /device:TPU:1, one launch (start us, length us, event | category | flops | bytes accessed | tf_op | source)
XLA Modules:
  0.0 50.9 jit_solution(602756104070713205)
XLA Ops:
  0.0 0.0 copy-start.4
  0.0 2.6 %pack.1 = bf16[16,8,1152]{2,1,0:T(8,128)(2,1)} custom-call(bf16[3,128,512]{2,1,0:T(8,128)(2,1)} %features_hbm.1, f32[3,3,128]{2,1,0:T(4,128)} %bitcast.3), custom_call_target="tpu_custom_call" | custom-call | tf_op jit(solution)/shard_map/pack/pallas_call | solution.py:264
  2.6 9.8 %all-to-all-start = ((bf16[16,8,1152]{2,1,0:T(8,128)(2,1)}), bf16[16,8,1152]{2,1,0:T(8,128)(2,1)S(1)}, u32[]{:S(2)}, u32[]{:S(2)}) async-start(bf16[16,8,1152]{2,1,0:T(8,128)(2,1)} %pack.1), calls=%async_computation | async-start | bytes 589824 | tf_op jit(solution)/shard_map/all_to_all | solution.py:50
  12.4 0.0 copy-done.4
  12.4 0.0 copy-start.1
  12.4 0.0 copy-start.2
  12.5 0.0 copy-start
  12.5 3.0 %collective-permute-start = (bf16[128,512]{1,0:T(8,128)(2,1)S(1)}, bf16[128,512]{1,0:T(8,128)(2,1)S(1)}, u32[]{:S(2)}, u32[]{:S(2)}) collective-permute-start(bf16[128,512]{1,0:T(8,128)(2,1)S(1)} %get-tuple-element.31), channel_id=1, source_target_pairs={{0,8},{4,12},{8,0},{12,4},{1,9},{5,13},{9,1},{13,5},{2,10},{6,14},... | collective-permute-start | bytes 393224 | tf_op jit(solution)/shard_map/ppermute | solution.py:25
  15.5 0.8 %collective-permute-start.1 = (bf16[128,512]{1,0:T(8,128)(2,1)S(1)}, bf16[128,512]{1,0:T(8,128)(2,1)S(1)}, u32[]{:S(2)}, u32[]{:S(2)}) collective-permute-start(bf16[128,512]{1,0:T(8,128)(2,1)S(1)} %get-tuple-element.30), channel_id=1, source_target_pairs={{0,12},{4,0},{8,4},{12,8},{1,13},{5,1},{9,5},{13,9},{2,14},{6,2},{... | collective-permute-start | bytes 393224 | tf_op jit(solution)/shard_map/ppermute | solution.py:25
  16.3 0.0 copy-start.3
  16.3 0.7 %collective-permute-start.2 = (bf16[128,512]{1,0:T(8,128)(2,1)S(1)}, bf16[128,512]{1,0:T(8,128)(2,1)S(1)}, u32[]{:S(2)}, u32[]{:S(2)}) collective-permute-start(bf16[128,512]{1,0:T(8,128)(2,1)S(1)} %get-tuple-element.32), channel_id=1, source_target_pairs={{0,4},{4,8},{8,12},{12,0},{1,5},{5,9},{9,13},{13,1},{2,6},{6,10},{... | collective-permute-start | bytes 393224 | tf_op jit(solution)/shard_map/ppermute | solution.py:25
  17.0 0.0 copy-done.1
  17.0 0.0 copy-done.2
  17.0 0.0 copy-done
  17.0 0.0 copy-done.3
  17.0 0.6 %prep.1 = (bf16[8,256,128]{2,1,0:T(8,128)(2,1)S(1)}, bf16[1024,256]{1,0:T(8,128)(2,1)S(1)}, bf16[384,1024]{1,0:T(8,128)(2,1)S(1)}, f32[8,128]{1,0:T(8,128)S(1)}, f32[9,8,128]{2,1,0:T(8,128)S(1)}) custom-call(f32[8,16]{1,0:T(8,128)S(1)} %copy-done.1, f32[8,16]{1,0:T(8,128)S(1)} %copy-done.2, f32[1,128]{1,0:T(1,128)S(1)} %bitcast.5, f32[3,3,128]{2,1,0:T(4,128)S(1)} %bitcast.4), custom_call_target="tpu_custom_call" | custom-call | flops 2000000 | bytes 1600000 | tf_op jit(solution)/shard_map/prep/pallas_call | solution.py:287
  17.6 0.0 all-to-all-done.held
  17.6 1.0 %conv.1.gated = bf16[32,8,512]{2,1,0:T(8,128)(2,1)S(1)} custom-call(bf16[16,8,1152]{2,1,0:T(8,128)(2,1)S(1)} %all-to-all-done.held, f32[9,8,128]{2,1,0:T(8,128)S(1)} %get-tuple-element.17.taps, bf16[8,256,128]{2,1,0:T(8,128)(2,1)S(1)} %get-tuple-element.18.toeplitz, bf16[1024,256]{1,0:T(8,128)(2,1)S(1)} %get-tuple-element.19.enter, ...), custom_call_target="tpu_custom_call" | custom-call | flops 20000000000 | bytes 2500000 | tf_op jit(solution)/shard_map/conv/pallas_call | solution.py:303
  18.6 0.0 collective-permute-done.w1.w2
  18.6 2.3 %collective-permute-done.1.w2.w1 = bf16[128,512]{1,0:T(8,128)(2,1)S(1)} collective-permute-done((bf16[128,512]{1,0:T(8,128)(2,1)S(1)}, bf16[128,512]{1,0:T(8,128)(2,1)S(1)}, u32[]{:S(2)}, u32[]{:S(2)}) %collective-permute-start.1) | collective-permute-done | bytes 131104 | tf_op jit(solution)/shard_map/ppermute | solution.py:25
  20.9 0.7 %collective-permute-done.2.w3 = bf16[128,512]{1,0:T(8,128)(2,1)S(1)} collective-permute-done((bf16[128,512]{1,0:T(8,128)(2,1)S(1)}, bf16[128,512]{1,0:T(8,128)(2,1)S(1)}, u32[]{:S(2)}, u32[]{:S(2)}) %collective-permute-start.2) | collective-permute-done | bytes 131104 | tf_op jit(solution)/shard_map/ppermute | solution.py:25
  21.7 13.8 %all_to_all.10.gated = bf16[32,8,512]{2,1,0:T(8,128)(2,1)S(1)} all-to-all(bf16[32,8,512]{2,1,0:T(8,128)(2,1)S(1)} %hold.1), channel_id=1, replica_groups={{82,80,18,16,194,192,130,128,66,64,2,0,242,240,178,176,114,112,50,48,22..., dimensions={0} | all-to-all | bytes 524288 | tf_op jit(solution)/shard_map/all_to_all | solution.py:50
  35.5 0.1 settle.1.own
  35.5 3.7 %collective-permute-start.3 = (bf16[256,512]{1,0:T(8,128)(2,1)S(1)}, bf16[256,512]{1,0:T(8,128)(2,1)S(1)}, u32[]{:S(2)}, u32[]{:S(2)}) collective-permute-start(bf16[256,512]{1,0:T(8,128)(2,1)S(1)} %settle.1.own), channel_id=1, source_target_pairs={{0,1},{1,0},{2,3},{3,2},{4,5},{5,4},{6,7},{7,6},{8,9},{9,8},{10,11... | collective-permute-start | bytes 786440 | tf_op jit(solution)/shard_map/ppermute | solution.py:25
  39.2 0.3 own.1
  39.5 0.9 %collective-permute-done.3.other = bf16[256,512]{1,0:T(8,128)(2,1)S(1)} collective-permute-done((bf16[256,512]{1,0:T(8,128)(2,1)S(1)}, bf16[256,512]{1,0:T(8,128)(2,1)S(1)}, u32[]{:S(2)}, u32[]{:S(2)}) %collective-permute-start.3) | collective-permute-done | bytes 262176 | tf_op jit(solution)/shard_map/ppermute | solution.py:25
  40.4 0.3 other.1
  40.6 2.8 %collective-permute-start.4 = (bf16[128,512]{1,0:T(8,128)(2,1)S(1)}, bf16[128,512]{1,0:T(8,128)(2,1)S(1)}, u32[]{:S(2)}, u32[]{:S(2)}) collective-permute-start(bf16[128,512]{1,0:T(8,128)(2,1)S(1)} %get-tuple-element.26), channel_id=1, source_target_pairs={{0,8},{4,12},{8,0},{12,4},{1,9},{5,13},{9,1},{13,5},{2,10},{6,14},... | collective-permute-start | bytes 393224 | tf_op jit(solution)/shard_map/ppermute | solution.py:25
  43.4 0.6 %collective-permute-start.5 = (bf16[128,512]{1,0:T(8,128)(2,1)S(1)}, bf16[128,512]{1,0:T(8,128)(2,1)S(1)}, u32[]{:S(2)}, u32[]{:S(2)}) collective-permute-start(bf16[128,512]{1,0:T(8,128)(2,1)S(1)} %get-tuple-element.27), channel_id=1, source_target_pairs={{0,4},{4,8},{8,12},{12,0},{1,5},{5,9},{9,13},{13,1},{2,6},{6,10},{... | collective-permute-start | bytes 393224 | tf_op jit(solution)/shard_map/ppermute | solution.py:25
  44.0 2.1 %collective-permute-start.6 = (bf16[128,512]{1,0:T(8,128)(2,1)S(1)}, bf16[128,512]{1,0:T(8,128)(2,1)S(1)}, u32[]{:S(2)}, u32[]{:S(2)}) collective-permute-start(bf16[128,512]{1,0:T(8,128)(2,1)S(1)} %get-tuple-element.28), channel_id=1, source_target_pairs={{0,12},{4,0},{8,4},{12,8},{1,13},{5,1},{9,5},{13,9},{2,14},{6,2},{... | collective-permute-start | bytes 393224 | tf_op jit(solution)/shard_map/ppermute | solution.py:25
  46.1 0.2 home.1.o0
  46.3 0.6 %collective-permute-done.4.o1 = bf16[128,512]{1,0:T(8,128)(2,1)S(1)} collective-permute-done((bf16[128,512]{1,0:T(8,128)(2,1)S(1)}, bf16[128,512]{1,0:T(8,128)(2,1)S(1)}, u32[]{:S(2)}, u32[]{:S(2)}) %collective-permute-start.4) | collective-permute-done | bytes 131104 | tf_op jit(solution)/shard_map/ppermute | solution.py:25
  46.9 3.3 %collective-permute-done.5.o2 = bf16[128,512]{1,0:T(8,128)(2,1)S(1)} collective-permute-done((bf16[128,512]{1,0:T(8,128)(2,1)S(1)}, bf16[128,512]{1,0:T(8,128)(2,1)S(1)}, u32[]{:S(2)}, u32[]{:S(2)}) %collective-permute-start.5) | collective-permute-done | bytes 131104 | tf_op jit(solution)/shard_map/ppermute | solution.py:25
  50.2 0.0 collective-permute-done.6.o3
  50.2 0.7 %add.42 = bf16[128,512]{1,0:T(8,128)(2,1)} custom-call(f32[128,512]{1,0:T(8,128)S(1)} %home.1.o0, bf16[128,512]{1,0:T(8,128)(2,1)S(1)} %collective-permute-done.4.o1, bf16[128,512]{1,0:T(8,128)(2,1)S(1)} %collective-permute-done.5.o2, bf16[128,512]{1,0:T(8,128)(2,1)S(1)} %collective-permute-done.6.o3), custom_call_target="tpu_custom_call" | custom-call | tf_op jit(solution)/shard_map/add/pallas_call | solution.py:363
  (2 shorter events, 0.1 us)
Async XLA Ops:
  0.0 12.4 %copy-start.4 = (bf16[128,2048]{1,0:T(8,128)(2,1)S(1)}, bf16[128,2048]{1,0:T(8,128)(2,1)}, u32[]{:S(2)}) copy-start(bf16[128,2048]{1,0:T(8,128)(2,1)} %param.11) | copy-start | bytes 1572868
  2.6 15.0 %all-to-all-start = ((bf16[16,8,1152]{2,1,0:T(8,128)(2,1)}), bf16[16,8,1152]{2,1,0:T(8,128)(2,1)S(1)}, u32[]{:S(2)}, u32[]{:S(2)}) async-start(bf16[16,8,1152]{2,1,0:T(8,128)(2,1)} %pack.1), calls=%async_computation | async-start | bytes 589824 | tf_op jit(solution)/shard_map/all_to_all | solution.py:50
  12.4 4.6 %copy-start.1 = (f32[8,16]{1,0:T(8,128)S(1)}, f32[8,16]{1,0:T(8,128)}, u32[]{:S(2)}) copy-start(f32[8,16]{1,0:T(8,128)} %decay.1) | copy-start | bytes 1540
  12.4 4.6 %copy-start.2 = (f32[8,16]{1,0:T(8,128)S(1)}, f32[8,16]{1,0:T(8,128)}, u32[]{:S(2)}) copy-start(f32[8,16]{1,0:T(8,128)} %residue.1) | copy-start | bytes 1540
  12.5 4.5 %copy-start = (f32[3,128,3]{1,2,0:T(4,128)S(1)}, f32[3,128,3]{1,2,0:T(4,128)}, u32[]{:S(2)}) copy-start(f32[3,128,3]{1,2,0:T(4,128)} %param.7) | copy-start | bytes 13828
  12.5 6.1 %collective-permute-start = (bf16[128,512]{1,0:T(8,128)(2,1)S(1)}, bf16[128,512]{1,0:T(8,128)(2,1)S(1)}, u32[]{:S(2)}, u32[]{:S(2)}) collective-permute-start(bf16[128,512]{1,0:T(8,128)(2,1)S(1)} %get-tuple-element.31), channel_id=1, source_target_pairs={{0,8},{4,12},{8,0},{12,4},{1,9},{5,13},{9,1},{13,5},{2,10},{6,14},... | collective-permute-start | bytes 393224 | tf_op jit(solution)/shard_map/ppermute | solution.py:25
  15.5 5.4 %collective-permute-start.1 = (bf16[128,512]{1,0:T(8,128)(2,1)S(1)}, bf16[128,512]{1,0:T(8,128)(2,1)S(1)}, u32[]{:S(2)}, u32[]{:S(2)}) collective-permute-start(bf16[128,512]{1,0:T(8,128)(2,1)S(1)} %get-tuple-element.30), channel_id=1, source_target_pairs={{0,12},{4,0},{8,4},{12,8},{1,13},{5,1},{9,5},{13,9},{2,14},{6,2},{... | collective-permute-start | bytes 393224 | tf_op jit(solution)/shard_map/ppermute | solution.py:25
  16.3 0.7 %copy-start.3 = (f32[128]{0:T(128)S(1)}, f32[128]{0:T(128)}, u32[]{:S(2)}) copy-start(f32[128]{0:T(128)} %param.10) | copy-start | bytes 1540
  16.3 5.4 %collective-permute-start.2 = (bf16[128,512]{1,0:T(8,128)(2,1)S(1)}, bf16[128,512]{1,0:T(8,128)(2,1)S(1)}, u32[]{:S(2)}, u32[]{:S(2)}) collective-permute-start(bf16[128,512]{1,0:T(8,128)(2,1)S(1)} %get-tuple-element.32), channel_id=1, source_target_pairs={{0,4},{4,8},{8,12},{12,0},{1,5},{5,9},{9,13},{13,1},{2,6},{6,10},{... | collective-permute-start | bytes 393224 | tf_op jit(solution)/shard_map/ppermute | solution.py:25
  35.5 4.8 %collective-permute-start.3 = (bf16[256,512]{1,0:T(8,128)(2,1)S(1)}, bf16[256,512]{1,0:T(8,128)(2,1)S(1)}, u32[]{:S(2)}, u32[]{:S(2)}) collective-permute-start(bf16[256,512]{1,0:T(8,128)(2,1)S(1)} %settle.1.own), channel_id=1, source_target_pairs={{0,1},{1,0},{2,3},{3,2},{4,5},{5,4},{6,7},{7,6},{8,9},{9,8},{10,11... | collective-permute-start | bytes 786440 | tf_op jit(solution)/shard_map/ppermute | solution.py:25
  40.6 6.3 %collective-permute-start.4 = (bf16[128,512]{1,0:T(8,128)(2,1)S(1)}, bf16[128,512]{1,0:T(8,128)(2,1)S(1)}, u32[]{:S(2)}, u32[]{:S(2)}) collective-permute-start(bf16[128,512]{1,0:T(8,128)(2,1)S(1)} %get-tuple-element.26), channel_id=1, source_target_pairs={{0,8},{4,12},{8,0},{12,4},{1,9},{5,13},{9,1},{13,5},{2,10},{6,14},... | collective-permute-start | bytes 393224 | tf_op jit(solution)/shard_map/ppermute | solution.py:25
  43.4 6.8 %collective-permute-start.5 = (bf16[128,512]{1,0:T(8,128)(2,1)S(1)}, bf16[128,512]{1,0:T(8,128)(2,1)S(1)}, u32[]{:S(2)}, u32[]{:S(2)}) collective-permute-start(bf16[128,512]{1,0:T(8,128)(2,1)S(1)} %get-tuple-element.27), channel_id=1, source_target_pairs={{0,4},{4,8},{8,12},{12,0},{1,5},{5,9},{9,13},{13,1},{2,6},{6,10},{... | collective-permute-start | bytes 393224 | tf_op jit(solution)/shard_map/ppermute | solution.py:25
  44.0 6.2 %collective-permute-start.6 = (bf16[128,512]{1,0:T(8,128)(2,1)S(1)}, bf16[128,512]{1,0:T(8,128)(2,1)S(1)}, u32[]{:S(2)}, u32[]{:S(2)}) collective-permute-start(bf16[128,512]{1,0:T(8,128)(2,1)S(1)} %get-tuple-element.28), channel_id=1, source_target_pairs={{0,12},{4,0},{8,4},{12,8},{1,13},{5,1},{9,5},{13,9},{2,14},{6,2},{... | collective-permute-start | bytes 393224 | tf_op jit(solution)/shard_map/ppermute | solution.py:25
